TPU v7x, 32 devices: a whole 2x2x4 slice. The times are simulated.
32 devices in a mesh: frame: 16 (over z, y, core), pos: 2 (over x).
Axes of the slice: x: 2, y: 2, z: 4, core: 2. Of those that a mesh axis runs over, the one named last changes fastest.
Arguments:
- spatial_qkv: bfloat16 [2, 16, 384, 3, 1152], P(None, 'frame', 'pos'), may hold values from -9 to 9
- residual: bfloat16 [2, 16, 384, 1152], P(None, 'frame', 'pos'), may hold values from -0.59765625 to 0.59765625
- spatial_gate: float32 [2, 1152], replicated, may hold values from 0.5 to 2
- spatial_proj: bfloat16 [1152, 1152], replicated, may hold values from -0.1875 to 0.1875
- spatial_qgain: float32 [72], replicated, may hold values from 0.5 to 8
- spatial_kgain: float32 [72], replicated, may hold values from 0.5 to 8
- temporal_shift: float32 [2, 1152], replicated, may hold values from -3 to 3
- temporal_scale: float32 [2, 1152], replicated, may hold values from -0.5 to 0.5
- temporal_qkv: bfloat16 [1152, 3456], replicated, as said below
- temporal_qgain: float32 [72], replicated, may hold values from 0.6 to 6
- temporal_kgain: float32 [72], replicated, may hold values from 0.6 to 6
Outputs:
- temporal_out: bfloat16 [2, 16, 384, 1152], P(None, 'frame', 'pos')
Inputs may be any that keep to these rules, and one draw needn't show every extreme that they name: `temporal_qkv`: entries are of the size of a weight with fan-in 1152.
All inputs are finite; a program needn't handle non-finite values.
Results may differ from a plain program's by a relative error of at most 0.028.
The roundings to bfloat16 on the way count: a program that leaves them out, or rounds other values in their place, can miss the bound.
Values may be sent and summed in bfloat16 or wider, within the bound.
No kernel may reach another device: no remote copies, remote signals or barrier semaphores. Data moves between devices by JAX's collectives and lax.ppermute only.
A program may use at most 128 MiB of HBM per device.

v0:
```python
import math

import jax
import jax.numpy as jnp
from jax import lax
from jax.sharding import PartitionSpec as P

EPSILON = 1e-06


def head_norm(values, gain):
    widened = values.astype(jnp.float32)
    factor = lax.rsqrt(jnp.mean(widened * widened, axis=-1, keepdims=True) + EPSILON)
    return (widened * factor * gain).astype(jnp.bfloat16)


def softmax_weights(scores):
    row_top = jnp.max(scores, axis=-1, keepdims=True)
    expons = jnp.exp(scores - row_top)
    return (expons / jnp.sum(expons, axis=-1, keepdims=True)).astype(jnp.bfloat16)


def spatial_attend(element, query_gain, keys_gain):
    query_norm = head_norm(element[:, 0], query_gain)
    keys_norm = head_norm(element[:, 1], keys_gain)
    scores = jnp.einsum(
        "qhd,khd->hqk", query_norm, keys_norm, preferred_element_type=jnp.float32
    ) / math.sqrt(element.shape[-1])
    weights = softmax_weights(scores)
    return jnp.einsum(
        "hqk,khd->qhd", weights, element[:, 2], preferred_element_type=jnp.float32
    ).astype(jnp.bfloat16)


def per_device(
    spatial_qkv,
    residual,
    spatial_gate,
    spatial_proj,
    spatial_qgain,
    spatial_kgain,
    temporal_shift,
    temporal_scale,
    temporal_qkv,
    temporal_qgain,
    temporal_kgain,
):
    videos, frames_loc, pos_loc, triple, width = spatial_qkv.shape
    head_dim = spatial_qgain.shape[0]
    heads = width // head_dim
    pos_count = lax.axis_size("pos")
    frame_count = lax.axis_size("frame")
    heads_loc = heads // pos_count
    group_width = heads_loc * head_dim
    entries = videos * frames_loc
    all_pos = pos_count * pos_loc
    packed = spatial_qkv.reshape(entries, 1, pos_loc, 3, pos_count, group_width)
    by_heads = lax.all_to_all(packed, "pos", split_axis=4, concat_axis=1, tiled=True)
    by_heads = by_heads.reshape(entries, all_pos, 3, heads_loc, head_dim)
    attended = lax.map(
        lambda element: spatial_attend(element, spatial_qgain, spatial_kgain), by_heads
    )
    outgoing = attended.reshape(entries, pos_count, pos_loc, 1, group_width)
    returned = lax.all_to_all(outgoing, "pos", split_axis=1, concat_axis=3, tiled=True)
    mixed = jnp.dot(
        returned.reshape(entries * pos_loc, width), spatial_proj, preferred_element_type=jnp.float32
    )
    mixed = mixed.reshape(videos, frames_loc, pos_loc, width)
    updated = (residual.astype(jnp.float32) + spatial_gate[:, None, None, :] * mixed).astype(
        jnp.bfloat16
    )
    widened = updated.astype(jnp.float32)
    centred = widened - jnp.mean(widened, axis=-1, keepdims=True)
    spread = jnp.mean(centred * centred, axis=-1, keepdims=True)
    scaled = centred * lax.rsqrt(spread + EPSILON) * (1.0 + temporal_scale[:, None, None, :])
    normed = (scaled + temporal_shift[:, None, None, :]).astype(jnp.bfloat16)
    pos_group = pos_loc // frame_count
    frames_all = frames_loc * frame_count
    moved = lax.all_to_all(normed, "frame", split_axis=2, concat_axis=1, tiled=True)
    by_frames = jnp.dot(
        moved.reshape(videos * frames_all * pos_group, width),
        temporal_qkv,
        preferred_element_type=jnp.float32,
    )
    by_frames = by_frames.astype(jnp.bfloat16)
    arranged = by_frames.reshape(videos, frames_all, pos_group, 3, heads, head_dim)
    query_norm = head_norm(arranged[:, :, :, 0], temporal_qgain)
    keys_norm = head_norm(arranged[:, :, :, 1], temporal_kgain)
    scores = jnp.einsum(
        "bfphd,bgphd->bphfg", query_norm, keys_norm, preferred_element_type=jnp.float32
    ) / math.sqrt(head_dim)
    weights = softmax_weights(scores)
    result = jnp.einsum(
        "bphfg,bgphd->bfphd", weights, arranged[:, :, :, 2], preferred_element_type=jnp.float32
    )
    result = result.astype(jnp.bfloat16).reshape(videos, frames_all, pos_group, width)
    return lax.all_to_all(result, "frame", split_axis=1, concat_axis=2, tiled=True)


def solution(mesh):
    return jax.shard_map(
        per_device,
        mesh=mesh,
        in_specs=(
            P(None, "frame", "pos", None, None),
            P(None, "frame", "pos", None),
            P(),
            P(),
            P(),
            P(),
            P(),
            P(),
            P(),
            P(),
            P(),
        ),
        out_specs=P(None, "frame", "pos", None),
        check_vma=False,
    )
```

profile of v0, /device:TPU:0, one launch (start us, length us, event | category | flops | bytes accessed | tf_op | source)
XLA Modules:
  0.0 225.0 jit_solution(17201572388065575915)
XLA Ops:
  0.0 7.5 %reshape.113 = bf16[2,1,192,3,2,576]{5,4,2,3,0,1:T(2,128)(2,1)} reshape(bf16[2,1,192,3,1152]{4,2,3,1,0:T(8,128)(2,1)} %param.13) | data formatting | bytes 5308416 | tf_op jit(solution)/shard_map/reshape | solution.py:57
  7.5 3.9 %copy.63 = bf16[2,1,192,3,2,576]{5,2,3,1,0,4:T(8,128)(2,1)} copy(bf16[2,1,192,3,2,576]{5,4,2,3,0,1:T(2,128)(2,1)} %reshape.113) | data formatting | bytes 5308416 | tf_op jit(solution)/shard_map/reshape | solution.py:57
  11.4 5.1 %all-to-all-start = ((bf16[2,1,192,3,2,576]{5,2,3,1,0,4:T(8,128)(2,1)}), bf16[2,1,192,3,2,576]{5,2,3,1,0,4:T(8,128)(2,1)}, u32[]{:S(2)}, u32[]{:S(2)}) async-start(bf16[2,1,192,3,2,576]{5,2,3,1,0,4:T(8,128)(2,1)} %copy.63), calls=%async_computation | async-start | bytes 5898240 | tf_op jit(solution)/shard_map/all_to_all | solution.py:58
  16.5 35.5 %all-to-all-done = bf16[2,1,192,3,2,576]{5,2,3,1,0,4:T(8,128)(2,1)} async-done(((bf16[2,1,192,3,2,576]{5,2,3,1,0,4:T(8,128)(2,1)}), bf16[2,1,192,3,2,576]{5,2,3,1,0,4:T(8,128)(2,1)}, u32[]{:S(2)}, u32[]{:S(2)}) %all-to-all-start) | async-done | bytes 2654240 | tf_op jit(solution)/shard_map/all_to_all | solution.py:58
  52.1 9.1 %copy.64 = bf16[2,2,1,192,3,1,576]{3,1,6,4,0,5,2:T(2,128)(2,1)} copy(bf16[2,2,1,192,3,1,576]{6,3,4,0,1,5,2:T(8,128)(2,1)} %bitcast.10) | data formatting | bytes 5308416 | tf_op jit(solution)/shard_map/all_to_all | solution.py:58
  61.2 8.2 %reshape.114 = bf16[2,384,3,8,72]{1,4,3,2,0:T(8,128)(2,1)} reshape(bf16[2,2,1,192,3,1,576]{3,1,6,4,0,5,2:T(2,128)(2,1)} %copy.64) | data formatting | bytes 5308416 | tf_op jit(solution)/shard_map/reshape | solution.py:59
  69.3 23.9 %while.10 = (s32[]{:T(128)}, bf16[2,384,8,72]{1,3,2,0:T(8,128)(2,1)S(1)}, bf16[2,384,3,8,72]{1,4,3,2,0:T(8,128)(2,1)}, f32[72]{0:T(128)S(1)}, f32[72]{0:T(128)}, /*index=5*/s32[]{:T(128)}) while((s32[]{:T(128)}, bf16[2,384,8,72]{1,3,2,0:T(8,128)(2,1)S(1)}, bf16[2,384,3,8,72]{1,4,3,2,0:T(8,128)(2,1)}, f32[72]{0:T(128)S(1)}, f32[72]{0:T(128)}, ...), condition=%wide.region_5.6_spmd, body=%wide.region_0.5_spmd.sunk | while | flops 348961152 | bytes 20178308 | solution.py:60
  69.3 1.5 dynamic-slice_bitcast_fusion.2
  70.8 1.1 copy-done.1
  72.8 5.5 %fusion.78 = (f32[8,384]{1,0:T(8,128)}, f32[8,384,384]{1,2,0:T(8,128)}) fusion(f32[72]{0:T(128)} %get-tuple-element.117, f32[384,8]{0,1:T(8,128)S(1)} %get-tuple-element.97, bf16[384,3,8,72]{0,3,2,1:T(8,128)(2,1)} %copy-done.1, f32[72]{0:T(128)S(1)} %get-tuple-element.116, f32[384,8]{0,1:T(8,128)} %get-tuple-element.98), kind=kOutput, calls=%fused_computation.71.clone.1 | convolution fusion | flops 175178112 | bytes 5640992 | tf_op jit(solution)/shard_map/while/body/eval_jaxpr/sub | solution.py:19
  78.3 3.0 %fusion.79 = bf16[2,384,8,72]{1,3,2,0:T(8,128)(2,1)S(1)} fusion(bf16[2,384,8,72]{1,3,2,0:T(8,128)(2,1)S(1)} %get-tuple-element.108, s32[]{:T(128)} %get-tuple-element.107, f32[8,384,384]{1,2,0:T(8,128)} %get-tuple-element.99, f32[8,384]{1,0:T(8,128)} %get-tuple-element.100, bf16[384,3,8,72]{0,3,2,1:T(8,128)(2,1)} %copy-done.1), kind=kOutput, calls=%fused_computation.10.clone.1 | convolution fusion | flops 172449792 | bytes 5616128 | tf_op jit(solution)/shard_map/while/body/eval_jaxpr/hqk,khd->qhd/dot_general | solution.py:30
  81.3 1.5 dynamic-slice_bitcast_fusion.2
  84.7 5.5 %fusion.78 = (f32[8,384]{1,0:T(8,128)}, f32[8,384,384]{1,2,0:T(8,128)}) fusion(f32[72]{0:T(128)} %get-tuple-element.117, f32[384,8]{0,1:T(8,128)S(1)} %get-tuple-element.97, bf16[384,3,8,72]{0,3,2,1:T(8,128)(2,1)} %copy-done.1, f32[72]{0:T(128)S(1)} %get-tuple-element.116, f32[384,8]{0,1:T(8,128)} %get-tuple-element.98), kind=kOutput, calls=%fused_computation.71.clone.1 | convolution fusion | flops 175178112 | bytes 5640992 | tf_op jit(solution)/shard_map/while/body/eval_jaxpr/sub | solution.py:19
  90.3 3.0 %fusion.79 = bf16[2,384,8,72]{1,3,2,0:T(8,128)(2,1)S(1)} fusion(bf16[2,384,8,72]{1,3,2,0:T(8,128)(2,1)S(1)} %get-tuple-element.108, s32[]{:T(128)} %get-tuple-element.107, f32[8,384,384]{1,2,0:T(8,128)} %get-tuple-element.99, f32[8,384]{1,0:T(8,128)} %get-tuple-element.100, bf16[384,3,8,72]{0,3,2,1:T(8,128)(2,1)} %copy-done.1), kind=kOutput, calls=%fused_computation.10.clone.1 | convolution fusion | flops 172449792 | bytes 5616128 | tf_op jit(solution)/shard_map/while/body/eval_jaxpr/hqk,khd->qhd/dot_general | solution.py:30
  93.3 1.6 reshape.115
  94.9 3.7 %copy.65 = bf16[2,2,192,1,576]{4,2,3,0,1:T(8,128)(2,1)} copy(bf16[2,2,192,1,576]{2,1,4,0,3:T(2,128)(2,1)} %reshape.115) | data formatting | bytes 1769472 | tf_op jit(solution)/shard_map/reshape | solution.py:63
  98.6 4.6 %all-to-all-start.1 = ((bf16[2,2,192,1,576]{4,2,3,0,1:T(8,128)(2,1)}), bf16[2,2,192,1,576]{4,2,3,0,1:T(8,128)(2,1)}, u32[]{:S(2)}, u32[]{:S(2)}) async-start(bf16[2,2,192,1,576]{4,2,3,0,1:T(8,128)(2,1)} %copy.65), calls=%async_computation.1 | async-start | bytes 1966080 | tf_op jit(solution)/shard_map/all_to_all | solution.py:64
  103.2 12.5 %all-to-all-done.1 = bf16[2,2,192,1,576]{4,2,3,0,1:T(8,128)(2,1)} async-done(((bf16[2,2,192,1,576]{4,2,3,0,1:T(8,128)(2,1)}), bf16[2,2,192,1,576]{4,2,3,0,1:T(8,128)(2,1)}, u32[]{:S(2)}, u32[]{:S(2)}) %all-to-all-start.1) | async-done | bytes 884768 | tf_op jit(solution)/shard_map/all_to_all | solution.py:64
  115.7 3.2 %copy.66 = bf16[2,1,192,2,1,576]{5,3,2,0,4,1:T(2,128)(2,1)} copy(bf16[2,1,192,2,1,576]{5,2,0,3,4,1:T(8,128)(2,1)} %bitcast.12) | data formatting | bytes 1769472 | tf_op jit(solution)/shard_map/all_to_all | solution.py:64
  118.9 2.4 %dot_general.20 = bf16[2,192,1152]{2,1,0:T(8,128)(2,1)S(1)} reshape(bf16[2,1,192,2,1,576]{5,3,2,0,4,1:T(2,128)(2,1)} %copy.66) | data formatting | bytes 1769472 | tf_op jit(solution)/shard_map/dot_general | solution.py:65
  121.4 2.9 %fusion.65 = (f32[2,192]{1,0:T(2,128)S(1)}, f32[2,1,192,1152]{3,2,0,1:T(8,128)S(1)}) fusion(bf16[2,192,1152]{2,1,0:T(8,128)(2,1)S(1)} %dot_general.20, bf16[1152,1152]{1,0:T(8,128)(2,1)S(1)} %copy-done, f32[2,1152]{1,0:T(2,128)} %param.15, bf16[2,1,192,1152]{3,2,1,0:T(8,128)(2,1)} %param.14), kind=kOutput, calls=%fused_computation.73 | convolution fusion | flops 1021869696 | bytes 6203904 | tf_op jit(solution)/shard_map/dot_general | solution.py:65
  125.9 27.6 %all_to_all.51 = bf16[2,1,192,1152]{3,0,1,2:T(2,128)(2,1)S(1)} all-to-all(bf16[2,1,192,1152]{3,0,1,2:T(2,128)(2,1)S(1)} %copy.67), channel_id=1, replica_groups=mesh['frame'=16,'pos'=2] {'frame'}, dimensions={2} | all-to-all | bytes 1769472 | tf_op jit(solution)/shard_map/all_to_all | solution.py:79
  153.7 5.0 %convolution_convert_fusion = bf16[384,3456]{1,0:T(8,128)(2,1)} fusion(bf16[384,1152]{1,0:T(8,128)(2,1)S(1)} %bitcast.121, bf16[1152,3456]{1,0:T(8,128)(2,1)S(1)} %bitcast.123), kind=kOutput, calls=%fused_computation.30 | convolution fusion | flops 3058974720 | bytes 11501568 | tf_op jit(solution)/shard_map/dot_general | solution.py:80
  158.7 10.7 %reshape.117 = bf16[2,16,12,3,16,72]{5,4,3,2,1,0:T(8,128)(2,1)} reshape(bf16[384,3456]{1,0:T(8,128)(2,1)} %convolution_convert_fusion) | data formatting | bytes 5308416 | tf_op jit(solution)/shard_map/reshape | solution.py:86
  169.4 3.3 %fusion.64 = (bf16[2,16,12,1,16,72]{5,4,3,2,1,0:T(8,128)(2,1)S(1)}, bf16[2,16,12,1,16,72]{5,4,3,2,1,0:T(8,128)(2,1)S(1)}, bf16[2,16,12,1,16,72]{5,4,3,2,1,0:T(8,128)(2,1)S(1)}) fusion(bf16[2,16,12,3,16,72]{5,4,3,2,1,0:T(8,128)(2,1)} %reshape.117), kind=kLoop, calls=%fused_computation.72 | loop fusion | bytes 5308416 | tf_op jit(solution)/shard_map/slice | solution.py:94
  172.7 2.2 fusion.30
  175.0 2.4 %fusion.44 = f32[2,12,16,16,16]{3,4,2,1,0:T(8,128)S(1)} fusion(f32[72]{0:T(128)S(1)} %copy-done.5, f32[2,16,12,16]{1,3,2,0:T(8,128)S(1)} %add_rsqrt_fusion.2, f32[72]{0:T(128)S(1)} %copy-done.6, f32[2,16,12,16]{1,3,2,0:T(8,128)S(1)} %add_rsqrt_fusion.3, bf16[2,16,12,1,16,72]{5,4,3,2,1,0:T(8,128)(2,1)S(1)} %get-tuple-element.50, ...), kind=kOutput, calls=%fused_computation.54 | convolution fusion | flops 17694720 | bytes 2212416 | tf_op jit(solution)/shard_map/bfphd,bgphd->bphfg/dot_general | solution.py:89
  177.4 13.3 %fusion.66 = (f32[2,12,16,16]{3,2,1,0:T(8,128)S(1)}, f32[2,12,16,16,16]{3,4,2,1,0:T(8,128)S(1)}) fusion(f32[2,12,16,16,16]{3,4,2,1,0:T(8,128)S(1)} %fusion.44), kind=kOutput, calls=%fused_computation.74 | output fusion | flops 393231 | bytes 811008 | tf_op jit(solution)/shard_map/sub | solution.py:19
  190.7 1.2 fusion.53
  191.9 1.6 copy.78
  193.5 4.3 %reshape.124 = bf16[2,16,12,1152]{3,0,2,1:T(2,128)(2,1)S(1)} reshape(bf16[2,16,12,16,72]{4,3,0,2,1:T(8,128)(2,1)} %copy.78) | data formatting | bytes 1769472 | tf_op jit(solution)/shard_map/reshape | solution.py:96
  197.9 26.1 %all_to_all.52 = bf16[2,16,12,1152]{3,0,2,1:T(2,128)(2,1)S(1)} all-to-all(bf16[2,16,12,1152]{3,0,2,1:T(2,128)(2,1)S(1)} %reshape.124), channel_id=1, replica_groups=mesh['frame'=16,'pos'=2] {'frame'}, dimensions={1} | all-to-all | bytes 1769472 | tf_op jit(solution)/shard_map/all_to_all | solution.py:97
  (35 shorter events, 5.6 us)
Async XLA Ops:
  0.0 121.3 %copy-start = (bf16[1152,1152]{1,0:T(8,128)(2,1)S(1)}, bf16[1152,1152]{1,0:T(8,128)(2,1)}, u32[]{:S(2)}) copy-start(bf16[1152,1152]{1,0:T(8,128)(2,1)} %param.16) | copy-start | bytes 7962628
  11.4 40.7 %all-to-all-start = ((bf16[2,1,192,3,2,576]{5,2,3,1,0,4:T(8,128)(2,1)}), bf16[2,1,192,3,2,576]{5,2,3,1,0,4:T(8,128)(2,1)}, u32[]{:S(2)}, u32[]{:S(2)}) async-start(bf16[2,1,192,3,2,576]{5,2,3,1,0,4:T(8,128)(2,1)} %copy.63), calls=%async_computation | async-start | bytes 5898240 | tf_op jit(solution)/shard_map/all_to_all | solution.py:58
  61.2 8.2 %copy-start.4 = (f32[72]{0:T(128)S(1)}, f32[72]{0:T(128)}, u32[]{:S(2)}) copy-start(f32[72]{0:T(128)} %param.17) | copy-start | bytes 868
  70.8 1.1 copy-start.1
  82.8 1.1 copy-start.1
  94.9 8.3 %copy-start.3 = (f32[2,1152]{1,0:T(2,128)S(1)}, f32[2,1152]{1,0:T(2,128)}, u32[]{:S(2)}) copy-start(f32[2,1152]{1,0:T(2,128)} %param.20) | copy-start | bytes 27652
  98.6 17.1 %all-to-all-start.1 = ((bf16[2,2,192,1,576]{4,2,3,0,1:T(8,128)(2,1)}), bf16[2,2,192,1,576]{4,2,3,0,1:T(8,128)(2,1)}, u32[]{:S(2)}, u32[]{:S(2)}) async-start(bf16[2,2,192,1,576]{4,2,3,0,1:T(8,128)(2,1)} %copy.65), calls=%async_computation.1 | async-start | bytes 1966080 | tf_op jit(solution)/shard_map/all_to_all | solution.py:64
  121.4 3.3 %copy-start.2 = (f32[2,1152]{1,0:T(2,128)S(1)}, f32[2,1152]{1,0:T(2,128)}, u32[]{:S(2)}) copy-start(f32[2,1152]{1,0:T(2,128)} %param.19) | copy-start | bytes 27652
  121.4 32.3 %slice-start = ((s8[7962624]{0:T(1024)(128)(4,1)}), s8[4194304]{0:T(1024)(128)(4,1)S(1)}, s32[]{:S(2)}) async-start(s8[7962624]{0:T(1024)(128)(4,1)} %bitcast.122), calls=%async_computation.4 | async-start | bytes 8388608
  124.3 29.4 %slice-start.1 = ((s8[7962624]{0:T(1024)(128)(4,1)}), s8[3768320]{0:T(1024)(128)(4,1)S(1)}, s32[]{:S(2)}) async-start(s8[7962624]{0:T(1024)(128)(4,1)} %bitcast.122), calls=%async_computation.5 | async-start | bytes 7536640
  172.6 2.3 %copy-start.5 = (f32[72]{0:T(128)S(1)}, f32[72]{0:T(128)}, u32[]{:S(2)}) copy-start(f32[72]{0:T(128)} %param.23) | copy-start | bytes 868
  172.7 2.3 %copy-start.6 = (f32[72]{0:T(128)S(1)}, f32[72]{0:T(128)}, u32[]{:S(2)}) copy-start(f32[72]{0:T(128)} %param.22) | copy-start | bytes 868
where the time goes:
time: 226 us; the launch traced here: 225 us
  local copies, waits for them, and re-layouts  66.7 us (30%)
  blocking collectives  53.8 us (24%)
  waiting for transfers between devices  48 us (21%)
  matrix products  28.6 us (13%)
  other arithmetic  18 us (8%)
  starting transfers between devices  9.67 us (4%)
    all_to_all x1, waiting for transfers between devices, per_device(): lax.all_to_all(packed, 'pos', split_axis=4, concat_axis=1, tiled=True)  35.5 us
    all_to_all x1, blocking collectives, per_device(): lax.all_to_all(normed, 'frame', split_axis=2, concat_axis=1, tiled=True)  27.6 us
    all_to_all x1, blocking collectives, per_device(): lax.all_to_all(result, 'frame', split_axis=1, concat_axis=2, tiled=True)  26.1 us
    sub x1, other arithmetic, softmax_weights(): expons = jnp.exp(scores - row_top)  13.3 us
    all_to_all x1, waiting for transfers between devices, per_device(): lax.all_to_all(outgoing, 'pos', split_axis=1, concat_axis=3, tiled=True)  12.5 us
    reshape x2, local copies, waits for them, and re-layouts, per_device(): packed = spatial_qkv.reshape(entries, 1, pos_loc, 3, pos_count, group_width)  11.4 us
    sub x2, matrix products, softmax_weights(): expons = jnp.exp(scores - row_top)  11.1 us
    reshape x1, local copies, waits for them, and re-layouts, per_device(): by_frames.reshape(videos, frames_all, pos_group, 3, heads, head_dim)  10.7 us
  transfers between devices with their start and end apart: 2, of which 2 were waited for; matrix products, arithmetic and copies ran while one was open for 0% of the time, Pallas kernels for 0%

commit v1 on v0

v1 whole, which is shorter than its diff:
```python
import functools
import math

import jax
import jax.numpy as jnp
from jax import lax
from jax.experimental import pallas as pl
from jax.experimental.pallas import tpu as pltpu
from jax.sharding import PartitionSpec as P

EPSILON = 1e-06
LANES = 128
F32 = jnp.float32
BF16 = jnp.bfloat16


def segment_masks(width, head_dim):
    feature = lax.broadcasted_iota(jnp.int32, (width, LANES), 0)
    head = lax.broadcasted_iota(jnp.int32, (width, LANES), 1)
    inside = feature - head * head_dim
    gather = jnp.where((inside >= 0) & (inside < head_dim), 1.0, 0.0).astype(BF16)
    feature = lax.broadcasted_iota(jnp.int32, (LANES, width), 1)
    head = lax.broadcasted_iota(jnp.int32, (LANES, width), 0)
    inside = feature - head * head_dim
    spread = jnp.where((inside >= 0) & (inside < head_dim), 1.0, 0.0).astype(BF16)
    return gather, spread


def split_dot(values, matrix):
    high = values.astype(BF16)
    low = (values - high.astype(F32)).astype(BF16)
    return jnp.dot(high, matrix, preferred_element_type=F32) + jnp.dot(
        low, matrix, preferred_element_type=F32
    )


def head_norm(values, gain_row, gather, spread, head_dim):
    widened = values.astype(F32)
    squares = split_dot(widened * widened, gather)
    factor = lax.rsqrt(squares * (1.0 / head_dim) + EPSILON)
    return (widened * split_dot(factor, spread) * gain_row).astype(BF16)


def head_window(head, head_dim, width):
    tiles = width // LANES
    start = LANES * min(head * head_dim // LANES, max(tiles - 2, 0))
    span = min(2 * LANES, width)
    lane = lax.broadcasted_iota(jnp.int32, (1, span), 1) + start
    mask = (lane >= head * head_dim) & (lane < (head + 1) * head_dim)
    return start, span, mask


def softmax_rows(scores, scale):
    top = jnp.max(scores, axis=-1, keepdims=True)
    expons = jnp.exp2((scores - top) * scale)
    total = jnp.sum(expons, axis=-1, keepdims=True)
    return (expons * (1.0 / total)).astype(BF16)


def spatial_kernel(head_dim, remotes, *refs):
    qkv_ref = refs[0]
    remote_refs = refs[1 : 1 + remotes]
    residual_ref, proj_ref, rows_ref, gains_ref, out_ref, keys, values, attended = refs[1 + remotes :]
    pos_loc, width = out_ref.shape
    heads = width // head_dim
    scale = math.log2(math.e) / math.sqrt(head_dim)
    gather, spread = segment_masks(width, head_dim)
    query = head_norm(qkv_ref[0, 0], gains_ref[0:1, :], gather, spread, head_dim)
    key_gain = gains_ref[1:2, :]
    keys[0:pos_loc, :] = head_norm(qkv_ref[0, 1], key_gain, gather, spread, head_dim)
    values[0:pos_loc, :] = qkv_ref[0, 2]
    for j, remote in enumerate(remote_refs):
        place = slice((j + 1) * pos_loc, (j + 2) * pos_loc)
        keys[place, :] = head_norm(remote[0], key_gain, gather, spread, head_dim)
        values[place, :] = remote[1]
    for head in range(heads):
        start, span, mask = head_window(head, head_dim, width)
        window = slice(start, start + span)
        own = jnp.where(mask, query[:, window], jnp.zeros((), BF16))
        scores = lax.dot_general(
            own, keys[:, window], (((1,), (1,)), ((), ())), preferred_element_type=F32
        )
        weights = softmax_rows(scores, scale)
        part = jnp.dot(weights, values[:, window], preferred_element_type=F32)
        attended[:, window] = jnp.where(mask, part, attended[:, window])
    mixed = jnp.dot(attended[...].astype(BF16), proj_ref[...], preferred_element_type=F32)
    updated = (residual_ref[0].astype(F32) + rows_ref[0, 0:1, :] * mixed).astype(BF16)
    widened = updated.astype(F32)
    centred = widened - jnp.mean(widened, axis=-1, keepdims=True)
    spread_of = jnp.mean(centred * centred, axis=-1, keepdims=True)
    scaled = centred * lax.rsqrt(spread_of + EPSILON) * (1.0 + rows_ref[0, 1:2, :])
    out_ref[...] = (scaled + rows_ref[0, 2:3, :]).astype(BF16)


def spatial(video, head_dim, qkv, remotes, residual, proj, rows, gains):
    _, _, pos_loc, width = qkv.shape
    all_pos = pos_loc * (1 + len(remotes))
    whole = lambda a: pl.BlockSpec(a.shape, lambda i: (0,) * a.ndim)
    return pl.pallas_call(
        functools.partial(spatial_kernel, head_dim, len(remotes)),
        grid=(1,),
        out_shape=jax.ShapeDtypeStruct((pos_loc, width), BF16),
        in_specs=[pl.BlockSpec((1, 3, pos_loc, width), lambda i: (video, 0, 0, 0))]
        + [whole(r) for r in remotes]
        + [
            pl.BlockSpec((1, pos_loc, width), lambda i: (video, 0, 0)),
            whole(proj),
            pl.BlockSpec((1, 3, width), lambda i: (video, 0, 0)),
            whole(gains),
        ],
        out_specs=pl.BlockSpec((pos_loc, width), lambda i: (0, 0)),
        scratch_shapes=[
            pltpu.VMEM((all_pos, width), BF16),
            pltpu.VMEM((all_pos, width), BF16),
            pltpu.VMEM((pos_loc, width), F32),
        ],
        compiler_params=pltpu.CompilerParams(vmem_limit_bytes=40 * 2**20),
        cost_estimate=pl.CostEstimate(
            flops=4 * pos_loc * all_pos * width + 2 * pos_loc * width * width,
            bytes_accessed=2 * width * (8 * pos_loc + width),
            transcendentals=0,
        ),
        name=f"spatial_{video}",
    )(qkv, *remotes, residual, proj, rows, gains)


def temporal_kernel(head_dim, block_tokens, in_ref, weight_ref, gains_ref, out_ref, arranged, query, keys, values, attended):
    frames, tokens, width = in_ref.shape
    heads = width // head_dim
    rows = frames * block_tokens
    blocks = tokens // block_tokens
    scale = math.log2(math.e) / math.sqrt(head_dim)
    gather, spread = segment_masks(width, head_dim)
    incoming = in_ref[...].astype(F32)
    for b in range(blocks):
        piece = incoming[:, b * block_tokens : (b + 1) * block_tokens, :]
        arranged[b * rows : (b + 1) * rows, :] = piece.reshape(rows, width).astype(BF16)
    for i, (place, gain) in enumerate(((query, 0), (keys, 1), (values, None))):
        projected = jnp.dot(
            arranged[...], weight_ref[:, i * width : (i + 1) * width], preferred_element_type=F32
        ).astype(BF16)
        if gain is not None:
            projected = head_norm(projected, gains_ref[gain : gain + 1, :], gather, spread, head_dim)
        place[...] = projected
    first = lax.broadcasted_iota(jnp.int32, (rows, rows), 0)
    second = lax.broadcasted_iota(jnp.int32, (rows, rows), 1)
    same = lax.rem(first, block_tokens) == lax.rem(second, block_tokens)
    for b in range(blocks):
        place = slice(b * rows, (b + 1) * rows)
        for head in range(heads):
            start, span, mask = head_window(head, head_dim, width)
            window = slice(start, start + span)
            own = jnp.where(mask, query[place, window], jnp.zeros((), BF16))
            scores = lax.dot_general(
                own, keys[place, window], (((1,), (1,)), ((), ())), preferred_element_type=F32
            )
            weights = softmax_rows(jnp.where(same, scores, -1e30), scale)
            part = jnp.dot(weights, values[place, window], preferred_element_type=F32)
            attended[place, window] = jnp.where(mask, part, attended[place, window])
    pieces = [
        attended[b * rows : (b + 1) * rows, :].reshape(frames, block_tokens, width)
        for b in range(blocks)
    ]
    out_ref[...] = jnp.concatenate(pieces, axis=1).astype(BF16)


def temporal(head_dim, moved, weight, gains):
    frames, tokens, width = moved.shape
    block_tokens = 8 if tokens % 8 == 0 else tokens
    total = frames * tokens
    whole = lambda a: pl.BlockSpec(a.shape, lambda i: (0,) * a.ndim)
    return pl.pallas_call(
        functools.partial(temporal_kernel, head_dim, block_tokens),
        grid=(1,),
        out_shape=jax.ShapeDtypeStruct(moved.shape, BF16),
        in_specs=[whole(moved), whole(weight), whole(gains)],
        out_specs=whole(moved),
        scratch_shapes=[pltpu.VMEM((total, width), BF16)] * 4 + [pltpu.VMEM((total, width), F32)],
        compiler_params=pltpu.CompilerParams(vmem_limit_bytes=44 * 2**20),
        cost_estimate=pl.CostEstimate(
            flops=2 * total * width * 3 * width, bytes_accessed=2 * width * (3 * width + 2 * total), transcendentals=0
        ),
        name="temporal",
    )(moved, weight, gains)


def per_device(
    spatial_qkv,
    residual,
    spatial_gate,
    spatial_proj,
    spatial_qgain,
    spatial_kgain,
    temporal_shift,
    temporal_scale,
    temporal_qkv,
    temporal_qgain,
    temporal_kgain,
):
    videos, frames_loc, pos_loc, _, width = spatial_qkv.shape
    head_dim = spatial_qgain.shape[0]
    heads = width // head_dim
    pos_count = lax.axis_size("pos")
    frame_count = lax.axis_size("frame")
    assert frames_loc == 1
    qkv = jnp.transpose(spatial_qkv.reshape(videos, pos_loc, 3, width), (0, 2, 1, 3))
    residual = residual.reshape(videos, pos_loc, width)
    remotes = []
    for video in range(videos):
        own = qkv[video, 1:]
        remotes.append(
            [
                lax.ppermute(own, "pos", [(i, (i + s) % pos_count) for i in range(pos_count)])
                for s in range(1, pos_count)
            ]
        )
    rows = jnp.stack([spatial_gate, temporal_scale, temporal_shift], axis=1)
    tile = lambda a, b: jnp.tile(jnp.stack([a, b]), (1, heads))
    spatial_gains = tile(spatial_qgain, spatial_kgain)
    temporal_gains = tile(temporal_qgain, temporal_kgain)
    normed = [
        spatial(video, head_dim, qkv, remotes[video], residual, spatial_proj, rows, spatial_gains)
        for video in range(videos)
    ]
    tokens = videos * pos_loc // frame_count
    outgoing = jnp.concatenate(normed, axis=0).reshape(frame_count, tokens, width)
    moved = lax.all_to_all(outgoing, "frame", split_axis=0, concat_axis=0, tiled=True)
    result = temporal(head_dim, moved, temporal_qkv, temporal_gains)
    back = lax.all_to_all(result, "frame", split_axis=0, concat_axis=0, tiled=True)
    return back.reshape(videos, frames_loc, pos_loc, width)


def solution(mesh):
    return jax.shard_map(
        per_device,
        mesh=mesh,
        in_specs=(
            P(None, "frame", "pos", None, None),
            P(None, "frame", "pos", None),
            P(),
            P(),
            P(),
            P(),
            P(),
            P(),
            P(),
            P(),
            P(),
        ),
        out_specs=P(None, "frame", "pos", None),
        check_vma=False,
    )
```

time: 226 us -> 126 us (0.56)
  local copies, waits for them, and re-layouts: 66.7 us -> 12.2 us
  Pallas kernels: 0 us -> 30.6 us
  matrix products: 28.6 us -> 0 us
  blocking collectives: 53.8 us -> 27.8 us
  other arithmetic: 18 us -> 1.76 us
  waiting for transfers between devices: 48 us -> 43.1 us
    reshape x8 -> x0, local copies, waits for them, and re-layouts: 41.5 us -> none  [the longest x2 11.4 us: per_device(): packed = spatial_qkv.reshape(entries, 1, pos_loc, 3, pos_count, group_width)]
    pallas_call x0 -> x3, Pallas kernels: none -> 30.6 us  [the longest x2 20.5 us: spatial(): pl.pallas_call(functools.partial(spatial_kernel, head_dim, len(remotes)),...]
    all_to_all x2 -> x1, waiting for transfers between devices: 48 us -> 20.2 us  [per_device(): lax.all_to_all(outgoing, 'frame', split_axis=0, concat_axis=0, tiled=True)]
    all_to_all x2 -> x1, blocking collectives: 53.8 us -> 27.8 us  [per_device(): lax.all_to_all(result, 'frame', split_axis=0, concat_axis=0, tiled=True)]
    ppermute x0 -> x2, waiting for transfers between devices: none -> 23 us  [per_device(): lax.ppermute(own, 'pos', [(i, (i + s) % pos_count) for i in range(pos_cou...]
    dot_general x6 -> x0, matrix products: 17.5 us -> none  [the longest x2 5.99 us: spatial_attend(): jnp.einsum('hqk,khd->qhd', weights, element[:, 2], preferred_element_type...]
    all_to_all x4 -> x0, local copies, waits for them, and re-layouts: 13.4 us -> none  [the longest x1 9.1 us: per_device(): lax.all_to_all(packed, 'pos', split_axis=4, concat_axis=1, tiled=True)]
    sub x1 -> x0, other arithmetic: 13.3 us -> none  [softmax_weights(): expons = jnp.exp(scores - row_top)]
  transfers between devices with their start and end apart: 2 -> 3, of which waited for: 2 -> 3; matrix products, arithmetic and copies ran while one was open for 0% -> 3% of each run, Pallas kernels for 0% -> 8%
where the time goes in v1:
time: 126 us; the launch traced here: 125 us
  waiting for transfers between devices  43.1 us (34%)
  Pallas kernels  30.6 us (24%)
  blocking collectives  27.8 us (22%)
  local copies, waits for them, and re-layouts  12.2 us (10%)
  starting transfers between devices  9.18 us (7%)
  other arithmetic  1.76 us (1%)
    all_to_all x1, blocking collectives, per_device(): lax.all_to_all(result, 'frame', split_axis=0, concat_axis=0, tiled=True)  27.8 us
    ppermute x2, waiting for transfers between devices, per_device(): lax.ppermute(own, 'pos', [(i, (i + s) % pos_count) for i in range(pos_cou...  23 us
    pallas_call x2, Pallas kernels, spatial(): pl.pallas_call(functools.partial(spatial_kernel, head_dim, len(remotes)),...  20.5 us
    all_to_all x1, waiting for transfers between devices, per_device(): lax.all_to_all(outgoing, 'frame', split_axis=0, concat_axis=0, tiled=True)  20.2 us
    pallas_call x1, Pallas kernels, temporal(): pl.pallas_call(functools.partial(temporal_kernel, head_dim, block_tokens)...  10.1 us
    all_to_all x1, starting transfers between devices, per_device(): lax.all_to_all(outgoing, 'frame', split_axis=0, concat_axis=0, tiled=True)  6.19 us
    unnamed x23, local copies, waits for them, and re-layouts  5.96 us
    ppermute x2, starting transfers between devices, per_device(): lax.ppermute(own, 'pos', [(i, (i + s) % pos_count) for i in range(pos_cou...  2.99 us
  transfers between devices with their start and end apart: 3, of which 3 were waited for; matrix products, arithmetic and copies ran while one was open for 3% of the time, Pallas kernels for 8%

profile of v1, /device:TPU:0, one launch (start us, length us, event | category | flops | bytes accessed | tf_op | source)
XLA Modules:
  0.0 124.7 jit_solution(3692933331514429607)
XLA Ops:
  0.0 0.0 copy-start.7
  0.0 0.0 copy-start.2
  0.0 2.9 %slice_bitcast_fusion.1 = (bf16[2,192,1152]{2,1,0:T(8,128)(2,1)}, bf16[2,192,1152]{2,1,0:T(8,128)(2,1)}) fusion(bf16[2,3,192,1152]{3,2,1,0:T(8,128)(2,1)} %bitcast.16), kind=kLoop, calls=%fused_computation.1 | loop fusion | bytes 3538944 | tf_op jit(solution)/shard_map/squeeze | solution.py:210
  3.0 3.0 %collective-permute-start.1 = (bf16[2,192,1152]{2,1,0:T(8,128)(2,1)}, bf16[2,192,1152]{2,1,0:T(8,128)(2,1)}, u32[]{:S(2)}, u32[]{:S(2)}) collective-permute-start(bf16[2,192,1152]{2,1,0:T(8,128)(2,1)} %get-tuple-element.6), channel_id=1, source_target_pairs={{0,1},{1,0},{2,3},{3,2},{4,5},{5,4},{6,7},{7,6},{8,9},{9,8},{10,11... | collective-permute-start | bytes 2654216 | tf_op jit(solution)/shard_map/ppermute | solution.py:213
  5.9 0.0 collective-permute-start
  5.9 0.0 copy-done.4
  5.9 0.6 stack.30
  6.5 0.0 copy-done.5
  6.6 0.6 stack.31
  7.2 0.0 copy-done.6
  7.2 0.6 stack.32
  7.8 0.0 copy-done.8
  7.8 0.0 copy-done.7
  7.8 0.6 tile.8
  8.4 0.8 tile.9.refs_5_
  9.2 0.8 pad_maximum_fusion.1.refs_4_
  10.0 16.7 %collective-permute-done.1.refs_1_ = bf16[2,192,1152]{2,1,0:T(8,128)(2,1)} collective-permute-done((bf16[2,192,1152]{2,1,0:T(8,128)(2,1)}, bf16[2,192,1152]{2,1,0:T(8,128)(2,1)}, u32[]{:S(2)}, u32[]{:S(2)}) %collective-permute-start.1) | collective-permute-done | bytes 884768 | tf_op jit(solution)/shard_map/ppermute | solution.py:213
  26.7 0.0 copy-done
  26.7 1.7 %copy-done.1 = bf16[1152,1152]{1,0:T(8,128)(2,1)S(1)} copy-done((bf16[1152,1152]{1,0:T(8,128)(2,1)S(1)}, bf16[1152,1152]{1,0:T(8,128)(2,1)}, u32[]{:S(2)}) %copy-start.1) | copy-done | bytes 2654232
  28.5 10.1 %spatial_1.1 = bf16[192,1152]{1,0:T(8,128)(2,1)S(1)} custom-call(bf16[2,3,192,1152]{3,2,1,0:T(8,128)(2,1)S(1)} %bitcast.17, bf16[2,192,1152]{2,1,0:T(8,128)(2,1)} %collective-permute-done.1.refs_1_, bf16[2,192,1152]{2,1,0:T(8,128)(2,1)S(1)} %bitcast.19, bf16[1152,1152]{1,0:T(8,128)(2,1)S(1)} %copy-done.1, f32[2,3,1152]{2,1,0:T(4,128)S(1)} %pad_maximum_fusion.1.refs_4_, ...), custom_call_target="tpu_custom_call" | custom-call | flops 849346560 | bytes 6193152 | tf_op jit(solution)/shard_map/spatial_1/pallas_call | solution.py:99
  38.6 6.2 %collective-permute-done.refs_1_ = bf16[2,192,1152]{2,1,0:T(8,128)(2,1)} collective-permute-done((bf16[2,192,1152]{2,1,0:T(8,128)(2,1)}, bf16[2,192,1152]{2,1,0:T(8,128)(2,1)}, u32[]{:S(2)}, u32[]{:S(2)}) %collective-permute-start) | collective-permute-done | bytes 884768 | tf_op jit(solution)/shard_map/ppermute | solution.py:213
  44.8 10.3 %spatial_0.1 = bf16[192,1152]{1,0:T(8,128)(2,1)S(1)} custom-call(bf16[2,3,192,1152]{3,2,1,0:T(8,128)(2,1)S(1)} %bitcast.18, bf16[2,192,1152]{2,1,0:T(8,128)(2,1)} %collective-permute-done.refs_1_, bf16[2,192,1152]{2,1,0:T(8,128)(2,1)S(1)} %bitcast.20, bf16[1152,1152]{1,0:T(8,128)(2,1)S(1)} %copy-done.1, f32[2,3,1152]{2,1,0:T(4,128)S(1)} %pad_maximum_fusion.1.refs_4_, ...), custom_call_target="tpu_custom_call" | custom-call | flops 849346560 | bytes 6193152 | tf_op jit(solution)/shard_map/spatial_0/pallas_call | solution.py:99
  55.1 0.0 copy-start.9
  55.2 0.0 copy-start.10
  55.2 1.0 pad_maximum_fusion
  56.2 6.2 %all-to-all-start = ((bf16[16,24,1152]{2,1,0:T(8,128)(2,1)}), bf16[16,24,1152]{2,1,0:T(8,128)(2,1)S(1)}, u32[]{:S(2)}, u32[]{:S(2)}) async-start(bf16[16,24,1152]{2,1,0:T(8,128)(2,1)} %bitcast.8), calls=%async_computation | async-start | bytes 1769472 | tf_op jit(solution)/shard_map/all_to_all | solution.py:227
  62.4 0.1 tile.21.gains_ref
  62.5 20.2 %all-to-all-done.in_ref = bf16[16,24,1152]{2,1,0:T(8,128)(2,1)S(1)} async-done(((bf16[16,24,1152]{2,1,0:T(8,128)(2,1)}), bf16[16,24,1152]{2,1,0:T(8,128)(2,1)S(1)}, u32[]{:S(2)}, u32[]{:S(2)}) %all-to-all-start) | async-done | bytes 884768 | tf_op jit(solution)/shard_map/all_to_all | solution.py:227
  82.6 3.3 %copy-done.3 = bf16[1152,3456]{1,0:T(8,128)(2,1)S(1)} copy-done((bf16[1152,3456]{1,0:T(8,128)(2,1)S(1)}, bf16[1152,3456]{1,0:T(8,128)(2,1)}, u32[]{:S(2)}) %copy-start.3) | copy-done | bytes 7962648
  85.9 10.1 %temporal.1 = bf16[16,24,1152]{2,1,0:T(8,128)(2,1)S(1)} custom-call(bf16[16,24,1152]{2,1,0:T(8,128)(2,1)S(1)} %all-to-all-done.in_ref, bf16[1152,3456]{1,0:T(8,128)(2,1)S(1)} %copy-done.3, f32[2,1152]{1,0:T(2,128)S(1)} %tile.21.gains_ref), custom_call_target="tpu_custom_call" | custom-call | flops 3057647616 | bytes 9732096 | tf_op jit(solution)/shard_map/temporal/pallas_call | solution.py:172
  96.0 27.8 %all_to_all.10 = bf16[16,24,1152]{2,1,0:T(8,128)(2,1)S(1)} all-to-all(bf16[16,24,1152]{2,1,0:T(8,128)(2,1)S(1)} %temporal.1), channel_id=1, replica_groups=mesh['frame'=16,'pos'=2] {'frame'}, dimensions={0} | all-to-all | bytes 1769472 | tf_op jit(solution)/shard_map/all_to_all | solution.py:229
  123.8 0.9 copy.14
  (13 shorter events, 0.0 us)
Async XLA Ops:
  0.0 26.7 %copy-start = (bf16[2,1,192,3,1152]{4,2,3,1,0:T(8,128)(2,1)S(1)}, bf16[2,1,192,3,1152]{4,2,3,1,0:T(8,128)(2,1)}, u32[]{:S(2)}) copy-start(bf16[2,1,192,3,1152]{4,2,3,1,0:T(8,128)(2,1)} %param.11) | copy-start | bytes 7962628
  0.0 5.9 %copy-start.4 = (f32[2,1152]{1,0:T(2,128)S(1)}, f32[2,1152]{1,0:T(2,128)}, u32[]{:S(2)}) copy-start(f32[2,1152]{1,0:T(2,128)} %param.13) | copy-start | bytes 27652
  0.0 6.5 %copy-start.5 = (f32[2,1152]{1,0:T(2,128)S(1)}, f32[2,1152]{1,0:T(2,128)}, u32[]{:S(2)}) copy-start(f32[2,1152]{1,0:T(2,128)} %param.18) | copy-start | bytes 27652
  0.0 7.1 %copy-start.6 = (f32[2,1152]{1,0:T(2,128)S(1)}, f32[2,1152]{1,0:T(2,128)}, u32[]{:S(2)}) copy-start(f32[2,1152]{1,0:T(2,128)} %param.17) | copy-start | bytes 27652
  0.0 7.8 %copy-start.8 = (f32[72]{0:T(128)S(1)}, f32[72]{0:T(128)}, u32[]{:S(2)}) copy-start(f32[72]{0:T(128)} %param.15) | copy-start | bytes 868
  0.0 7.7 %copy-start.7 = (f32[72]{0:T(128)S(1)}, f32[72]{0:T(128)}, u32[]{:S(2)}) copy-start(f32[72]{0:T(128)} %param.16) | copy-start | bytes 868
  0.0 26.7 %copy-start.2 = (bf16[2,1,192,1152]{3,2,1,0:T(8,128)(2,1)S(1)}, bf16[2,1,192,1152]{3,2,1,0:T(8,128)(2,1)}, u32[]{:S(2)}) copy-start(bf16[2,1,192,1152]{3,2,1,0:T(8,128)(2,1)} %param.12) | copy-start | bytes 2654212
  3.0 23.7 %collective-permute-start.1 = (bf16[2,192,1152]{2,1,0:T(8,128)(2,1)}, bf16[2,192,1152]{2,1,0:T(8,128)(2,1)}, u32[]{:S(2)}, u32[]{:S(2)}) collective-permute-start(bf16[2,192,1152]{2,1,0:T(8,128)(2,1)} %get-tuple-element.6), channel_id=1, source_target_pairs={{0,1},{1,0},{2,3},{3,2},{4,5},{5,4},{6,7},{7,6},{8,9},{9,8},{10,11... | collective-permute-start | bytes 2654216 | tf_op jit(solution)/shard_map/ppermute | solution.py:213
  5.9 38.9 %collective-permute-start = (bf16[2,192,1152]{2,1,0:T(8,128)(2,1)}, bf16[2,192,1152]{2,1,0:T(8,128)(2,1)}, u32[]{:S(2)}, u32[]{:S(2)}) collective-permute-start(bf16[2,192,1152]{2,1,0:T(8,128)(2,1)} %get-tuple-element.5), channel_id=1, source_target_pairs={{0,1},{1,0},{2,3},{3,2},{4,5},{5,4},{6,7},{7,6},{8,9},{9,8},{10,11... | collective-permute-start | bytes 2654216 | tf_op jit(solution)/shard_map/ppermute | solution.py:213
  26.7 1.8 %copy-start.1 = (bf16[1152,1152]{1,0:T(8,128)(2,1)S(1)}, bf16[1152,1152]{1,0:T(8,128)(2,1)}, u32[]{:S(2)}) copy-start(bf16[1152,1152]{1,0:T(8,128)(2,1)} %refs_3_.3) | copy-start | bytes 7962628
  55.1 7.2 %copy-start.9 = (f32[72]{0:T(128)S(1)}, f32[72]{0:T(128)}, u32[]{:S(2)}) copy-start(f32[72]{0:T(128)} %param.21) | copy-start | bytes 868
  55.2 7.2 %copy-start.10 = (f32[72]{0:T(128)S(1)}, f32[72]{0:T(128)}, u32[]{:S(2)}) copy-start(f32[72]{0:T(128)} %param.20) | copy-start | bytes 868
  56.2 26.5 %all-to-all-start = ((bf16[16,24,1152]{2,1,0:T(8,128)(2,1)}), bf16[16,24,1152]{2,1,0:T(8,128)(2,1)S(1)}, u32[]{:S(2)}, u32[]{:S(2)}) async-start(bf16[16,24,1152]{2,1,0:T(8,128)(2,1)} %bitcast.8), calls=%async_computation | async-start | bytes 1769472 | tf_op jit(solution)/shard_map/all_to_all | solution.py:227
  82.6 3.3 %copy-start.3 = (bf16[1152,3456]{1,0:T(8,128)(2,1)S(1)}, bf16[1152,3456]{1,0:T(8,128)(2,1)}, u32[]{:S(2)}) copy-start(bf16[1152,3456]{1,0:T(8,128)(2,1)} %weight_ref.1) | copy-start | bytes 23887876

commit v2 on v1

v2 whole, which is shorter than its diff:
```python
import functools
import math

import jax
import jax.numpy as jnp
from jax import lax
from jax.experimental import pallas as pl
from jax.experimental.pallas import tpu as pltpu
from jax.sharding import PartitionSpec as P

EPSILON = 1e-06
LANES = 128
F32 = jnp.float32
BF16 = jnp.bfloat16
VMEM_LIMIT = 24 * 2**20
TEMPORAL_LIMIT = 57 * 2**20
SMALL, LARGE = 5 * 10**8, 2 * 10**10


def segment_masks(width, head_dim):
    feature = lax.broadcasted_iota(jnp.int32, (width, LANES), 0)
    head = lax.broadcasted_iota(jnp.int32, (width, LANES), 1)
    inside = feature - head * head_dim
    gather = jnp.where((inside >= 0) & (inside < head_dim), 1.0, 0.0).astype(BF16)
    feature = lax.broadcasted_iota(jnp.int32, (LANES, width), 1)
    head = lax.broadcasted_iota(jnp.int32, (LANES, width), 0)
    inside = feature - head * head_dim
    spread = jnp.where((inside >= 0) & (inside < head_dim), 1.0, 0.0).astype(BF16)
    return gather, spread


def split_dot(values, matrix):
    high = values.astype(BF16)
    low = (values - high.astype(F32)).astype(BF16)
    return jnp.dot(high, matrix, preferred_element_type=F32) + jnp.dot(
        low, matrix, preferred_element_type=F32
    )


def head_norm(values, gain_row, gather, spread, head_dim):
    widened = values.astype(F32)
    squares = split_dot(widened * widened, gather)
    factor = lax.rsqrt(squares * (1.0 / head_dim) + EPSILON)
    return (widened * split_dot(factor, spread) * gain_row).astype(BF16)


def head_window(head, head_dim, width):
    tiles = width // LANES
    start = LANES * min(head * head_dim // LANES, max(tiles - 2, 0))
    span = min(2 * LANES, width)
    lane = lax.broadcasted_iota(jnp.int32, (1, span), 1) + start
    mask = (lane >= head * head_dim) & (lane < (head + 1) * head_dim)
    return start, span, mask


def softmax_rows(scores, scale):
    top = jnp.max(scores, axis=-1, keepdims=True)
    expons = jnp.exp2((scores - top) * scale)
    total = jnp.sum(expons, axis=-1, keepdims=True)
    return (expons * (1.0 / total)).astype(BF16)


def score_kernel(head_dim, video, remotes, *refs):
    qkv_ref = refs[0]
    remote_refs = refs[1 : 1 + remotes]
    gains_ref, out_ref, query, keys = refs[1 + remotes :]
    pos_loc, width = query.shape
    scale = math.log2(math.e) / math.sqrt(head_dim)
    gather, spread = segment_masks(width, head_dim)
    query[...] = head_norm(qkv_ref[video, 0], gains_ref[0:1, :], gather, spread, head_dim)
    key_gain = gains_ref[1:2, :]
    keys[0:pos_loc, :] = head_norm(qkv_ref[video, 1], key_gain, gather, spread, head_dim)
    for j, remote in enumerate(remote_refs):
        place = slice((j + 1) * pos_loc, (j + 2) * pos_loc)
        keys[place, :] = head_norm(remote[...], key_gain, gather, spread, head_dim)
    for head in range(width // head_dim):
        start, span, mask = head_window(head, head_dim, width)
        window = slice(start, start + span)
        own = jnp.where(mask, query[:, window], jnp.zeros((), BF16))
        scores = lax.dot_general(
            own, keys[:, window], (((1,), (1,)), ((), ())), preferred_element_type=F32
        )
        out_ref[head] = softmax_rows(scores, scale)


def in_vmem(count):
    return [pl.BlockSpec(memory_space=pltpu.VMEM)] * count


def score_weights(video, head_dim, qkv, remote_keys, gains):
    _, _, pos_loc, width = qkv.shape
    all_pos = pos_loc * (1 + len(remote_keys))
    heads = width // head_dim
    return pl.pallas_call(
        functools.partial(score_kernel, head_dim, video, len(remote_keys)),
        out_shape=jax.ShapeDtypeStruct((heads, pos_loc, all_pos), BF16),
        in_specs=in_vmem(2 + len(remote_keys)),
        out_specs=pl.BlockSpec(memory_space=pltpu.VMEM),
        scratch_shapes=[pltpu.VMEM((pos_loc, width), BF16), pltpu.VMEM((all_pos, width), BF16)],
        compiler_params=pltpu.CompilerParams(vmem_limit_bytes=VMEM_LIMIT),
        cost_estimate=pl.CostEstimate(flops=SMALL, bytes_accessed=2**20, transcendentals=0),
        name=f"scores_{video}",
    )(qkv, *remote_keys, gains)


def attend_kernel(head_dim, video, remotes, sub, *refs):
    weights_ref, qkv_ref = refs[:2]
    remote_refs = refs[2 : 2 + remotes]
    residual_ref, proj_ref, gate_ref, scale_ref, shift_ref, out_ref, values, attended = refs[2 + remotes :]
    pos_loc, width = attended.shape
    row = slice(video, video + 1)
    values[0:pos_loc, :] = qkv_ref[video, 2]
    for j, remote in enumerate(remote_refs):
        values[(j + 1) * pos_loc : (j + 2) * pos_loc, :] = remote[...]
    for head in range(width // head_dim):
        start, span, mask = head_window(head, head_dim, width)
        window = slice(start, start + span)
        part = jnp.dot(weights_ref[head], values[:, window], preferred_element_type=F32)
        attended[:, window] = jnp.where(mask, part, attended[:, window])
    mixed = jnp.dot(attended[...].astype(BF16), proj_ref[...], preferred_element_type=F32)
    updated = (residual_ref[video].astype(F32) + gate_ref[row, :] * mixed).astype(BF16)
    widened = updated.astype(F32)
    centred = widened - jnp.mean(widened, axis=-1, keepdims=True)
    spread_of = jnp.mean(centred * centred, axis=-1, keepdims=True)
    scaled = centred * lax.rsqrt(spread_of + EPSILON) * (1.0 + scale_ref[row, :])
    attended[...] = scaled + shift_ref[row, :]
    for i in range(pos_loc // sub):
        out_ref[i] = attended[i * sub : (i + 1) * sub, :].astype(BF16)


def attend(video, head_dim, sub, cost, weights, qkv, remote_values, residual, proj, gate, scale, shift):
    _, _, pos_loc, width = qkv.shape
    all_pos = pos_loc * (1 + len(remote_values))
    return pl.pallas_call(
        functools.partial(attend_kernel, head_dim, video, len(remote_values), sub),
        out_shape=jax.ShapeDtypeStruct((pos_loc // sub, sub, width), BF16),
        in_specs=in_vmem(7 + len(remote_values)),
        out_specs=pl.BlockSpec(memory_space=pltpu.VMEM),
        scratch_shapes=[pltpu.VMEM((all_pos, width), BF16), pltpu.VMEM((pos_loc, width), F32)],
        compiler_params=pltpu.CompilerParams(vmem_limit_bytes=VMEM_LIMIT),
        cost_estimate=pl.CostEstimate(flops=cost, bytes_accessed=2**20, transcendentals=0),
        name=f"attend_{video}",
    )(weights, qkv, *remote_values, residual, proj, gate, scale, shift)


def temporal_kernel(
    head_dim, tokens, in_ref, weight_ref, gains_ref, out_ref, arranged, query, keys, values, bias, held, arrived
):
    pieces, sub, width = in_ref.shape
    columns = [slice(i * width, (i + 1) * width) for i in range(3)]
    copies = [
        pltpu.make_async_copy(weight_ref.at[:, c], held.at[:, c], arrived.at[i])
        for i, c in enumerate(columns)
    ]
    for copy in copies:
        copy.start()
    rows = pieces * sub
    scale = math.log2(math.e) / math.sqrt(head_dim)
    gather, spread = segment_masks(width, head_dim)
    for i in range(pieces):
        arranged[i * sub : (i + 1) * sub, :] = in_ref[i].astype(F32)
    incoming = arranged[...].astype(BF16)
    for i, (place, gain) in enumerate(((query, 2), (keys, 3), (values, None))):
        copies[i].wait()
        projected = jnp.dot(
            incoming, held[:, columns[i]], preferred_element_type=F32
        ).astype(BF16)
        if gain is not None:
            projected = head_norm(projected, gains_ref[gain : gain + 1, :], gather, spread, head_dim)
        place[...] = projected
    first = lax.broadcasted_iota(jnp.int32, (rows, rows), 0)
    second = lax.broadcasted_iota(jnp.int32, (rows, rows), 1)
    same = lax.rem(first, tokens) == lax.rem(second, tokens)
    bias[...] = jnp.where(same, 0.0, -1e30)
    for head in range(width // head_dim):
        start, span, mask = head_window(head, head_dim, width)
        window = slice(start, start + span)
        own = jnp.where(mask, query[:, window], jnp.zeros((), BF16))
        scores = lax.dot_general(
            own, keys[:, window], (((1,), (1,)), ((), ())), preferred_element_type=F32
        )
        weights = softmax_rows(scores + bias[...], scale)
        part = jnp.dot(weights, values[:, window], preferred_element_type=F32)
        arranged[:, window] = jnp.where(mask, part, arranged[:, window])
    for i in range(pieces):
        out_ref[i] = arranged[i * sub : (i + 1) * sub, :].astype(BF16)


def temporal(video, head_dim, tokens, moved, weight, gains):
    pieces, sub, width = moved.shape
    rows = pieces * sub
    return pl.pallas_call(
        functools.partial(temporal_kernel, head_dim, tokens),
        out_shape=jax.ShapeDtypeStruct(moved.shape, BF16),
        in_specs=in_vmem(1) + [pl.BlockSpec(memory_space=pltpu.HBM)] + in_vmem(1),
        out_specs=pl.BlockSpec(memory_space=pltpu.VMEM),
        scratch_shapes=[pltpu.VMEM((rows, width), F32)]
        + [pltpu.VMEM((rows, width), BF16)] * 3
        + [
            pltpu.VMEM((rows, rows), F32),
            pltpu.VMEM((width, 3 * width), BF16),
            pltpu.SemaphoreType.DMA((3,)),
        ],
        compiler_params=pltpu.CompilerParams(vmem_limit_bytes=TEMPORAL_LIMIT),
        cost_estimate=pl.CostEstimate(flops=SMALL, bytes_accessed=2**20, transcendentals=0),
        name=f"temporal_{video}",
    )(moved, weight, gains)


def exchange(blocks, frame_count):
    pieces, sub, width = blocks.shape
    split = blocks.reshape(frame_count, pieces // frame_count, sub, width)
    moved = lax.all_to_all(split, "frame", split_axis=0, concat_axis=0, tiled=True)
    return moved.reshape(pieces, sub, width)


def per_device(
    spatial_qkv,
    residual,
    spatial_gate,
    spatial_proj,
    spatial_qgain,
    spatial_kgain,
    temporal_shift,
    temporal_scale,
    temporal_qkv,
    temporal_qgain,
    temporal_kgain,
):
    videos, frames_loc, pos_loc, _, width = spatial_qkv.shape
    head_dim = spatial_qgain.shape[0]
    heads = width // head_dim
    pos_count = lax.axis_size("pos")
    frame_count = lax.axis_size("frame")
    assert frames_loc == 1
    tokens = pos_loc // frame_count
    sub = math.gcd(tokens, 8)
    qkv = jnp.transpose(spatial_qkv.reshape(videos, pos_loc, 3, width), (0, 2, 1, 3))
    residual = residual.reshape(videos, pos_loc, width)
    steps = [[(i, (i + s) % pos_count) for i in range(pos_count)] for s in range(1, pos_count)]
    remotes = {}
    for video in reversed(range(videos)):
        for which in (2, 1):
            own = qkv[video, which]
            remotes[video, which] = [lax.ppermute(own, "pos", step) for step in steps]
    gains = jnp.tile(
        jnp.stack([spatial_qgain, spatial_kgain, temporal_qgain, temporal_kgain]), (1, heads)
    )
    results = []
    for video in range(videos):
        weights = score_weights(video, head_dim, qkv, remotes[video, 1], gains)
        normed = attend(
            video, head_dim, sub, LARGE if video == videos - 1 else SMALL, weights, qkv, remotes[video, 2], residual,
            spatial_proj, spatial_gate, temporal_scale, temporal_shift,
        )
        moved = exchange(normed, frame_count)
        result = temporal(video, head_dim, tokens, moved, temporal_qkv, gains)
        back = exchange(result, frame_count)
        results.append(back.reshape(pos_loc, width))
    return jnp.stack(results).reshape(videos, frames_loc, pos_loc, width)


def solution(mesh):
    return jax.shard_map(
        per_device,
        mesh=mesh,
        in_specs=(
            P(None, "frame", "pos", None, None),
            P(None, "frame", "pos", None),
            P(),
            P(),
            P(),
            P(),
            P(),
            P(),
            P(),
            P(),
            P(),
        ),
        out_specs=P(None, "frame", "pos", None),
        check_vma=False,
    )
```

time: 126 us -> 103 us (0.82)
  blocking collectives: 27.8 us -> 0 us
  starting transfers between devices: 9.18 us -> 23.9 us
  waiting for transfers between devices: 43.1 us -> 36.8 us
  local copies, waits for them, and re-layouts: 12.2 us -> 6.1 us
  Pallas kernels: 30.6 us -> 34.5 us
    all_to_all x1 -> x0, blocking collectives: 27.8 us -> none  [per_device(): lax.all_to_all(result, 'frame', split_axis=0, concat_axis=0, tiled=True)]
    all_to_all x1 -> x4, starting transfers between devices: 6.19 us -> 18.8 us  [exchange(): lax.all_to_all(split, 'frame', split_axis=0, concat_axis=0, tiled=True)]
    ppermute x2 -> x4, waiting for transfers between devices: 23 us -> 14.6 us  [per_device(): remotes[video, which] = [lax.ppermute(own, 'pos', step) for step in steps]]
    pallas_call x3 -> x6, Pallas kernels: 30.6 us -> 34.5 us  [the longest x2 18.1 us: temporal(): pl.pallas_call(functools.partial(temporal_kernel, head_dim, tokens), out_...]
    unnamed x23 -> x34, local copies, waits for them, and re-layouts: 5.96 us -> 2.4 us
    another operation x7 -> x4, local copies, waits for them, and re-layouts: 3.31 us -> 0.9 us  [the longest x2 0.7 us: per_device(): jnp.tile(jnp.stack([spatial_qgain, spatial_kgain, temporal_qgain, tempora...]
    ppermute x2 -> x4, starting transfers between devices: 2.99 us -> 5.03 us  [per_device(): remotes[video, which] = [lax.ppermute(own, 'pos', step) for step in steps]]
    all_to_all x1 -> x4, waiting for transfers between devices: 20.2 us -> 22.2 us  [exchange(): lax.all_to_all(split, 'frame', split_axis=0, concat_axis=0, tiled=True)]
  transfers between devices with their start and end apart: 3 -> 8, of which waited for: 3 -> 7; matrix products, arithmetic and copies ran while one was open for 3% -> 1% of each run, Pallas kernels for 8% -> 34%
where the time goes in v2:
time: 103 us; the launch traced here: 102 us
  waiting for transfers between devices  36.8 us (36%)
  Pallas kernels  34.5 us (33%)
  starting transfers between devices  23.9 us (23%)
  local copies, waits for them, and re-layouts  6.1 us (6%)
    all_to_all x4, waiting for transfers between devices, exchange(): lax.all_to_all(split, 'frame', split_axis=0, concat_axis=0, tiled=True)  22.2 us
    all_to_all x4, starting transfers between devices, exchange(): lax.all_to_all(split, 'frame', split_axis=0, concat_axis=0, tiled=True)  18.8 us
    pallas_call x2, Pallas kernels, temporal(): pl.pallas_call(functools.partial(temporal_kernel, head_dim, tokens), out_...  18.1 us
    ppermute x4, waiting for transfers between devices, per_device(): remotes[video, which] = [lax.ppermute(own, 'pos', step) for step in steps]  14.6 us
    pallas_call x2, Pallas kernels, score_weights(): pl.pallas_call(functools.partial(score_kernel, head_dim, video, len(remot...  9.39 us
    pallas_call x2, Pallas kernels, attend(): pl.pallas_call(functools.partial(attend_kernel, head_dim, video, len(remo...  6.93 us
    ppermute x4, starting transfers between devices, per_device(): remotes[video, which] = [lax.ppermute(own, 'pos', step) for step in steps]  5.03 us
    squeeze x1, local copies, waits for them, and re-layouts, per_device(): own = qkv[video, which]  2.8 us
  transfers between devices with their start and end apart: 8, of which 7 were waited for; matrix products, arithmetic and copies ran while one was open for 1% of the time, Pallas kernels for 34%

profile of v2, /device:TPU:0, one launch (start us, length us, event | category | flops | bytes accessed | tf_op | source)
XLA Modules:
  0.0 102.4 jit_solution(4875753627136565163)
XLA Ops:
  0.0 2.8 %slice_bitcast_fusion.2 = (bf16[192,1152]{1,0:T(8,128)(2,1)}, bf16[192,1152]{1,0:T(8,128)(2,1)}, bf16[192,1152]{1,0:T(8,128)(2,1)}, bf16[192,1152]{1,0:T(8,128)(2,1)}) fusion(bf16[2,3,192,1152]{3,2,1,0:T(8,128)(2,1)} %bitcast.24), kind=kLoop, calls=%fused_computation.3 | loop fusion | bytes 3538944 | tf_op jit(solution)/shard_map/squeeze | solution.py:244
  2.8 3.0 %collective-permute-start = (bf16[192,1152]{1,0:T(8,128)(2,1)}, bf16[192,1152]{1,0:T(8,128)(2,1)}, u32[]{:S(2)}, u32[]{:S(2)}) collective-permute-start(bf16[192,1152]{1,0:T(8,128)(2,1)} %get-tuple-element.8), channel_id=1, source_target_pairs={{0,1},{1,0},{2,3},{3,2},{4,5},{5,4},{6,7},{7,6},{8,9},{9,8},{10,11... | collective-permute-start | bytes 1327112 | tf_op jit(solution)/shard_map/ppermute | solution.py:245
  5.8 0.0 collective-permute-start.1
  5.8 2.0 %collective-permute-start.2 = (bf16[192,1152]{1,0:T(8,128)(2,1)}, bf16[192,1152]{1,0:T(8,128)(2,1)}, u32[]{:S(2)}, u32[]{:S(2)}) collective-permute-start(bf16[192,1152]{1,0:T(8,128)(2,1)} %get-tuple-element.7), channel_id=1, source_target_pairs={{0,1},{1,0},{2,3},{3,2},{4,5},{5,4},{6,7},{7,6},{8,9},{9,8},{10,11... | collective-permute-start | bytes 1327112 | tf_op jit(solution)/shard_map/ppermute | solution.py:245
  7.8 0.0 collective-permute-start.3
  7.9 0.7 tile.10.refs_2_.gains_ref
  8.6 8.5 %collective-permute-done.refs_1_ = bf16[192,1152]{1,0:T(8,128)(2,1)} collective-permute-done((bf16[192,1152]{1,0:T(8,128)(2,1)}, bf16[192,1152]{1,0:T(8,128)(2,1)}, u32[]{:S(2)}, u32[]{:S(2)}) %collective-permute-start) | collective-permute-done | bytes 442400 | tf_op jit(solution)/shard_map/ppermute | solution.py:245
  17.1 0.7 copy-done.4
  17.8 4.7 %scores_0.1.refs_0_ = bf16[16,192,384]{2,1,0:T(8,128)(2,1)S(1)} custom-call(bf16[2,3,192,1152]{3,2,1,0:T(8,128)(2,1)S(1)} %bitcast.25, bf16[192,1152]{1,0:T(8,128)(2,1)} %collective-permute-done.refs_1_, f32[4,1152]{1,0:T(4,128)S(1)} %copy-done.4), custom_call_target="tpu_custom_call" | custom-call | flops 500000000 | bytes 1048576 | tf_op jit(solution)/shard_map/scores_0/pallas_call | solution.py:94
  22.5 4.0 %collective-permute-done.1.refs_2_ = bf16[192,1152]{1,0:T(8,128)(2,1)} collective-permute-done((bf16[192,1152]{1,0:T(8,128)(2,1)}, bf16[192,1152]{1,0:T(8,128)(2,1)}, u32[]{:S(2)}, u32[]{:S(2)}) %collective-permute-start.1) | collective-permute-done | bytes 442400 | tf_op jit(solution)/shard_map/ppermute | solution.py:245
  26.6 3.8 %attend_0.1 = bf16[48,4,1152]{2,1,0:T(4,128)(2,1)} custom-call(bf16[16,192,384]{2,1,0:T(8,128)(2,1)S(1)} %scores_0.1.refs_0_, bf16[2,3,192,1152]{3,2,1,0:T(8,128)(2,1)S(1)} %bitcast.26, bf16[192,1152]{1,0:T(8,128)(2,1)} %collective-permute-done.1.refs_2_, bf16[2,192,1152]{2,1,0:T(8,128)(2,1)S(1)} %bitcast.29, bf16[1152,1152]{1,0:T(8,128)(2,1)S(1)} %copy-done.1, ...), custom_call_target="tpu_custom_call" | custom-call | flops 500000000 | bytes 1048576 | tf_op jit(solution)/shard_map/attend_0/pallas_call | solution.py:134
  30.4 6.6 %all-to-all-start = ((bf16[16,3,4,1152]{3,2,1,0:T(4,128)(2,1)}), bf16[16,3,4,1152]{3,2,1,0:T(4,128)(2,1)}, u32[]{:S(2)}, u32[]{:S(2)}) async-start(bf16[16,3,4,1152]{3,2,1,0:T(4,128)(2,1)} %bitcast.10), calls=%async_computation | async-start | bytes 884736 | tf_op jit(solution)/shard_map/all_to_all | solution.py:213
  37.0 0.0 copy-start.2
  37.0 0.0 collective-permute-done.2.refs_1_
  37.0 0.9 copy-done.5
  37.9 4.7 %scores_1.1.refs_0_ = bf16[16,192,384]{2,1,0:T(8,128)(2,1)S(1)} custom-call(bf16[2,3,192,1152]{3,2,1,0:T(8,128)(2,1)S(1)} %bitcast.27, bf16[192,1152]{1,0:T(8,128)(2,1)} %collective-permute-done.2.refs_1_, f32[4,1152]{1,0:T(4,128)S(1)} %copy-done.5), custom_call_target="tpu_custom_call" | custom-call | flops 500000000 | bytes 1048576 | tf_op jit(solution)/shard_map/scores_1/pallas_call | solution.py:94
  42.6 2.1 %collective-permute-done.3.refs_2_ = bf16[192,1152]{1,0:T(8,128)(2,1)} collective-permute-done((bf16[192,1152]{1,0:T(8,128)(2,1)}, bf16[192,1152]{1,0:T(8,128)(2,1)}, u32[]{:S(2)}, u32[]{:S(2)}) %collective-permute-start.3) | collective-permute-done | bytes 442400 | tf_op jit(solution)/shard_map/ppermute | solution.py:245
  44.7 3.1 %attend_1.1 = bf16[48,4,1152]{2,1,0:T(4,128)(2,1)S(1)} custom-call(bf16[16,192,384]{2,1,0:T(8,128)(2,1)S(1)} %scores_1.1.refs_0_, bf16[2,3,192,1152]{3,2,1,0:T(8,128)(2,1)S(1)} %bitcast.28, bf16[192,1152]{1,0:T(8,128)(2,1)} %collective-permute-done.3.refs_2_, bf16[2,192,1152]{2,1,0:T(8,128)(2,1)S(1)} %bitcast.30, bf16[1152,1152]{1,0:T(8,128)(2,1)S(1)} %copy-done.2, ...), custom_call_target="tpu_custom_call" | custom-call | flops 20000000000 | bytes 1048576 | tf_op jit(solution)/shard_map/attend_1/pallas_call | solution.py:134
  47.8 0.0 copy-start.6
  47.8 0.8 copy-done.6
  48.6 1.5 %all-to-all-done = bf16[16,3,4,1152]{3,2,1,0:T(4,128)(2,1)} async-done(((bf16[16,3,4,1152]{3,2,1,0:T(4,128)(2,1)}), bf16[16,3,4,1152]{3,2,1,0:T(4,128)(2,1)}, u32[]{:S(2)}, u32[]{:S(2)}) %all-to-all-start) | async-done | bytes 442400 | tf_op jit(solution)/shard_map/all_to_all | solution.py:213
  50.0 4.7 %all-to-all-start.2 = ((bf16[16,3,4,1152]{3,2,1,0:T(4,128)(2,1)}), bf16[16,3,4,1152]{3,2,1,0:T(4,128)(2,1)S(1)}, u32[]{:S(2)}, u32[]{:S(2)}) async-start(bf16[16,3,4,1152]{3,2,1,0:T(4,128)(2,1)} %bitcast.31), calls=%async_computation.2 | async-start | bytes 884736 | tf_op jit(solution)/shard_map/all_to_all | solution.py:213
  54.8 9.1 %temporal_0.1 = bf16[48,4,1152]{2,1,0:T(4,128)(2,1)} custom-call(bf16[48,4,1152]{2,1,0:T(4,128)(2,1)} %bitcast.11.in_ref, bf16[1152,3456]{1,0:T(8,128)(2,1)} %weight_ref.3, f32[4,1152]{1,0:T(4,128)} %tile.10.refs_2_.gains_ref), custom_call_target="tpu_custom_call" | custom-call | flops 500000000 | bytes 1048576 | tf_op jit(solution)/shard_map/temporal_0/pallas_call | solution.py:192
  63.8 3.9 %all-to-all-done.2 = bf16[16,3,4,1152]{3,2,1,0:T(4,128)(2,1)S(1)} async-done(((bf16[16,3,4,1152]{3,2,1,0:T(4,128)(2,1)}), bf16[16,3,4,1152]{3,2,1,0:T(4,128)(2,1)S(1)}, u32[]{:S(2)}, u32[]{:S(2)}) %all-to-all-start.2) | async-done | bytes 442400 | tf_op jit(solution)/shard_map/all_to_all | solution.py:213
  67.7 3.8 %all-to-all-start.1 = ((bf16[16,3,4,1152]{3,2,1,0:T(4,128)(2,1)}), bf16[16,3,4,1152]{3,2,1,0:T(4,128)(2,1)S(1)}, u32[]{:S(2)}, u32[]{:S(2)}) async-start(bf16[16,3,4,1152]{3,2,1,0:T(4,128)(2,1)} %bitcast.33), calls=%async_computation.1 | async-start | bytes 884736 | tf_op jit(solution)/shard_map/all_to_all | solution.py:213
  71.6 9.1 %temporal_1.1 = bf16[48,4,1152]{2,1,0:T(4,128)(2,1)} custom-call(bf16[48,4,1152]{2,1,0:T(4,128)(2,1)} %bitcast.32, bf16[1152,3456]{1,0:T(8,128)(2,1)} %weight_ref.3, f32[4,1152]{1,0:T(4,128)} %tile.10.refs_2_.gains_ref), custom_call_target="tpu_custom_call" | custom-call | flops 500000000 | bytes 1048576 | tf_op jit(solution)/shard_map/temporal_1/pallas_call | solution.py:192
  80.6 3.9 %all-to-all-done.1 = bf16[16,3,4,1152]{3,2,1,0:T(4,128)(2,1)S(1)} async-done(((bf16[16,3,4,1152]{3,2,1,0:T(4,128)(2,1)}), bf16[16,3,4,1152]{3,2,1,0:T(4,128)(2,1)S(1)}, u32[]{:S(2)}, u32[]{:S(2)}) %all-to-all-start.1) | async-done | bytes 442400 | tf_op jit(solution)/shard_map/all_to_all | solution.py:213
  84.5 3.8 %all-to-all-start.3 = ((bf16[16,3,4,1152]{3,2,1,0:T(4,128)(2,1)}), bf16[16,3,4,1152]{3,2,1,0:T(4,128)(2,1)S(1)}, u32[]{:S(2)}, u32[]{:S(2)}) async-start(bf16[16,3,4,1152]{3,2,1,0:T(4,128)(2,1)} %bitcast.34), calls=%async_computation.3 | async-start | bytes 884736 | tf_op jit(solution)/shard_map/all_to_all | solution.py:213
  88.3 0.1 stack_reshape_reshape.6
  88.4 12.9 %all-to-all-done.3 = bf16[16,3,4,1152]{3,2,1,0:T(4,128)(2,1)S(1)} async-done(((bf16[16,3,4,1152]{3,2,1,0:T(4,128)(2,1)}), bf16[16,3,4,1152]{3,2,1,0:T(4,128)(2,1)S(1)}, u32[]{:S(2)}, u32[]{:S(2)}) %all-to-all-start.3) | async-done | bytes 442400 | tf_op jit(solution)/shard_map/all_to_all | solution.py:213
  101.3 0.1 stack_reshape_reshape.7
  101.4 1.0 maximum_bitcast_fusion
  (31 shorter events, 0.1 us)
Async XLA Ops:
  0.0 17.1 %copy-start = (bf16[2,1,192,3,1152]{4,2,3,1,0:T(8,128)(2,1)S(1)}, bf16[2,1,192,3,1152]{4,2,3,1,0:T(8,128)(2,1)}, u32[]{:S(2)}) copy-start(bf16[2,1,192,3,1152]{4,2,3,1,0:T(8,128)(2,1)} %param.11) | copy-start | bytes 7962628
  0.0 7.8 %copy-start.13 = (f32[72]{0:T(128)S(1)}, f32[72]{0:T(128)}, u32[]{:S(2)}) copy-start(f32[72]{0:T(128)} %param.21) | copy-start | bytes 868
  0.0 7.8 %copy-start.14 = (f32[72]{0:T(128)S(1)}, f32[72]{0:T(128)}, u32[]{:S(2)}) copy-start(f32[72]{0:T(128)} %param.20) | copy-start | bytes 868
  0.0 7.8 %copy-start.15 = (f32[72]{0:T(128)S(1)}, f32[72]{0:T(128)}, u32[]{:S(2)}) copy-start(f32[72]{0:T(128)} %param.16) | copy-start | bytes 868
  0.0 7.8 %copy-start.16 = (f32[72]{0:T(128)S(1)}, f32[72]{0:T(128)}, u32[]{:S(2)}) copy-start(f32[72]{0:T(128)} %param.15) | copy-start | bytes 868
  2.8 14.3 %collective-permute-start = (bf16[192,1152]{1,0:T(8,128)(2,1)}, bf16[192,1152]{1,0:T(8,128)(2,1)}, u32[]{:S(2)}, u32[]{:S(2)}) collective-permute-start(bf16[192,1152]{1,0:T(8,128)(2,1)} %get-tuple-element.8), channel_id=1, source_target_pairs={{0,1},{1,0},{2,3},{3,2},{4,5},{5,4},{6,7},{7,6},{8,9},{9,8},{10,11... | collective-permute-start | bytes 1327112 | tf_op jit(solution)/shard_map/ppermute | solution.py:245
  5.8 20.8 %collective-permute-start.1 = (bf16[192,1152]{1,0:T(8,128)(2,1)}, bf16[192,1152]{1,0:T(8,128)(2,1)}, u32[]{:S(2)}, u32[]{:S(2)}) collective-permute-start(bf16[192,1152]{1,0:T(8,128)(2,1)} %get-tuple-element.5), channel_id=1, source_target_pairs={{0,1},{1,0},{2,3},{3,2},{4,5},{5,4},{6,7},{7,6},{8,9},{9,8},{10,11... | collective-permute-start | bytes 1327112 | tf_op jit(solution)/shard_map/ppermute | solution.py:245
  5.8 31.2 %collective-permute-start.2 = (bf16[192,1152]{1,0:T(8,128)(2,1)}, bf16[192,1152]{1,0:T(8,128)(2,1)}, u32[]{:S(2)}, u32[]{:S(2)}) collective-permute-start(bf16[192,1152]{1,0:T(8,128)(2,1)} %get-tuple-element.7), channel_id=1, source_target_pairs={{0,1},{1,0},{2,3},{3,2},{4,5},{5,4},{6,7},{7,6},{8,9},{9,8},{10,11... | collective-permute-start | bytes 1327112 | tf_op jit(solution)/shard_map/ppermute | solution.py:245
  7.8 36.9 %collective-permute-start.3 = (bf16[192,1152]{1,0:T(8,128)(2,1)}, bf16[192,1152]{1,0:T(8,128)(2,1)}, u32[]{:S(2)}, u32[]{:S(2)}) collective-permute-start(bf16[192,1152]{1,0:T(8,128)(2,1)} %get-tuple-element.6), channel_id=1, source_target_pairs={{0,1},{1,0},{2,3},{3,2},{4,5},{5,4},{6,7},{7,6},{8,9},{9,8},{10,11... | collective-permute-start | bytes 1327112 | tf_op jit(solution)/shard_map/ppermute | solution.py:245
  8.6 18.0 %copy-start.1 = (bf16[1152,1152]{1,0:T(8,128)(2,1)S(1)}, bf16[1152,1152]{1,0:T(8,128)(2,1)}, u32[]{:S(2)}) copy-start(bf16[1152,1152]{1,0:T(8,128)(2,1)} %refs_4_.3) | copy-start | bytes 7962628
  8.6 18.0 %copy-start.3 = (bf16[2,1,192,1152]{3,2,1,0:T(8,128)(2,1)S(1)}, bf16[2,1,192,1152]{3,2,1,0:T(8,128)(2,1)}, u32[]{:S(2)}) copy-start(bf16[2,1,192,1152]{3,2,1,0:T(8,128)(2,1)} %param.12) | copy-start | bytes 2654212
  17.1 0.7 copy-start.4
  17.8 8.8 %copy-start.7 = (f32[2,1152]{1,0:T(2,128)S(1)}, f32[2,1152]{1,0:T(2,128)}, u32[]{:S(2)}) copy-start(f32[2,1152]{1,0:T(2,128)} %refs_5_.3) | copy-start | bytes 27652
  17.8 8.8 %copy-start.8 = (f32[2,1152]{1,0:T(2,128)S(1)}, f32[2,1152]{1,0:T(2,128)}, u32[]{:S(2)}) copy-start(f32[2,1152]{1,0:T(2,128)} %refs_6_.3) | copy-start | bytes 27652
  17.8 8.8 %copy-start.10 = (f32[2,1152]{1,0:T(2,128)S(1)}, f32[2,1152]{1,0:T(2,128)}, u32[]{:S(2)}) copy-start(f32[2,1152]{1,0:T(2,128)} %refs_7_.3) | copy-start | bytes 27652
  30.4 19.6 %all-to-all-start = ((bf16[16,3,4,1152]{3,2,1,0:T(4,128)(2,1)}), bf16[16,3,4,1152]{3,2,1,0:T(4,128)(2,1)}, u32[]{:S(2)}, u32[]{:S(2)}) async-start(bf16[16,3,4,1152]{3,2,1,0:T(4,128)(2,1)} %bitcast.10), calls=%async_computation | async-start | bytes 884736 | tf_op jit(solution)/shard_map/all_to_all | solution.py:213
  37.0 7.7 %copy-start.2 = (bf16[1152,1152]{1,0:T(8,128)(2,1)S(1)}, bf16[1152,1152]{1,0:T(8,128)(2,1)}, u32[]{:S(2)}) copy-start(bf16[1152,1152]{1,0:T(8,128)(2,1)} %refs_4_.3) | copy-start | bytes 7962628
  37.0 0.9 copy-start.5
  37.9 6.8 %copy-start.9 = (f32[2,1152]{1,0:T(2,128)S(1)}, f32[2,1152]{1,0:T(2,128)}, u32[]{:S(2)}) copy-start(f32[2,1152]{1,0:T(2,128)} %refs_6_.3) | copy-start | bytes 27652
  37.9 6.8 %copy-start.11 = (f32[2,1152]{1,0:T(2,128)S(1)}, f32[2,1152]{1,0:T(2,128)}, u32[]{:S(2)}) copy-start(f32[2,1152]{1,0:T(2,128)} %refs_7_.3) | copy-start | bytes 27652
  47.8 0.8 copy-start.6
  50.0 17.7 %all-to-all-start.2 = ((bf16[16,3,4,1152]{3,2,1,0:T(4,128)(2,1)}), bf16[16,3,4,1152]{3,2,1,0:T(4,128)(2,1)S(1)}, u32[]{:S(2)}, u32[]{:S(2)}) async-start(bf16[16,3,4,1152]{3,2,1,0:T(4,128)(2,1)} %bitcast.31), calls=%async_computation.2 | async-start | bytes 884736 | tf_op jit(solution)/shard_map/all_to_all | solution.py:213
  67.7 3.8 %copy-start.12 = (bf16[16,3,4,1152]{3,2,1,0:T(4,128)(2,1)}, bf16[16,3,4,1152]{3,2,1,0:T(4,128)(2,1)S(1)}, u32[]{:S(2)}) copy-start(bf16[16,3,4,1152]{3,2,1,0:T(4,128)(2,1)S(1)} %all-to-all-done.2) | copy-start | bytes 1327108
  67.7 16.8 %all-to-all-start.1 = ((bf16[16,3,4,1152]{3,2,1,0:T(4,128)(2,1)}), bf16[16,3,4,1152]{3,2,1,0:T(4,128)(2,1)S(1)}, u32[]{:S(2)}, u32[]{:S(2)}) async-start(bf16[16,3,4,1152]{3,2,1,0:T(4,128)(2,1)} %bitcast.33), calls=%async_computation.1 | async-start | bytes 884736 | tf_op jit(solution)/shard_map/all_to_all | solution.py:213
  84.5 16.8 %all-to-all-start.3 = ((bf16[16,3,4,1152]{3,2,1,0:T(4,128)(2,1)}), bf16[16,3,4,1152]{3,2,1,0:T(4,128)(2,1)S(1)}, u32[]{:S(2)}, u32[]{:S(2)}) async-start(bf16[16,3,4,1152]{3,2,1,0:T(4,128)(2,1)} %bitcast.34), calls=%async_computation.3 | async-start | bytes 884736 | tf_op jit(solution)/shard_map/all_to_all | solution.py:213

commit v3 on v2

--- a/solution.py
+++ b/solution.py
@@ -12,8 +12,11 @@
 LANES = 128
 F32 = jnp.float32
 BF16 = jnp.bfloat16
+TEMPORAL_LIMIT = 50 * 2**20
 VMEM_LIMIT = 24 * 2**20
-TEMPORAL_LIMIT = 57 * 2**20
+TLAST = 5 * 10**8
+PLACE = 7 * 10**9
+SHUFFLE_LIMIT = 8 * 2**20
 SMALL, LARGE = 5 * 10**8, 2 * 10**10
 
 
@@ -37,7 +40,8 @@
     )
 
 
-def head_norm(values, gain_row, gather, spread, head_dim):
+def head_norm(values, gain_ref, gather, spread, head_dim):
+    gain_row = jnp.concatenate([gain_ref[...]] * (values.shape[1] // head_dim), axis=1)
     widened = values.astype(F32)
     squares = split_dot(widened * widened, gather)
     factor = lax.rsqrt(squares * (1.0 / head_dim) + EPSILON)
@@ -63,12 +67,11 @@
 def score_kernel(head_dim, video, remotes, *refs):
     qkv_ref = refs[0]
     remote_refs = refs[1 : 1 + remotes]
-    gains_ref, out_ref, query, keys = refs[1 + remotes :]
+    query_gain, key_gain, out_ref, query, keys = refs[1 + remotes :]
     pos_loc, width = query.shape
     scale = math.log2(math.e) / math.sqrt(head_dim)
     gather, spread = segment_masks(width, head_dim)
-    query[...] = head_norm(qkv_ref[video, 0], gains_ref[0:1, :], gather, spread, head_dim)
-    key_gain = gains_ref[1:2, :]
+    query[...] = head_norm(qkv_ref[video, 0], query_gain, gather, spread, head_dim)
     keys[0:pos_loc, :] = head_norm(qkv_ref[video, 1], key_gain, gather, spread, head_dim)
     for j, remote in enumerate(remote_refs):
         place = slice((j + 1) * pos_loc, (j + 2) * pos_loc)
@@ -87,20 +90,20 @@
     return [pl.BlockSpec(memory_space=pltpu.VMEM)] * count
 
 
-def score_weights(video, head_dim, qkv, remote_keys, gains):
+def score_weights(video, head_dim, qkv, remote_keys, query_gain, key_gain):
     _, _, pos_loc, width = qkv.shape
     all_pos = pos_loc * (1 + len(remote_keys))
     heads = width // head_dim
     return pl.pallas_call(
         functools.partial(score_kernel, head_dim, video, len(remote_keys)),
         out_shape=jax.ShapeDtypeStruct((heads, pos_loc, all_pos), BF16),
-        in_specs=in_vmem(2 + len(remote_keys)),
+        in_specs=in_vmem(3 + len(remote_keys)),
         out_specs=pl.BlockSpec(memory_space=pltpu.VMEM),
         scratch_shapes=[pltpu.VMEM((pos_loc, width), BF16), pltpu.VMEM((all_pos, width), BF16)],
         compiler_params=pltpu.CompilerParams(vmem_limit_bytes=VMEM_LIMIT),
         cost_estimate=pl.CostEstimate(flops=SMALL, bytes_accessed=2**20, transcendentals=0),
         name=f"scores_{video}",
-    )(qkv, *remote_keys, gains)
+    )(qkv, *remote_keys, query_gain, key_gain)
 
 
 def attend_kernel(head_dim, video, remotes, sub, *refs):
@@ -143,14 +146,16 @@
     )(weights, qkv, *remote_values, residual, proj, gate, scale, shift)
 
 
-def temporal_kernel(
-    head_dim, tokens, in_ref, weight_ref, gains_ref, out_ref, arranged, query, keys, values, bias, held, arrived
-):
+def temporal_kernel(head_dim, tokens, outer, *refs):
+    me_ref, in_ref, weight_ref, query_gain, key_gain = refs[:5]
+    arranged, query, keys, values, bias, total, held, arrived = refs[-8:]
+    out_refs = refs[5:-8]
     pieces, sub, width = in_ref.shape
-    columns = [slice(i * width, (i + 1) * width) for i in range(3)]
+    cuts = [0, max(width // 4 // 256, 1) * 256, max(width // 2 // 256, 1) * 256, width]
     copies = [
-        pltpu.make_async_copy(weight_ref.at[:, c], held.at[:, c], arrived.at[i])
-        for i, c in enumerate(columns)
+        pltpu.make_async_copy(weight_ref.at[low:high], held.at[low:high], arrived.at[i])
+        for i, (low, high) in enumerate(zip(cuts[:-1], cuts[1:]))
+        if low < high
     ]
     for copy in copies:
         copy.start()
@@ -160,13 +165,18 @@
     for i in range(pieces):
         arranged[i * sub : (i + 1) * sub, :] = in_ref[i].astype(F32)
     incoming = arranged[...].astype(BF16)
-    for i, (place, gain) in enumerate(((query, 2), (keys, 3), (values, None))):
-        copies[i].wait()
-        projected = jnp.dot(
-            incoming, held[:, columns[i]], preferred_element_type=F32
-        ).astype(BF16)
+    half = cuts[2]
+    columns = [slice(i * width, (i + 1) * width) for i in range(3)]
+    for copy in copies[:-1]:
+        copy.wait()
+    for c in columns:
+        total[:, c] = jnp.dot(incoming[:, :half], held[:half, c], preferred_element_type=F32)
+    copies[-1].wait()
+    for place, gain, c in ((query, query_gain, columns[0]), (keys, key_gain, columns[1]), (values, None, columns[2])):
+        rest = jnp.dot(incoming[:, half:], held[half:, c], preferred_element_type=F32)
+        projected = (total[:, c] + rest).astype(BF16)
         if gain is not None:
-            projected = head_norm(projected, gains_ref[gain : gain + 1, :], gather, spread, head_dim)
+            projected = head_norm(projected, gain, gather, spread, head_dim)
         place[...] = projected
     first = lax.broadcasted_iota(jnp.int32, (rows, rows), 0)
     second = lax.broadcasted_iota(jnp.int32, (rows, rows), 1)
@@ -182,29 +192,109 @@
         weights = softmax_rows(scores + bias[...], scale)
         part = jnp.dot(weights, values[:, window], preferred_element_type=F32)
         arranged[:, window] = jnp.where(mask, part, arranged[:, window])
-    for i in range(pieces):
-        out_ref[i] = arranged[i * sub : (i + 1) * sub, :].astype(BF16)
-
-
-def temporal(video, head_dim, tokens, moved, weight, gains):
+    if outer == 1:
+        for i in range(pieces):
+            out_refs[0][i] = arranged[i * sub : (i + 1) * sub, :].astype(BF16)
+        return
+    share = rows // outer
+    me = lax.div(me_ref[0], rows // tokens // outer)
+    for s in range(outer):
+        block = arranged[pl.ds(pl.multiple_of(send_to(me, s, outer) * share, sub), share), :]
+        for i in range(share // sub):
+            out_refs[s][i] = block[i * sub : (i + 1) * sub, :].astype(BF16)
+
+
+def temporal(video, head_dim, tokens, outer, cost, me, moved, weight, gains):
     pieces, sub, width = moved.shape
     rows = pieces * sub
     return pl.pallas_call(
-        functools.partial(temporal_kernel, head_dim, tokens),
-        out_shape=jax.ShapeDtypeStruct(moved.shape, BF16),
-        in_specs=in_vmem(1) + [pl.BlockSpec(memory_space=pltpu.HBM)] + in_vmem(1),
-        out_specs=pl.BlockSpec(memory_space=pltpu.VMEM),
+        functools.partial(temporal_kernel, head_dim, tokens, outer),
+        out_shape=[jax.ShapeDtypeStruct((pieces // outer, sub, width), BF16)] * outer,
+        in_specs=[pl.BlockSpec(memory_space=pltpu.SMEM)]
+        + in_vmem(1)
+        + [pl.BlockSpec(memory_space=pltpu.HBM)]
+        + in_vmem(2),
+        out_specs=in_vmem(outer),
         scratch_shapes=[pltpu.VMEM((rows, width), F32)]
         + [pltpu.VMEM((rows, width), BF16)] * 3
         + [
             pltpu.VMEM((rows, rows), F32),
+            pltpu.VMEM((rows, 3 * width), F32),
             pltpu.VMEM((width, 3 * width), BF16),
             pltpu.SemaphoreType.DMA((3,)),
         ],
         compiler_params=pltpu.CompilerParams(vmem_limit_bytes=TEMPORAL_LIMIT),
-        cost_estimate=pl.CostEstimate(flops=SMALL, bytes_accessed=2**20, transcendentals=0),
+        cost_estimate=pl.CostEstimate(flops=cost, bytes_accessed=2**20, transcendentals=0),
         name=f"temporal_{video}",
-    )(moved, weight, gains)
+    )(me, moved, weight, *gains)
+
+
+def send_to(me, step, count):
+    return me ^ step if count & (count - 1) == 0 else lax.rem(me + step, count)
+
+
+def come_from(me, step, count):
+    return me ^ step if count & (count - 1) == 0 else lax.rem(me + count - step, count)
+
+
+def partners(step, count):
+    return [i ^ step if count & (count - 1) == 0 else (i + step) % count for i in range(count)]
+
+
+def regroup_kernel(outer, inner, me_ref, *refs):
+    share = refs[0].shape[0] // inner
+    me = lax.rem(me_ref[0], inner)
+    for t in range(inner):
+        to = send_to(me, t, inner)
+        for s in range(outer):
+            refs[outer + t][s * share : (s + 1) * share] = refs[s][pl.ds(to * share, share)]
+
+
+def place_kernel(outer, inner, me_ref, *refs):
+    share = refs[0].shape[0] // outer
+    me = me_ref[0]
+    for t in range(inner):
+        low = come_from(lax.rem(me, inner), t, inner)
+        for s in range(outer):
+            high = come_from(lax.div(me, inner), s, outer)
+            refs[inner][pl.ds((high * inner + low) * share, share)] = refs[t][
+                s * share : (s + 1) * share
+            ]
+
+
+def shuffle(kernel, name, cost, outer, inner, me, arrays, shapes):
+    return pl.pallas_call(
+        functools.partial(kernel, outer, inner),
+        out_shape=[jax.ShapeDtypeStruct(shape, BF16) for shape in shapes],
+        in_specs=[pl.BlockSpec(memory_space=pltpu.SMEM)] + in_vmem(len(arrays)),
+        out_specs=in_vmem(len(shapes)),
+        compiler_params=pltpu.CompilerParams(vmem_limit_bytes=SHUFFLE_LIMIT),
+        cost_estimate=pl.CostEstimate(flops=cost, bytes_accessed=2**20, transcendentals=0),
+        name=name,
+    )(me, *arrays)
+
+
+def way_back(blocks, me, outer, inner):
+    pieces, sub, width = blocks[0].shape
+    count = outer * inner
+    held = [blocks[0]]
+    for s in range(1, outer):
+        to = partners(s, outer)
+        pairs = [(i, to[i // inner] * inner + i % inner) for i in range(count)]
+        held.append(lax.ppermute(blocks[s], "frame", pairs))
+    share = pieces // inner
+    grouped = shuffle(
+        regroup_kernel, "regroup", 1000, outer, inner, me, held, [(outer * share, sub, width)] * inner
+    )
+    held = [grouped[0]]
+    for t in range(1, inner):
+        to = partners(t, inner)
+        pairs = [(i, i // inner * inner + to[i % inner]) for i in range(count)]
+        held.append(lax.ppermute(grouped[t], "frame", pairs))
+    (placed,) = shuffle(
+        place_kernel, "place", PLACE, outer, inner, me, held, [(count * share, sub, width)]
+    )
+    return placed
 
 
 def exchange(blocks, frame_count):
@@ -229,12 +319,14 @@
 ):
     videos, frames_loc, pos_loc, _, width = spatial_qkv.shape
     head_dim = spatial_qgain.shape[0]
-    heads = width // head_dim
     pos_count = lax.axis_size("pos")
     frame_count = lax.axis_size("frame")
     assert frames_loc == 1
     tokens = pos_loc // frame_count
     sub = math.gcd(tokens, 8)
+    inner = math.gcd(frame_count, 4)
+    outer = frame_count // inner
+    me = lax.axis_index("frame").astype(jnp.int32).reshape(1)
     qkv = jnp.transpose(spatial_qkv.reshape(videos, pos_loc, 3, width), (0, 2, 1, 3))
     residual = residual.reshape(videos, pos_loc, width)
     steps = [[(i, (i + s) % pos_count) for i in range(pos_count)] for s in range(1, pos_count)]
@@ -243,20 +335,30 @@
         for which in (2, 1):
             own = qkv[video, which]
             remotes[video, which] = [lax.ppermute(own, "pos", step) for step in steps]
-    gains = jnp.tile(
-        jnp.stack([spatial_qgain, spatial_kgain, temporal_qgain, temporal_kgain]), (1, heads)
-    )
+    spatial_gains = [g.reshape(1, head_dim) for g in (spatial_qgain, spatial_kgain)]
+    temporal_gains = [g.reshape(1, head_dim) for g in (temporal_qgain, temporal_kgain)]
     results = []
+    waiting = []
+    blocks = ()
     for video in range(videos):
-        weights = score_weights(video, head_dim, qkv, remotes[video, 1], gains)
+        weights = score_weights(video, head_dim, qkv, remotes[video, 1], *spatial_gains)
         normed = attend(
             video, head_dim, sub, LARGE if video == videos - 1 else SMALL, weights, qkv, remotes[video, 2], residual,
             spatial_proj, spatial_gate, temporal_scale, temporal_shift,
         )
+        if video > 0:
+            normed, moved = lax.optimization_barrier((normed, moved))
         moved = exchange(normed, frame_count)
-        result = temporal(video, head_dim, tokens, moved, temporal_qkv, gains)
-        back = exchange(result, frame_count)
-        results.append(back.reshape(pos_loc, width))
+        if video < videos - 1:
+            blocks = temporal(video, head_dim, tokens, outer, SMALL, me, moved, temporal_qkv, temporal_gains)
+            waiting.append(blocks)
+        else:
+            if video > 0:
+                moved, _ = lax.optimization_barrier((moved, blocks))
+            (result,) = temporal(video, head_dim, tokens, 1, TLAST, me, moved, temporal_qkv, temporal_gains)
+            results.append(exchange(result, frame_count))
+    results = [way_back(blocks, me, outer, inner) for blocks in waiting] + results
+    results = [r.reshape(pos_loc, width) for r in results]
     return jnp.stack(results).reshape(videos, frames_loc, pos_loc, width)
 
 

time: 103 us -> 95.3 us (0.925)
  waiting for transfers between devices: 36.8 us -> 30.8 us
  starting transfers between devices: 23.9 us -> 29 us
  Pallas kernels: 34.5 us -> 30.1 us
  local copies, waits for them, and re-layouts: 6.1 us -> 3.69 us
    all_to_all x4 -> x3, waiting for transfers between devices: 22.2 us -> 2.96 us  [exchange(): lax.all_to_all(split, 'frame', split_axis=0, concat_axis=0, tiled=True)]
    ppermute x0 -> x6, waiting for transfers between devices: none -> 8.93 us  [the longest x3 8.92 us: way_back(): held.append(lax.ppermute(grouped[t], 'frame', pairs))]
    ppermute x0 -> x6, starting transfers between devices: none -> 6.64 us  [the longest x3 4.48 us: way_back(): held.append(lax.ppermute(blocks[s], 'frame', pairs))]
    ppermute x4, waiting for transfers between devices: 14.6 us -> 18.9 us  [per_device(): remotes[video, which] = [lax.ppermute(own, 'pos', step) for step in steps]]
    pallas_call x2 -> x4, Pallas kernels: 18.1 us -> 16 us  [the longest x2 15.9 us: temporal(): pl.pallas_call(functools.partial(temporal_kernel, head_dim, tokens, outer...]
    pallas_call x2, Pallas kernels: 9.39 us -> 7.3 us  [score_weights(): pl.pallas_call(functools.partial(score_kernel, head_dim, video, len(remot...]
    unnamed x34 -> x30, local copies, waits for them, and re-layouts: 2.4 us -> 0.88 us
    all_to_all x4 -> x3, starting transfers between devices: 18.8 us -> 17.4 us  [exchange(): lax.all_to_all(split, 'frame', split_axis=0, concat_axis=0, tiled=True)]
  transfers between devices with their start and end apart: 8 -> 13, of which waited for: 7 -> 8; matrix products, arithmetic and copies ran while one was open for 1% -> 0% of each run, Pallas kernels for 34% -> 32%
where the time goes in v3:
time: 95.3 us; the launch traced here: 94.8 us
  waiting for transfers between devices  30.8 us (32%)
  Pallas kernels  30.1 us (32%)
  starting transfers between devices  29 us (30%)
  local copies, waits for them, and re-layouts  3.69 us (4%)
  other arithmetic  1 us (1%)
    ppermute x4, waiting for transfers between devices, per_device(): remotes[video, which] = [lax.ppermute(own, 'pos', step) for step in steps]  18.9 us
    all_to_all x3, starting transfers between devices, exchange(): lax.all_to_all(split, 'frame', split_axis=0, concat_axis=0, tiled=True)  17.4 us
    pallas_call x2, Pallas kernels, temporal(): pl.pallas_call(functools.partial(temporal_kernel, head_dim, tokens, outer...  15.9 us
    ppermute x3, waiting for transfers between devices, way_back(): held.append(lax.ppermute(grouped[t], 'frame', pairs))  8.92 us
    pallas_call x2, Pallas kernels, score_weights(): pl.pallas_call(functools.partial(score_kernel, head_dim, video, len(remot...  7.3 us
    pallas_call x2, Pallas kernels, attend(): pl.pallas_call(functools.partial(attend_kernel, head_dim, video, len(remo...  6.79 us
    ppermute x4, starting transfers between devices, per_device(): remotes[video, which] = [lax.ppermute(own, 'pos', step) for step in steps]  5.02 us
    ppermute x3, starting transfers between devices, way_back(): held.append(lax.ppermute(blocks[s], 'frame', pairs))  4.48 us
  transfers between devices with their start and end apart: 13, of which 8 were waited for; matrix products, arithmetic and copies ran while one was open for 0% of the time, Pallas kernels for 32%

profile of v3, /device:TPU:0, one launch (start us, length us, event | category | flops | bytes accessed | tf_op | source)
XLA Modules:
  0.0 94.8 jit_solution(3976002937721303969)
XLA Ops:
  0.0 2.6 %slice_bitcast_fusion.2 = (bf16[192,1152]{1,0:T(8,128)(2,1)S(1)}, bf16[192,1152]{1,0:T(8,128)(2,1)}, bf16[192,1152]{1,0:T(8,128)(2,1)}, bf16[192,1152]{1,0:T(8,128)(2,1)S(1)}) fusion(bf16[2,3,192,1152]{3,2,1,0:T(8,128)(2,1)} %bitcast.24), kind=kLoop, calls=%fused_computation.3 | loop fusion | bytes 3538944 | tf_op jit(solution)/shard_map/squeeze | solution.py:336
  2.6 2.9 %collective-permute-start = (bf16[192,1152]{1,0:T(8,128)(2,1)S(1)}, bf16[192,1152]{1,0:T(8,128)(2,1)S(1)}, u32[]{:S(2)}, u32[]{:S(2)}) collective-permute-start(bf16[192,1152]{1,0:T(8,128)(2,1)S(1)} %get-tuple-element.28), channel_id=1, source_target_pairs={{0,1},{1,0},{2,3},{3,2},{4,5},{5,4},{6,7},{7,6},{8,9},{9,8},{10,11... | collective-permute-start | bytes 1327112 | tf_op jit(solution)/shard_map/ppermute | solution.py:337
  5.6 2.0 %collective-permute-start.8 = (bf16[192,1152]{1,0:T(8,128)(2,1)}, bf16[192,1152]{1,0:T(8,128)(2,1)S(1)}, u32[]{:S(2)}, u32[]{:S(2)}) collective-permute-start(bf16[192,1152]{1,0:T(8,128)(2,1)} %get-tuple-element.27), channel_id=1, source_target_pairs={{0,1},{1,0},{2,3},{3,2},{4,5},{5,4},{6,7},{7,6},{8,9},{9,8},{10,11... | collective-permute-start | bytes 1327112 | tf_op jit(solution)/shard_map/ppermute | solution.py:337
  7.6 0.0 collective-permute-start.9
  7.6 8.9 %collective-permute-done.refs_1_ = bf16[192,1152]{1,0:T(8,128)(2,1)S(1)} collective-permute-done((bf16[192,1152]{1,0:T(8,128)(2,1)S(1)}, bf16[192,1152]{1,0:T(8,128)(2,1)S(1)}, u32[]{:S(2)}, u32[]{:S(2)}) %collective-permute-start) | collective-permute-done | bytes 442400 | tf_op jit(solution)/shard_map/ppermute | solution.py:337
  16.6 3.6 %scores_0.1.refs_0_ = bf16[16,192,384]{2,1,0:T(8,128)(2,1)S(1)} custom-call(bf16[2,3,192,1152]{3,2,1,0:T(8,128)(2,1)S(1)} %bitcast.25, bf16[192,1152]{1,0:T(8,128)(2,1)S(1)} %collective-permute-done.refs_1_, f32[1,72]{1,0:T(1,128)S(1)} %bitcast.33, f32[1,72]{1,0:T(1,128)S(1)} %bitcast.35), custom_call_target="tpu_custom_call" | custom-call | flops 500000000 | bytes 1048576 | tf_op jit(solution)/shard_map/scores_0/pallas_call | solution.py:97
  20.3 5.8 %collective-permute-done.1.refs_2_ = bf16[192,1152]{1,0:T(8,128)(2,1)S(1)} collective-permute-done((bf16[192,1152]{1,0:T(8,128)(2,1)S(1)}, bf16[192,1152]{1,0:T(8,128)(2,1)S(1)}, u32[]{:S(2)}, u32[]{:S(2)}) %collective-permute-start.1) | collective-permute-done | bytes 442400 | tf_op jit(solution)/shard_map/ppermute | solution.py:337
  26.1 2.9 %attend_0.1 = bf16[48,4,1152]{2,1,0:T(4,128)(2,1)} custom-call(bf16[16,192,384]{2,1,0:T(8,128)(2,1)S(1)} %scores_0.1.refs_0_, bf16[2,3,192,1152]{3,2,1,0:T(8,128)(2,1)S(1)} %bitcast.26, bf16[192,1152]{1,0:T(8,128)(2,1)S(1)} %collective-permute-done.1.refs_2_, bf16[2,192,1152]{2,1,0:T(8,128)(2,1)S(1)} %bitcast.31, bf16[1152,1152]{1,0:T(8,128)(2,1)S(1)} %copy-done.1, ...), custom_call_target="tpu_custom_call" | custom-call | flops 500000000 | bytes 1048576 | tf_op jit(solution)/shard_map/attend_0/pallas_call | solution.py:137
  29.0 6.5 %all-to-all-start = ((bf16[16,3,4,1152]{3,2,1,0:T(4,128)(2,1)}), bf16[16,3,4,1152]{3,2,1,0:T(4,128)(2,1)S(1)}, u32[]{:S(2)}, u32[]{:S(2)}) async-start(bf16[16,3,4,1152]{3,2,1,0:T(4,128)(2,1)} %bitcast.9), calls=%async_computation | async-start | bytes 884736 | tf_op jit(solution)/shard_map/all_to_all | solution.py:303
  35.6 0.8 copy-done.12
  36.4 3.7 %scores_1.1.refs_0_ = bf16[16,192,384]{2,1,0:T(8,128)(2,1)S(1)} custom-call(bf16[2,3,192,1152]{3,2,1,0:T(8,128)(2,1)S(1)} %bitcast.27, bf16[192,1152]{1,0:T(8,128)(2,1)S(1)} %collective-permute-done.8.refs_1_, f32[1,72]{1,0:T(1,128)S(1)} %bitcast.34, f32[1,72]{1,0:T(1,128)S(1)} %bitcast.36), custom_call_target="tpu_custom_call" | custom-call | flops 500000000 | bytes 1048576 | tf_op jit(solution)/shard_map/scores_1/pallas_call | solution.py:97
  40.1 4.2 %collective-permute-done.9.refs_2_ = bf16[192,1152]{1,0:T(8,128)(2,1)} collective-permute-done((bf16[192,1152]{1,0:T(8,128)(2,1)}, bf16[192,1152]{1,0:T(8,128)(2,1)}, u32[]{:S(2)}, u32[]{:S(2)}) %collective-permute-start.9) | collective-permute-done | bytes 442400 | tf_op jit(solution)/shard_map/ppermute | solution.py:337
  44.3 3.9 %attend_1.1 = bf16[48,4,1152]{2,1,0:T(4,128)(2,1)} custom-call(bf16[16,192,384]{2,1,0:T(8,128)(2,1)S(1)} %scores_1.1.refs_0_, bf16[2,3,192,1152]{3,2,1,0:T(8,128)(2,1)S(1)} %bitcast.28, bf16[192,1152]{1,0:T(8,128)(2,1)} %collective-permute-done.9.refs_2_, bf16[2,192,1152]{2,1,0:T(8,128)(2,1)S(1)} %bitcast.32, bf16[1152,1152]{1,0:T(8,128)(2,1)S(1)} %copy-done.2, ...), custom_call_target="tpu_custom_call" | custom-call | flops 20000000000 | bytes 1048576 | tf_op jit(solution)/shard_map/attend_1/pallas_call | solution.py:137
  48.1 0.4 all-to-all-done
  48.5 5.8 %all-to-all-start.1 = ((bf16[16,3,4,1152]{3,2,1,0:T(4,128)(2,1)}), bf16[16,3,4,1152]{3,2,1,0:T(4,128)(2,1)S(1)}, u32[]{:S(2)}, u32[]{:S(2)}) async-start(bf16[16,3,4,1152]{3,2,1,0:T(4,128)(2,1)} %bitcast.15), calls=%async_computation.1 | async-start | bytes 884736 | tf_op jit(solution)/shard_map/all_to_all | solution.py:303
  54.4 7.5 %temporal_0.1 = (bf16[12,4,1152]{2,1,0:T(4,128)(2,1)S(1)}, bf16[12,4,1152]{2,1,0:T(4,128)(2,1)S(1)}, bf16[12,4,1152]{2,1,0:T(4,128)(2,1)S(1)}, bf16[12,4,1152]{2,1,0:T(4,128)(2,1)S(1)}) custom-call(s32[1]{0:T(128)} %bitcast.refs_0_.me_ref, bf16[48,4,1152]{2,1,0:T(4,128)(2,1)S(1)} %bitcast.29, bf16[1152,3456]{1,0:T(8,128)(2,1)} %refs_2_.3, ...), custom_call_target="tpu_custom_call" | custom-call | flops 500000000 | bytes 1048576 | tf_op jit(solution)/shard_map/temporal_0/pallas_call | solution.py:210
  61.9 2.0 %collective-permute-start.2 = (bf16[12,4,1152]{2,1,0:T(4,128)(2,1)S(1)}, bf16[12,4,1152]{2,1,0:T(4,128)(2,1)S(1)}, u32[]{:S(2)}, u32[]{:S(2)}) collective-permute-start(bf16[12,4,1152]{2,1,0:T(4,128)(2,1)S(1)} %get-tuple-element.16), channel_id=1, source_target_pairs={{0,8},{2,10},{4,12},{6,14},{8,0},{10,2},{12,4},{14,6},{16,24},{18,... | collective-permute-start | bytes 331784 | tf_op jit(solution)/shard_map/ppermute | solution.py:284
  63.9 2.4 %collective-permute-start.3 = (bf16[12,4,1152]{2,1,0:T(4,128)(2,1)S(1)}, bf16[12,4,1152]{2,1,0:T(4,128)(2,1)S(1)}, u32[]{:S(2)}, u32[]{:S(2)}) collective-permute-start(bf16[12,4,1152]{2,1,0:T(4,128)(2,1)S(1)} %get-tuple-element.17), channel_id=1, source_target_pairs={{0,16},{2,18},{4,20},{6,22},{8,24},{10,26},{12,28},{14,30},{16,0},... | collective-permute-start | bytes 331784 | tf_op jit(solution)/shard_map/ppermute | solution.py:284
  66.3 0.1 collective-permute-start.4
  66.4 0.9 all-to-all-done.1
  67.4 8.3 %temporal_1.1 = bf16[48,4,1152]{2,1,0:T(4,128)(2,1)} custom-call(s32[1]{0:T(128)} %bitcast.refs_0_.me_ref, bf16[48,4,1152]{2,1,0:T(4,128)(2,1)S(1)} %bitcast.30, bf16[1152,3456]{1,0:T(8,128)(2,1)} %refs_2_.3, f32[1,72]{1,0:T(1,128)S(1)} %bitcast.38, f32[1,72]{1,0:T(1,128)S(1)} %bitcast.40), custom_call_target="tpu_custom_call" | custom-call | flops 500000000 | bytes 1048576 | tf_op jit(solution)/shard_map/temporal_1/pallas_call | solution.py:210
  75.7 5.0 %all-to-all-start.2 = ((bf16[16,3,4,1152]{3,2,1,0:T(4,128)(2,1)}), bf16[16,3,4,1152]{3,2,1,0:T(4,128)(2,1)S(1)}, u32[]{:S(2)}, u32[]{:S(2)}) async-start(bf16[16,3,4,1152]{3,2,1,0:T(4,128)(2,1)} %bitcast.17), calls=%async_computation.2 | async-start | bytes 884736 | tf_op jit(solution)/shard_map/all_to_all | solution.py:303
  80.8 0.1 regroup.1
  80.8 0.5 collective-permute-start.5
  81.3 1.7 %collective-permute-start.6 = (bf16[12,4,1152]{2,1,0:T(4,128)(2,1)S(1)}, bf16[12,4,1152]{2,1,0:T(4,128)(2,1)S(1)}, u32[]{:S(2)}, u32[]{:S(2)}) collective-permute-start(bf16[12,4,1152]{2,1,0:T(4,128)(2,1)S(1)} %get-tuple-element.21), channel_id=1, source_target_pairs={{0,4},{2,6},{4,0},{6,2},{8,12},{10,14},{12,8},{14,10},{16,20},{18,... | collective-permute-start | bytes 331784 | tf_op jit(solution)/shard_map/ppermute | solution.py:293
  83.0 7.1 %collective-permute-done.6.refs_2_ = bf16[12,4,1152]{2,1,0:T(4,128)(2,1)S(1)} collective-permute-done((bf16[12,4,1152]{2,1,0:T(4,128)(2,1)S(1)}, bf16[12,4,1152]{2,1,0:T(4,128)(2,1)S(1)}, u32[]{:S(2)}, u32[]{:S(2)}) %collective-permute-start.6) | collective-permute-done | bytes 110624 | tf_op jit(solution)/shard_map/ppermute | solution.py:293
  90.1 1.8 %collective-permute-done.7.refs_3_ = bf16[12,4,1152]{2,1,0:T(4,128)(2,1)S(1)} collective-permute-done((bf16[12,4,1152]{2,1,0:T(4,128)(2,1)S(1)}, bf16[12,4,1152]{2,1,0:T(4,128)(2,1)S(1)}, u32[]{:S(2)}, u32[]{:S(2)}) %collective-permute-start.7) | collective-permute-done | bytes 110624 | tf_op jit(solution)/shard_map/ppermute | solution.py:293
  91.9 0.1 place.1
  92.0 0.1 stack_reshape.3
  92.1 1.7 %all-to-all-done.2 = bf16[16,3,4,1152]{3,2,1,0:T(4,128)(2,1)S(1)} async-done(((bf16[16,3,4,1152]{3,2,1,0:T(4,128)(2,1)}), bf16[16,3,4,1152]{3,2,1,0:T(4,128)(2,1)S(1)}, u32[]{:S(2)}, u32[]{:S(2)}) %all-to-all-start.2) | async-done | bytes 442400 | tf_op jit(solution)/shard_map/all_to_all | solution.py:303
  93.7 0.1 stack_reshape_reshape.3
  93.8 1.0 %maximum_bitcast_fusion = bf16[2,1,192,1152]{3,2,1,0:T(8,128)(2,1)} fusion(bf16[1,192,1152]{2,1,0:T(8,128)(2,1)S(1)} %stack_reshape_reshape.3, bf16[1,192,1152]{2,1,0:T(8,128)(2,1)S(1)} %stack_reshape.3), kind=kLoop, calls=%fused_computation | loop fusion | flops 442368 | bytes 1769472 | tf_op jit(solution)/shard_map/reshape | solution.py:362
  (36 shorter events, 0.1 us)
Async XLA Ops:
  0.0 16.6 %copy-start = (bf16[2,1,192,3,1152]{4,2,3,1,0:T(8,128)(2,1)S(1)}, bf16[2,1,192,3,1152]{4,2,3,1,0:T(8,128)(2,1)}, u32[]{:S(2)}) copy-start(bf16[2,1,192,3,1152]{4,2,3,1,0:T(8,128)(2,1)} %param.11) | copy-start | bytes 7962628
  0.0 16.6 %copy-start.10 = (f32[72]{0:T(128)S(1)}, f32[72]{0:T(128)}, u32[]{:S(2)}) copy-start(f32[72]{0:T(128)} %param.15) | copy-start | bytes 868
  0.0 16.6 %copy-start.11 = (f32[72]{0:T(128)S(1)}, f32[72]{0:T(128)}, u32[]{:S(2)}) copy-start(f32[72]{0:T(128)} %param.16) | copy-start | bytes 868
  2.6 13.9 %collective-permute-start = (bf16[192,1152]{1,0:T(8,128)(2,1)S(1)}, bf16[192,1152]{1,0:T(8,128)(2,1)S(1)}, u32[]{:S(2)}, u32[]{:S(2)}) collective-permute-start(bf16[192,1152]{1,0:T(8,128)(2,1)S(1)} %get-tuple-element.28), channel_id=1, source_target_pairs={{0,1},{1,0},{2,3},{3,2},{4,5},{5,4},{6,7},{7,6},{8,9},{9,8},{10,11... | collective-permute-start | bytes 1327112 | tf_op jit(solution)/shard_map/ppermute | solution.py:337
  5.6 20.5 %collective-permute-start.1 = (bf16[192,1152]{1,0:T(8,128)(2,1)S(1)}, bf16[192,1152]{1,0:T(8,128)(2,1)S(1)}, u32[]{:S(2)}, u32[]{:S(2)}) collective-permute-start(bf16[192,1152]{1,0:T(8,128)(2,1)S(1)} %get-tuple-element.25), channel_id=1, source_target_pairs={{0,1},{1,0},{2,3},{3,2},{4,5},{5,4},{6,7},{7,6},{8,9},{9,8},{10,11... | collective-permute-start | bytes 1327112 | tf_op jit(solution)/shard_map/ppermute | solution.py:337
  5.6 30.0 %collective-permute-start.8 = (bf16[192,1152]{1,0:T(8,128)(2,1)}, bf16[192,1152]{1,0:T(8,128)(2,1)S(1)}, u32[]{:S(2)}, u32[]{:S(2)}) collective-permute-start(bf16[192,1152]{1,0:T(8,128)(2,1)} %get-tuple-element.27), channel_id=1, source_target_pairs={{0,1},{1,0},{2,3},{3,2},{4,5},{5,4},{6,7},{7,6},{8,9},{9,8},{10,11... | collective-permute-start | bytes 1327112 | tf_op jit(solution)/shard_map/ppermute | solution.py:337
  7.6 36.7 %collective-permute-start.9 = (bf16[192,1152]{1,0:T(8,128)(2,1)}, bf16[192,1152]{1,0:T(8,128)(2,1)}, u32[]{:S(2)}, u32[]{:S(2)}) collective-permute-start(bf16[192,1152]{1,0:T(8,128)(2,1)} %get-tuple-element.26), channel_id=1, source_target_pairs={{0,1},{1,0},{2,3},{3,2},{4,5},{5,4},{6,7},{7,6},{8,9},{9,8},{10,11... | collective-permute-start | bytes 1327112 | tf_op jit(solution)/shard_map/ppermute | solution.py:337
  16.6 9.5 %copy-start.1 = (bf16[1152,1152]{1,0:T(8,128)(2,1)S(1)}, bf16[1152,1152]{1,0:T(8,128)(2,1)}, u32[]{:S(2)}) copy-start(bf16[1152,1152]{1,0:T(8,128)(2,1)} %refs_4_.3) | copy-start | bytes 7962628
  16.6 9.5 %copy-start.3 = (bf16[2,1,192,1152]{3,2,1,0:T(8,128)(2,1)S(1)}, bf16[2,1,192,1152]{3,2,1,0:T(8,128)(2,1)}, u32[]{:S(2)}) copy-start(bf16[2,1,192,1152]{3,2,1,0:T(8,128)(2,1)} %param.12) | copy-start | bytes 2654212
  16.6 9.5 %copy-start.5 = (f32[2,1152]{1,0:T(2,128)S(1)}, f32[2,1152]{1,0:T(2,128)}, u32[]{:S(2)}) copy-start(f32[2,1152]{1,0:T(2,128)} %refs_5_.3) | copy-start | bytes 27652
  16.6 9.4 %copy-start.6 = (f32[2,1152]{1,0:T(2,128)S(1)}, f32[2,1152]{1,0:T(2,128)}, u32[]{:S(2)}) copy-start(f32[2,1152]{1,0:T(2,128)} %refs_6_.3) | copy-start | bytes 27652
  16.6 9.4 %copy-start.8 = (f32[2,1152]{1,0:T(2,128)S(1)}, f32[2,1152]{1,0:T(2,128)}, u32[]{:S(2)}) copy-start(f32[2,1152]{1,0:T(2,128)} %refs_7_.3) | copy-start | bytes 27652
  29.0 19.5 %all-to-all-start = ((bf16[16,3,4,1152]{3,2,1,0:T(4,128)(2,1)}), bf16[16,3,4,1152]{3,2,1,0:T(4,128)(2,1)S(1)}, u32[]{:S(2)}, u32[]{:S(2)}) async-start(bf16[16,3,4,1152]{3,2,1,0:T(4,128)(2,1)} %bitcast.9), calls=%async_computation | async-start | bytes 884736 | tf_op jit(solution)/shard_map/all_to_all | solution.py:303
  35.5 8.8 %copy-start.2 = (bf16[1152,1152]{1,0:T(8,128)(2,1)S(1)}, bf16[1152,1152]{1,0:T(8,128)(2,1)}, u32[]{:S(2)}) copy-start(bf16[1152,1152]{1,0:T(8,128)(2,1)} %refs_4_.3) | copy-start | bytes 7962628
  35.5 8.7 %copy-start.4 = (bf16[2,1,192,1152]{3,2,1,0:T(8,128)(2,1)S(1)}, bf16[2,1,192,1152]{3,2,1,0:T(8,128)(2,1)}, u32[]{:S(2)}) copy-start(bf16[2,1,192,1152]{3,2,1,0:T(8,128)(2,1)} %param.12) | copy-start | bytes 2654212
  35.5 8.7 %copy-start.7 = (f32[2,1152]{1,0:T(2,128)S(1)}, f32[2,1152]{1,0:T(2,128)}, u32[]{:S(2)}) copy-start(f32[2,1152]{1,0:T(2,128)} %refs_6_.3) | copy-start | bytes 27652
  35.5 8.7 %copy-start.9 = (f32[2,1152]{1,0:T(2,128)S(1)}, f32[2,1152]{1,0:T(2,128)}, u32[]{:S(2)}) copy-start(f32[2,1152]{1,0:T(2,128)} %refs_7_.3) | copy-start | bytes 27652
  35.6 0.8 copy-start.12
  40.0 14.3 %copy-start.13 = (f32[72]{0:T(128)S(1)}, f32[72]{0:T(128)}, u32[]{:S(2)}) copy-start(f32[72]{0:T(128)} %param.20) | copy-start | bytes 868
  40.0 14.3 %copy-start.14 = (f32[72]{0:T(128)S(1)}, f32[72]{0:T(128)}, u32[]{:S(2)}) copy-start(f32[72]{0:T(128)} %param.21) | copy-start | bytes 868
  48.5 18.9 %all-to-all-start.1 = ((bf16[16,3,4,1152]{3,2,1,0:T(4,128)(2,1)}), bf16[16,3,4,1152]{3,2,1,0:T(4,128)(2,1)S(1)}, u32[]{:S(2)}, u32[]{:S(2)}) async-start(bf16[16,3,4,1152]{3,2,1,0:T(4,128)(2,1)} %bitcast.15), calls=%async_computation.1 | async-start | bytes 884736 | tf_op jit(solution)/shard_map/all_to_all | solution.py:303
  61.9 18.8 %collective-permute-start.2 = (bf16[12,4,1152]{2,1,0:T(4,128)(2,1)S(1)}, bf16[12,4,1152]{2,1,0:T(4,128)(2,1)S(1)}, u32[]{:S(2)}, u32[]{:S(2)}) collective-permute-start(bf16[12,4,1152]{2,1,0:T(4,128)(2,1)S(1)} %get-tuple-element.16), channel_id=1, source_target_pairs={{0,8},{2,10},{4,12},{6,14},{8,0},{10,2},{12,4},{14,6},{16,24},{18,... | collective-permute-start | bytes 331784 | tf_op jit(solution)/shard_map/ppermute | solution.py:284
  63.9 16.9 %collective-permute-start.3 = (bf16[12,4,1152]{2,1,0:T(4,128)(2,1)S(1)}, bf16[12,4,1152]{2,1,0:T(4,128)(2,1)S(1)}, u32[]{:S(2)}, u32[]{:S(2)}) collective-permute-start(bf16[12,4,1152]{2,1,0:T(4,128)(2,1)S(1)} %get-tuple-element.17), channel_id=1, source_target_pairs={{0,16},{2,18},{4,20},{6,22},{8,24},{10,26},{12,28},{14,30},{16,0},... | collective-permute-start | bytes 331784 | tf_op jit(solution)/shard_map/ppermute | solution.py:284
  66.3 14.5 %collective-permute-start.4 = (bf16[12,4,1152]{2,1,0:T(4,128)(2,1)S(1)}, bf16[12,4,1152]{2,1,0:T(4,128)(2,1)S(1)}, u32[]{:S(2)}, u32[]{:S(2)}) collective-permute-start(bf16[12,4,1152]{2,1,0:T(4,128)(2,1)S(1)} %get-tuple-element.18), channel_id=1, source_target_pairs={{0,24},{2,26},{4,28},{6,30},{8,16},{10,18},{12,20},{14,22},{16,8},... | collective-permute-start | bytes 331784 | tf_op jit(solution)/shard_map/ppermute | solution.py:284
  75.7 18.0 %all-to-all-start.2 = ((bf16[16,3,4,1152]{3,2,1,0:T(4,128)(2,1)}), bf16[16,3,4,1152]{3,2,1,0:T(4,128)(2,1)S(1)}, u32[]{:S(2)}, u32[]{:S(2)}) async-start(bf16[16,3,4,1152]{3,2,1,0:T(4,128)(2,1)} %bitcast.17), calls=%async_computation.2 | async-start | bytes 884736 | tf_op jit(solution)/shard_map/all_to_all | solution.py:303
  80.8 2.2 %collective-permute-start.5 = (bf16[12,4,1152]{2,1,0:T(4,128)(2,1)S(1)}, bf16[12,4,1152]{2,1,0:T(4,128)(2,1)S(1)}, u32[]{:S(2)}, u32[]{:S(2)}) collective-permute-start(bf16[12,4,1152]{2,1,0:T(4,128)(2,1)S(1)} %get-tuple-element.20), channel_id=1, source_target_pairs={{0,2},{2,0},{4,6},{6,4},{8,10},{10,8},{12,14},{14,12},{16,18},{18,... | collective-permute-start | bytes 331784 | tf_op jit(solution)/shard_map/ppermute | solution.py:293
  81.3 8.8 %collective-permute-start.6 = (bf16[12,4,1152]{2,1,0:T(4,128)(2,1)S(1)}, bf16[12,4,1152]{2,1,0:T(4,128)(2,1)S(1)}, u32[]{:S(2)}, u32[]{:S(2)}) collective-permute-start(bf16[12,4,1152]{2,1,0:T(4,128)(2,1)S(1)} %get-tuple-element.21), channel_id=1, source_target_pairs={{0,4},{2,6},{4,0},{6,2},{8,12},{10,14},{12,8},{14,10},{16,20},{18,... | collective-permute-start | bytes 331784 | tf_op jit(solution)/shard_map/ppermute | solution.py:293
  83.0 8.9 %collective-permute-start.7 = (bf16[12,4,1152]{2,1,0:T(4,128)(2,1)S(1)}, bf16[12,4,1152]{2,1,0:T(4,128)(2,1)S(1)}, u32[]{:S(2)}, u32[]{:S(2)}) collective-permute-start(bf16[12,4,1152]{2,1,0:T(4,128)(2,1)S(1)} %get-tuple-element.22), channel_id=1, source_target_pairs={{0,6},{2,4},{4,2},{6,0},{8,14},{10,12},{12,10},{14,8},{16,22},{18,... | collective-permute-start | bytes 331784 | tf_op jit(solution)/shard_map/ppermute | solution.py:293

commit v4 on v3

--- a/solution.py
+++ b/solution.py
@@ -16,6 +16,8 @@
 VMEM_LIMIT = 24 * 2**20
 TLAST = 5 * 10**8
 PLACE = 7 * 10**9
+PICK_LIMIT = 8 * 2**20
+SPLITS = 2
 SHUFFLE_LIMIT = 8 * 2**20
 SMALL, LARGE = 5 * 10**8, 2 * 10**10
 
@@ -148,14 +150,19 @@
 
 def temporal_kernel(head_dim, tokens, outer, *refs):
     me_ref, in_ref, weight_ref, query_gain, key_gain = refs[:5]
-    arranged, query, keys, values, bias, total, held, arrived = refs[-8:]
-    out_refs = refs[5:-8]
+    arranged, query, keys, values, bias, held, arrived = refs[-7:]
+    out_refs = refs[5:-7]
     pieces, sub, width = in_ref.shape
-    cuts = [0, max(width // 4 // 256, 1) * 256, max(width // 2 // 256, 1) * 256, width]
+    columns = [slice(i * width, (i + 1) * width) for i in range(3)]
+    depth = width // SPLITS
     copies = [
-        pltpu.make_async_copy(weight_ref.at[low:high], held.at[low:high], arrived.at[i])
-        for i, (low, high) in enumerate(zip(cuts[:-1], cuts[1:]))
-        if low < high
+        pltpu.make_async_copy(
+            weight_ref.at[j * depth : (j + 1) * depth, c],
+            held.at[j * depth : (j + 1) * depth, c],
+            arrived.at[i, j],
+        )
+        for i, c in enumerate(columns)
+        for j in range(SPLITS)
     ]
     for copy in copies:
         copy.start()
@@ -165,16 +172,10 @@
     for i in range(pieces):
         arranged[i * sub : (i + 1) * sub, :] = in_ref[i].astype(F32)
     incoming = arranged[...].astype(BF16)
-    half = cuts[2]
-    columns = [slice(i * width, (i + 1) * width) for i in range(3)]
-    for copy in copies[:-1]:
-        copy.wait()
-    for c in columns:
-        total[:, c] = jnp.dot(incoming[:, :half], held[:half, c], preferred_element_type=F32)
-    copies[-1].wait()
-    for place, gain, c in ((query, query_gain, columns[0]), (keys, key_gain, columns[1]), (values, None, columns[2])):
-        rest = jnp.dot(incoming[:, half:], held[half:, c], preferred_element_type=F32)
-        projected = (total[:, c] + rest).astype(BF16)
+    for i, (place, gain) in enumerate(((query, query_gain), (keys, key_gain), (values, None))):
+        for copy in copies[i * SPLITS : (i + 1) * SPLITS]:
+            copy.wait()
+        projected = jnp.dot(incoming, held[:, columns[i]], preferred_element_type=F32).astype(BF16)
         if gain is not None:
             projected = head_norm(projected, gain, gather, spread, head_dim)
         place[...] = projected
@@ -219,9 +220,8 @@
         + [pltpu.VMEM((rows, width), BF16)] * 3
         + [
             pltpu.VMEM((rows, rows), F32),
-            pltpu.VMEM((rows, 3 * width), F32),
             pltpu.VMEM((width, 3 * width), BF16),
-            pltpu.SemaphoreType.DMA((3,)),
+            pltpu.SemaphoreType.DMA((3, SPLITS)),
         ],
         compiler_params=pltpu.CompilerParams(vmem_limit_bytes=TEMPORAL_LIMIT),
         cost_estimate=pl.CostEstimate(flops=cost, bytes_accessed=2**20, transcendentals=0),
@@ -295,6 +295,25 @@
         place_kernel, "place", PLACE, outer, inner, me, held, [(count * share, sub, width)]
     )
     return placed
+
+
+def pick_kernel(video, which, in_ref, out_ref, done):
+    copy = pltpu.make_async_copy(in_ref.at[video, which], out_ref, done)
+    copy.start()
+    copy.wait()
+
+
+def pick(qkv, video, which):
+    return pl.pallas_call(
+        functools.partial(pick_kernel, video, which),
+        out_shape=jax.ShapeDtypeStruct(qkv.shape[2:], BF16),
+        in_specs=[pl.BlockSpec(memory_space=pltpu.HBM)],
+        out_specs=pl.BlockSpec(memory_space=pltpu.VMEM),
+        scratch_shapes=[pltpu.SemaphoreType.DMA],
+        compiler_params=pltpu.CompilerParams(vmem_limit_bytes=PICK_LIMIT),
+        cost_estimate=pl.CostEstimate(flops=1000, bytes_accessed=2**20, transcendentals=0),
+        name=f"pick_{video}_{which}",
+    )(qkv)
 
 
 def exchange(blocks, frame_count):
@@ -333,7 +352,7 @@
     remotes = {}
     for video in reversed(range(videos)):
         for which in (2, 1):
-            own = qkv[video, which]
+            own = pick(qkv, video, which)
             remotes[video, which] = [lax.ppermute(own, "pos", step) for step in steps]
     spatial_gains = [g.reshape(1, head_dim) for g in (spatial_qgain, spatial_kgain)]
     temporal_gains = [g.reshape(1, head_dim) for g in (temporal_qgain, temporal_kgain)]

time: 95.3 us -> 94.2 us (0.988)
  waiting for transfers between devices: 30.8 us -> 28.5 us
  Pallas kernels: 30.1 us -> 32 us
    squeeze x1 -> x0, local copies, waits for them, and re-layouts: 2.6 us -> none  [per_device(): own = qkv[video, which]]
    pallas_call x0 -> x4, Pallas kernels: none -> 2.54 us  [pick(): pl.pallas_call(functools.partial(pick_kernel, video, which), out_shape=ja...]
    ppermute x4, waiting for transfers between devices: 18.9 us -> 16.4 us  [per_device(): remotes[video, which] = [lax.ppermute(own, 'pos', step) for step in steps]]
    unnamed x30 -> x32, local copies, waits for them, and re-layouts: 0.88 us -> 2.64 us
  transfers between devices with their start and end apart: 13 -> 13, of which waited for: 8 -> 8; matrix products, arithmetic and copies ran while one was open for 0% -> 0% of each run, Pallas kernels for 32% -> 34%
where the time goes in v4:
time: 94.2 us; the launch traced here: 93.7 us
  Pallas kernels  32 us (34%)
  starting transfers between devices  29 us (31%)
  waiting for transfers between devices  28.5 us (30%)
  local copies, waits for them, and re-layouts  2.84 us (3%)
  other arithmetic  1 us (1%)
    all_to_all x3, starting transfers between devices, exchange(): lax.all_to_all(split, 'frame', split_axis=0, concat_axis=0, tiled=True)  17.1 us
    ppermute x4, waiting for transfers between devices, per_device(): remotes[video, which] = [lax.ppermute(own, 'pos', step) for step in steps]  16.4 us
    pallas_call x2, Pallas kernels, temporal(): pl.pallas_call(functools.partial(temporal_kernel, head_dim, tokens, outer...  15.3 us
    ppermute x3, waiting for transfers between devices, way_back(): held.append(lax.ppermute(grouped[t], 'frame', pairs))  8.92 us
    pallas_call x2, Pallas kernels, score_weights(): pl.pallas_call(functools.partial(score_kernel, head_dim, video, len(remot...  7.3 us
    pallas_call x2, Pallas kernels, attend(): pl.pallas_call(functools.partial(attend_kernel, head_dim, video, len(remo...  6.78 us
    ppermute x4, starting transfers between devices, per_device(): remotes[video, which] = [lax.ppermute(own, 'pos', step) for step in steps]  5.25 us
    ppermute x3, starting transfers between devices, way_back(): held.append(lax.ppermute(blocks[s], 'frame', pairs))  4.48 us
  transfers between devices with their start and end apart: 13, of which 8 were waited for; matrix products, arithmetic and copies ran while one was open for 0% of the time, Pallas kernels for 34%

profile of v4, /device:TPU:0, one launch (start us, length us, event | category | flops | bytes accessed | tf_op | source)
XLA Modules:
  0.0 93.7 jit_solution(15208084078566026448)
XLA Ops:
  0.0 1.7 %copy-done = bf16[2,1,192,3,1152]{4,2,3,1,0:T(8,128)(2,1)S(1)} copy-done((bf16[2,1,192,3,1152]{4,2,3,1,0:T(8,128)(2,1)S(1)}, bf16[2,1,192,3,1152]{4,2,3,1,0:T(8,128)(2,1)}, u32[]{:S(2)}) %copy-start) | copy-done | bytes 2654232
  1.8 0.3 pick_0_1.1
  2.0 3.0 %collective-permute-start = (bf16[192,1152]{1,0:T(8,128)(2,1)S(1)}, bf16[192,1152]{1,0:T(8,128)(2,1)S(1)}, u32[]{:S(2)}, u32[]{:S(2)}) collective-permute-start(bf16[192,1152]{1,0:T(8,128)(2,1)S(1)} %pick_0_1.1), channel_id=1, source_target_pairs={{0,1},{1,0},{2,3},{3,2},{4,5},{5,4},{6,7},{7,6},{8,9},{9,8},{10,11... | collective-permute-start | bytes 1327112 | tf_op jit(solution)/shard_map/ppermute | solution.py:356
  5.0 0.3 pick_0_2.1
  5.4 1.0 %pick_1_1.1 = bf16[192,1152]{1,0:T(8,128)(2,1)} custom-call(bf16[2,3,192,1152]{3,2,1,0:T(8,128)(2,1)S(1)} %bitcast.18), custom_call_target="tpu_custom_call" | custom-call | flops 1000 | bytes 1048576 | tf_op jit(solution)/shard_map/pick_1_1/pallas_call | solution.py:307
  6.4 2.1 %collective-permute-start.8 = (bf16[192,1152]{1,0:T(8,128)(2,1)}, bf16[192,1152]{1,0:T(8,128)(2,1)S(1)}, u32[]{:S(2)}, u32[]{:S(2)}) collective-permute-start(bf16[192,1152]{1,0:T(8,128)(2,1)} %pick_1_1.1), channel_id=1, source_target_pairs={{0,1},{1,0},{2,3},{3,2},{4,5},{5,4},{6,7},{7,6},{8,9},{9,8},{10,11... | collective-permute-start | bytes 1327112 | tf_op jit(solution)/shard_map/ppermute | solution.py:356
  8.5 1.0 %pick_1_2.1 = bf16[192,1152]{1,0:T(8,128)(2,1)} custom-call(bf16[2,3,192,1152]{3,2,1,0:T(8,128)(2,1)S(1)} %bitcast.19), custom_call_target="tpu_custom_call" | custom-call | flops 1000 | bytes 1048576 | tf_op jit(solution)/shard_map/pick_1_2/pallas_call | solution.py:307
  9.6 6.4 %collective-permute-done.refs_1_ = bf16[192,1152]{1,0:T(8,128)(2,1)S(1)} collective-permute-done((bf16[192,1152]{1,0:T(8,128)(2,1)S(1)}, bf16[192,1152]{1,0:T(8,128)(2,1)S(1)}, u32[]{:S(2)}, u32[]{:S(2)}) %collective-permute-start) | collective-permute-done | bytes 442400 | tf_op jit(solution)/shard_map/ppermute | solution.py:356
  16.1 3.6 %scores_0.1.refs_0_ = bf16[16,192,384]{2,1,0:T(8,128)(2,1)S(1)} custom-call(bf16[2,3,192,1152]{3,2,1,0:T(8,128)(2,1)S(1)} %bitcast.20, bf16[192,1152]{1,0:T(8,128)(2,1)S(1)} %collective-permute-done.refs_1_, f32[1,72]{1,0:T(1,128)S(1)} %bitcast.28, f32[1,72]{1,0:T(1,128)S(1)} %bitcast.30), custom_call_target="tpu_custom_call" | custom-call | flops 500000000 | bytes 1048576 | tf_op jit(solution)/shard_map/scores_0/pallas_call | solution.py:99
  19.7 5.8 %collective-permute-done.1.refs_2_ = bf16[192,1152]{1,0:T(8,128)(2,1)S(1)} collective-permute-done((bf16[192,1152]{1,0:T(8,128)(2,1)S(1)}, bf16[192,1152]{1,0:T(8,128)(2,1)S(1)}, u32[]{:S(2)}, u32[]{:S(2)}) %collective-permute-start.1) | collective-permute-done | bytes 442400 | tf_op jit(solution)/shard_map/ppermute | solution.py:356
  25.5 2.9 %attend_0.1 = bf16[48,4,1152]{2,1,0:T(4,128)(2,1)} custom-call(bf16[16,192,384]{2,1,0:T(8,128)(2,1)S(1)} %scores_0.1.refs_0_, bf16[2,3,192,1152]{3,2,1,0:T(8,128)(2,1)S(1)} %bitcast.21, bf16[192,1152]{1,0:T(8,128)(2,1)S(1)} %collective-permute-done.1.refs_2_, bf16[2,192,1152]{2,1,0:T(8,128)(2,1)S(1)} %bitcast.26, bf16[1152,1152]{1,0:T(8,128)(2,1)S(1)} %copy-done.2, ...), custom_call_target="tpu_custom_call" | custom-call | flops 500000000 | bytes 1048576 | tf_op jit(solution)/shard_map/attend_0/pallas_call | solution.py:139
  28.5 6.5 %all-to-all-start = ((bf16[16,3,4,1152]{3,2,1,0:T(4,128)(2,1)}), bf16[16,3,4,1152]{3,2,1,0:T(4,128)(2,1)S(1)}, u32[]{:S(2)}, u32[]{:S(2)}) async-start(bf16[16,3,4,1152]{3,2,1,0:T(4,128)(2,1)} %bitcast.7), calls=%async_computation | async-start | bytes 884736 | tf_op jit(solution)/shard_map/all_to_all | solution.py:322
  35.0 0.8 copy-done.13
  35.8 3.6 %scores_1.1.refs_0_ = bf16[16,192,384]{2,1,0:T(8,128)(2,1)S(1)} custom-call(bf16[2,3,192,1152]{3,2,1,0:T(8,128)(2,1)S(1)} %bitcast.22, bf16[192,1152]{1,0:T(8,128)(2,1)S(1)} %collective-permute-done.8.refs_1_, f32[1,72]{1,0:T(1,128)S(1)} %bitcast.29, f32[1,72]{1,0:T(1,128)S(1)} %bitcast.31), custom_call_target="tpu_custom_call" | custom-call | flops 500000000 | bytes 1048576 | tf_op jit(solution)/shard_map/scores_1/pallas_call | solution.py:99
  39.5 4.2 %collective-permute-done.9.refs_2_ = bf16[192,1152]{1,0:T(8,128)(2,1)} collective-permute-done((bf16[192,1152]{1,0:T(8,128)(2,1)}, bf16[192,1152]{1,0:T(8,128)(2,1)}, u32[]{:S(2)}, u32[]{:S(2)}) %collective-permute-start.9) | collective-permute-done | bytes 442400 | tf_op jit(solution)/shard_map/ppermute | solution.py:356
  43.8 3.8 %attend_1.1 = bf16[48,4,1152]{2,1,0:T(4,128)(2,1)} custom-call(bf16[16,192,384]{2,1,0:T(8,128)(2,1)S(1)} %scores_1.1.refs_0_, bf16[2,3,192,1152]{3,2,1,0:T(8,128)(2,1)S(1)} %bitcast.23, bf16[192,1152]{1,0:T(8,128)(2,1)} %collective-permute-done.9.refs_2_, bf16[2,192,1152]{2,1,0:T(8,128)(2,1)S(1)} %bitcast.27, bf16[1152,1152]{1,0:T(8,128)(2,1)S(1)} %copy-done.3, ...), custom_call_target="tpu_custom_call" | custom-call | flops 20000000000 | bytes 1048576 | tf_op jit(solution)/shard_map/attend_1/pallas_call | solution.py:139
  47.6 0.4 all-to-all-done
  48.0 5.8 %all-to-all-start.1 = ((bf16[16,3,4,1152]{3,2,1,0:T(4,128)(2,1)}), bf16[16,3,4,1152]{3,2,1,0:T(4,128)(2,1)S(1)}, u32[]{:S(2)}, u32[]{:S(2)}) async-start(bf16[16,3,4,1152]{3,2,1,0:T(4,128)(2,1)} %bitcast.11), calls=%async_computation.1 | async-start | bytes 884736 | tf_op jit(solution)/shard_map/all_to_all | solution.py:322
  53.8 7.3 %temporal_0.1 = (bf16[12,4,1152]{2,1,0:T(4,128)(2,1)S(1)}, bf16[12,4,1152]{2,1,0:T(4,128)(2,1)S(1)}, bf16[12,4,1152]{2,1,0:T(4,128)(2,1)S(1)}, bf16[12,4,1152]{2,1,0:T(4,128)(2,1)S(1)}) custom-call(s32[1]{0:T(128)} %bitcast.refs_0_.me_ref, bf16[48,4,1152]{2,1,0:T(4,128)(2,1)S(1)} %bitcast.24, bf16[1152,3456]{1,0:T(8,128)(2,1)} %refs_2_.3, ...), custom_call_target="tpu_custom_call" | custom-call | flops 500000000 | bytes 1048576 | tf_op jit(solution)/shard_map/temporal_0/pallas_call | solution.py:211
  61.1 2.0 %collective-permute-start.2 = (bf16[12,4,1152]{2,1,0:T(4,128)(2,1)S(1)}, bf16[12,4,1152]{2,1,0:T(4,128)(2,1)S(1)}, u32[]{:S(2)}, u32[]{:S(2)}) collective-permute-start(bf16[12,4,1152]{2,1,0:T(4,128)(2,1)S(1)} %get-tuple-element.16), channel_id=1, source_target_pairs={{0,8},{2,10},{4,12},{6,14},{8,0},{10,2},{12,4},{14,6},{16,24},{18,... | collective-permute-start | bytes 331784 | tf_op jit(solution)/shard_map/ppermute | solution.py:284
  63.1 2.4 %collective-permute-start.3 = (bf16[12,4,1152]{2,1,0:T(4,128)(2,1)S(1)}, bf16[12,4,1152]{2,1,0:T(4,128)(2,1)S(1)}, u32[]{:S(2)}, u32[]{:S(2)}) collective-permute-start(bf16[12,4,1152]{2,1,0:T(4,128)(2,1)S(1)} %get-tuple-element.17), channel_id=1, source_target_pairs={{0,16},{2,18},{4,20},{6,22},{8,24},{10,26},{12,28},{14,30},{16,0},... | collective-permute-start | bytes 331784 | tf_op jit(solution)/shard_map/ppermute | solution.py:284
  65.4 0.2 collective-permute-start.4
  65.6 1.2 %all-to-all-done.1 = bf16[16,3,4,1152]{3,2,1,0:T(4,128)(2,1)S(1)} async-done(((bf16[16,3,4,1152]{3,2,1,0:T(4,128)(2,1)}), bf16[16,3,4,1152]{3,2,1,0:T(4,128)(2,1)S(1)}, u32[]{:S(2)}, u32[]{:S(2)}) %all-to-all-start.1) | async-done | bytes 442400 | tf_op jit(solution)/shard_map/all_to_all | solution.py:322
  66.8 8.0 %temporal_1.1 = bf16[48,4,1152]{2,1,0:T(4,128)(2,1)} custom-call(s32[1]{0:T(128)} %bitcast.refs_0_.me_ref, bf16[48,4,1152]{2,1,0:T(4,128)(2,1)S(1)} %bitcast.25, bf16[1152,3456]{1,0:T(8,128)(2,1)} %refs_2_.3, f32[1,72]{1,0:T(1,128)S(1)} %bitcast.33, f32[1,72]{1,0:T(1,128)S(1)} %bitcast.35), custom_call_target="tpu_custom_call" | custom-call | flops 500000000 | bytes 1048576 | tf_op jit(solution)/shard_map/temporal_1/pallas_call | solution.py:211
  74.9 4.8 %all-to-all-start.2 = ((bf16[16,3,4,1152]{3,2,1,0:T(4,128)(2,1)}), bf16[16,3,4,1152]{3,2,1,0:T(4,128)(2,1)S(1)}, u32[]{:S(2)}, u32[]{:S(2)}) async-start(bf16[16,3,4,1152]{3,2,1,0:T(4,128)(2,1)} %bitcast.13), calls=%async_computation.2 | async-start | bytes 884736 | tf_op jit(solution)/shard_map/all_to_all | solution.py:322
  79.7 0.5 collective-permute-start.5
  80.2 1.7 %collective-permute-start.6 = (bf16[12,4,1152]{2,1,0:T(4,128)(2,1)S(1)}, bf16[12,4,1152]{2,1,0:T(4,128)(2,1)S(1)}, u32[]{:S(2)}, u32[]{:S(2)}) collective-permute-start(bf16[12,4,1152]{2,1,0:T(4,128)(2,1)S(1)} %get-tuple-element.21), channel_id=1, source_target_pairs={{0,4},{2,6},{4,0},{6,2},{8,12},{10,14},{12,8},{14,10},{16,20},{18,... | collective-permute-start | bytes 331784 | tf_op jit(solution)/shard_map/ppermute | solution.py:293
  81.9 7.1 %collective-permute-done.6.refs_2_ = bf16[12,4,1152]{2,1,0:T(4,128)(2,1)S(1)} collective-permute-done((bf16[12,4,1152]{2,1,0:T(4,128)(2,1)S(1)}, bf16[12,4,1152]{2,1,0:T(4,128)(2,1)S(1)}, u32[]{:S(2)}, u32[]{:S(2)}) %collective-permute-start.6) | collective-permute-done | bytes 110624 | tf_op jit(solution)/shard_map/ppermute | solution.py:293
  89.0 1.8 %collective-permute-done.7.refs_3_ = bf16[12,4,1152]{2,1,0:T(4,128)(2,1)S(1)} collective-permute-done((bf16[12,4,1152]{2,1,0:T(4,128)(2,1)S(1)}, bf16[12,4,1152]{2,1,0:T(4,128)(2,1)S(1)}, u32[]{:S(2)}, u32[]{:S(2)}) %collective-permute-start.7) | collective-permute-done | bytes 110624 | tf_op jit(solution)/shard_map/ppermute | solution.py:293
  90.8 0.1 stack_reshape.3
  91.0 1.7 %all-to-all-done.2 = bf16[16,3,4,1152]{3,2,1,0:T(4,128)(2,1)S(1)} async-done(((bf16[16,3,4,1152]{3,2,1,0:T(4,128)(2,1)}), bf16[16,3,4,1152]{3,2,1,0:T(4,128)(2,1)S(1)}, u32[]{:S(2)}, u32[]{:S(2)}) %all-to-all-start.2) | async-done | bytes 442400 | tf_op jit(solution)/shard_map/all_to_all | solution.py:322
  92.7 1.0 %maximum_bitcast_fusion = bf16[2,1,192,1152]{3,2,1,0:T(8,128)(2,1)} fusion(bf16[1,192,1152]{2,1,0:T(8,128)(2,1)S(1)} %stack_reshape_reshape.3, bf16[1,192,1152]{2,1,0:T(8,128)(2,1)S(1)} %stack_reshape.3), kind=kLoop, calls=%fused_computation | loop fusion | flops 442368 | bytes 1769472 | tf_op jit(solution)/shard_map/reshape | solution.py:381
  (41 shorter events, 0.5 us)
Async XLA Ops:
  0.0 1.7 %copy-start = (bf16[2,1,192,3,1152]{4,2,3,1,0:T(8,128)(2,1)S(1)}, bf16[2,1,192,3,1152]{4,2,3,1,0:T(8,128)(2,1)}, u32[]{:S(2)}) copy-start(bf16[2,1,192,3,1152]{4,2,3,1,0:T(8,128)(2,1)} %param.11) | copy-start | bytes 7962628
  2.0 14.0 %collective-permute-start = (bf16[192,1152]{1,0:T(8,128)(2,1)S(1)}, bf16[192,1152]{1,0:T(8,128)(2,1)S(1)}, u32[]{:S(2)}, u32[]{:S(2)}) collective-permute-start(bf16[192,1152]{1,0:T(8,128)(2,1)S(1)} %pick_0_1.1), channel_id=1, source_target_pairs={{0,1},{1,0},{2,3},{3,2},{4,5},{5,4},{6,7},{7,6},{8,9},{9,8},{10,11... | collective-permute-start | bytes 1327112 | tf_op jit(solution)/shard_map/ppermute | solution.py:356
  5.3 10.7 %copy-start.1 = (bf16[2,1,192,3,1152]{4,2,3,1,0:T(8,128)(2,1)S(1)}, bf16[2,1,192,3,1152]{4,2,3,1,0:T(8,128)(2,1)}, u32[]{:S(2)}) copy-start(bf16[2,1,192,3,1152]{4,2,3,1,0:T(8,128)(2,1)} %param.11) | copy-start | bytes 7962628
  5.3 10.7 %copy-start.11 = (f32[72]{0:T(128)S(1)}, f32[72]{0:T(128)}, u32[]{:S(2)}) copy-start(f32[72]{0:T(128)} %param.15) | copy-start | bytes 868
  5.3 10.7 %copy-start.12 = (f32[72]{0:T(128)S(1)}, f32[72]{0:T(128)}, u32[]{:S(2)}) copy-start(f32[72]{0:T(128)} %param.16) | copy-start | bytes 868
  5.3 20.2 %collective-permute-start.1 = (bf16[192,1152]{1,0:T(8,128)(2,1)S(1)}, bf16[192,1152]{1,0:T(8,128)(2,1)S(1)}, u32[]{:S(2)}, u32[]{:S(2)}) collective-permute-start(bf16[192,1152]{1,0:T(8,128)(2,1)S(1)} %pick_0_2.1), channel_id=1, source_target_pairs={{0,1},{1,0},{2,3},{3,2},{4,5},{5,4},{6,7},{7,6},{8,9},{9,8},{10,11... | collective-permute-start | bytes 1327112 | tf_op jit(solution)/shard_map/ppermute | solution.py:356
  6.4 28.6 %collective-permute-start.8 = (bf16[192,1152]{1,0:T(8,128)(2,1)}, bf16[192,1152]{1,0:T(8,128)(2,1)S(1)}, u32[]{:S(2)}, u32[]{:S(2)}) collective-permute-start(bf16[192,1152]{1,0:T(8,128)(2,1)} %pick_1_1.1), channel_id=1, source_target_pairs={{0,1},{1,0},{2,3},{3,2},{4,5},{5,4},{6,7},{7,6},{8,9},{9,8},{10,11... | collective-permute-start | bytes 1327112 | tf_op jit(solution)/shard_map/ppermute | solution.py:356
  9.5 34.2 %collective-permute-start.9 = (bf16[192,1152]{1,0:T(8,128)(2,1)}, bf16[192,1152]{1,0:T(8,128)(2,1)}, u32[]{:S(2)}, u32[]{:S(2)}) collective-permute-start(bf16[192,1152]{1,0:T(8,128)(2,1)} %pick_1_2.1), channel_id=1, source_target_pairs={{0,1},{1,0},{2,3},{3,2},{4,5},{5,4},{6,7},{7,6},{8,9},{9,8},{10,11... | collective-permute-start | bytes 1327112 | tf_op jit(solution)/shard_map/ppermute | solution.py:356
  16.0 9.5 %copy-start.2 = (bf16[1152,1152]{1,0:T(8,128)(2,1)S(1)}, bf16[1152,1152]{1,0:T(8,128)(2,1)}, u32[]{:S(2)}) copy-start(bf16[1152,1152]{1,0:T(8,128)(2,1)} %refs_4_.3) | copy-start | bytes 7962628
  16.0 9.5 %copy-start.4 = (bf16[2,1,192,1152]{3,2,1,0:T(8,128)(2,1)S(1)}, bf16[2,1,192,1152]{3,2,1,0:T(8,128)(2,1)}, u32[]{:S(2)}) copy-start(bf16[2,1,192,1152]{3,2,1,0:T(8,128)(2,1)} %param.12) | copy-start | bytes 2654212
  16.0 9.5 %copy-start.6 = (f32[2,1152]{1,0:T(2,128)S(1)}, f32[2,1152]{1,0:T(2,128)}, u32[]{:S(2)}) copy-start(f32[2,1152]{1,0:T(2,128)} %refs_5_.3) | copy-start | bytes 27652
  16.1 9.4 %copy-start.7 = (f32[2,1152]{1,0:T(2,128)S(1)}, f32[2,1152]{1,0:T(2,128)}, u32[]{:S(2)}) copy-start(f32[2,1152]{1,0:T(2,128)} %refs_6_.3) | copy-start | bytes 27652
  16.1 9.4 %copy-start.9 = (f32[2,1152]{1,0:T(2,128)S(1)}, f32[2,1152]{1,0:T(2,128)}, u32[]{:S(2)}) copy-start(f32[2,1152]{1,0:T(2,128)} %refs_7_.3) | copy-start | bytes 27652
  28.5 19.5 %all-to-all-start = ((bf16[16,3,4,1152]{3,2,1,0:T(4,128)(2,1)}), bf16[16,3,4,1152]{3,2,1,0:T(4,128)(2,1)S(1)}, u32[]{:S(2)}, u32[]{:S(2)}) async-start(bf16[16,3,4,1152]{3,2,1,0:T(4,128)(2,1)} %bitcast.7), calls=%async_computation | async-start | bytes 884736 | tf_op jit(solution)/shard_map/all_to_all | solution.py:322
  35.0 8.8 %copy-start.3 = (bf16[1152,1152]{1,0:T(8,128)(2,1)S(1)}, bf16[1152,1152]{1,0:T(8,128)(2,1)}, u32[]{:S(2)}) copy-start(bf16[1152,1152]{1,0:T(8,128)(2,1)} %refs_4_.3) | copy-start | bytes 7962628
  35.0 8.8 %copy-start.5 = (bf16[2,1,192,1152]{3,2,1,0:T(8,128)(2,1)S(1)}, bf16[2,1,192,1152]{3,2,1,0:T(8,128)(2,1)}, u32[]{:S(2)}) copy-start(bf16[2,1,192,1152]{3,2,1,0:T(8,128)(2,1)} %param.12) | copy-start | bytes 2654212
  35.0 8.7 %copy-start.8 = (f32[2,1152]{1,0:T(2,128)S(1)}, f32[2,1152]{1,0:T(2,128)}, u32[]{:S(2)}) copy-start(f32[2,1152]{1,0:T(2,128)} %refs_6_.3) | copy-start | bytes 27652
  35.0 8.7 %copy-start.10 = (f32[2,1152]{1,0:T(2,128)S(1)}, f32[2,1152]{1,0:T(2,128)}, u32[]{:S(2)}) copy-start(f32[2,1152]{1,0:T(2,128)} %refs_7_.3) | copy-start | bytes 27652
  35.0 0.8 copy-start.13
  39.5 14.3 %copy-start.14 = (f32[72]{0:T(128)S(1)}, f32[72]{0:T(128)}, u32[]{:S(2)}) copy-start(f32[72]{0:T(128)} %param.20) | copy-start | bytes 868
  39.5 14.3 %copy-start.15 = (f32[72]{0:T(128)S(1)}, f32[72]{0:T(128)}, u32[]{:S(2)}) copy-start(f32[72]{0:T(128)} %param.21) | copy-start | bytes 868
  48.0 18.9 %all-to-all-start.1 = ((bf16[16,3,4,1152]{3,2,1,0:T(4,128)(2,1)}), bf16[16,3,4,1152]{3,2,1,0:T(4,128)(2,1)S(1)}, u32[]{:S(2)}, u32[]{:S(2)}) async-start(bf16[16,3,4,1152]{3,2,1,0:T(4,128)(2,1)} %bitcast.11), calls=%async_computation.1 | async-start | bytes 884736 | tf_op jit(solution)/shard_map/all_to_all | solution.py:322
  61.1 18.5 %collective-permute-start.2 = (bf16[12,4,1152]{2,1,0:T(4,128)(2,1)S(1)}, bf16[12,4,1152]{2,1,0:T(4,128)(2,1)S(1)}, u32[]{:S(2)}, u32[]{:S(2)}) collective-permute-start(bf16[12,4,1152]{2,1,0:T(4,128)(2,1)S(1)} %get-tuple-element.16), channel_id=1, source_target_pairs={{0,8},{2,10},{4,12},{6,14},{8,0},{10,2},{12,4},{14,6},{16,24},{18,... | collective-permute-start | bytes 331784 | tf_op jit(solution)/shard_map/ppermute | solution.py:284
  63.1 16.6 %collective-permute-start.3 = (bf16[12,4,1152]{2,1,0:T(4,128)(2,1)S(1)}, bf16[12,4,1152]{2,1,0:T(4,128)(2,1)S(1)}, u32[]{:S(2)}, u32[]{:S(2)}) collective-permute-start(bf16[12,4,1152]{2,1,0:T(4,128)(2,1)S(1)} %get-tuple-element.17), channel_id=1, source_target_pairs={{0,16},{2,18},{4,20},{6,22},{8,24},{10,26},{12,28},{14,30},{16,0},... | collective-permute-start | bytes 331784 | tf_op jit(solution)/shard_map/ppermute | solution.py:284
  65.4 14.2 %collective-permute-start.4 = (bf16[12,4,1152]{2,1,0:T(4,128)(2,1)S(1)}, bf16[12,4,1152]{2,1,0:T(4,128)(2,1)S(1)}, u32[]{:S(2)}, u32[]{:S(2)}) collective-permute-start(bf16[12,4,1152]{2,1,0:T(4,128)(2,1)S(1)} %get-tuple-element.18), channel_id=1, source_target_pairs={{0,24},{2,26},{4,28},{6,30},{8,16},{10,18},{12,20},{14,22},{16,8},... | collective-permute-start | bytes 331784 | tf_op jit(solution)/shard_map/ppermute | solution.py:284
  74.9 17.8 %all-to-all-start.2 = ((bf16[16,3,4,1152]{3,2,1,0:T(4,128)(2,1)}), bf16[16,3,4,1152]{3,2,1,0:T(4,128)(2,1)S(1)}, u32[]{:S(2)}, u32[]{:S(2)}) async-start(bf16[16,3,4,1152]{3,2,1,0:T(4,128)(2,1)} %bitcast.13), calls=%async_computation.2 | async-start | bytes 884736 | tf_op jit(solution)/shard_map/all_to_all | solution.py:322
  79.7 2.2 %collective-permute-start.5 = (bf16[12,4,1152]{2,1,0:T(4,128)(2,1)S(1)}, bf16[12,4,1152]{2,1,0:T(4,128)(2,1)S(1)}, u32[]{:S(2)}, u32[]{:S(2)}) collective-permute-start(bf16[12,4,1152]{2,1,0:T(4,128)(2,1)S(1)} %get-tuple-element.20), channel_id=1, source_target_pairs={{0,2},{2,0},{4,6},{6,4},{8,10},{10,8},{12,14},{14,12},{16,18},{18,... | collective-permute-start | bytes 331784 | tf_op jit(solution)/shard_map/ppermute | solution.py:293
  80.2 8.8 %collective-permute-start.6 = (bf16[12,4,1152]{2,1,0:T(4,128)(2,1)S(1)}, bf16[12,4,1152]{2,1,0:T(4,128)(2,1)S(1)}, u32[]{:S(2)}, u32[]{:S(2)}) collective-permute-start(bf16[12,4,1152]{2,1,0:T(4,128)(2,1)S(1)} %get-tuple-element.21), channel_id=1, source_target_pairs={{0,4},{2,6},{4,0},{6,2},{8,12},{10,14},{12,8},{14,10},{16,20},{18,... | collective-permute-start | bytes 331784 | tf_op jit(solution)/shard_map/ppermute | solution.py:293
  81.9 8.9 %collective-permute-start.7 = (bf16[12,4,1152]{2,1,0:T(4,128)(2,1)S(1)}, bf16[12,4,1152]{2,1,0:T(4,128)(2,1)S(1)}, u32[]{:S(2)}, u32[]{:S(2)}) collective-permute-start(bf16[12,4,1152]{2,1,0:T(4,128)(2,1)S(1)} %get-tuple-element.22), channel_id=1, source_target_pairs={{0,6},{2,4},{4,2},{6,0},{8,14},{10,12},{12,10},{14,8},{16,22},{18,... | collective-permute-start | bytes 331784 | tf_op jit(solution)/shard_map/ppermute | solution.py:293

commit v5 on v4

--- a/solution.py
+++ b/solution.py
@@ -27,8 +27,8 @@
     head = lax.broadcasted_iota(jnp.int32, (width, LANES), 1)
     inside = feature - head * head_dim
     gather = jnp.where((inside >= 0) & (inside < head_dim), 1.0, 0.0).astype(BF16)
-    feature = lax.broadcasted_iota(jnp.int32, (LANES, width), 1)
-    head = lax.broadcasted_iota(jnp.int32, (LANES, width), 0)
+    feature = lax.broadcasted_iota(jnp.int32, (2 * LANES, width), 1)
+    head = lax.rem(lax.broadcasted_iota(jnp.int32, (2 * LANES, width), 0), LANES)
     inside = feature - head * head_dim
     spread = jnp.where((inside >= 0) & (inside < head_dim), 1.0, 0.0).astype(BF16)
     return gather, spread
@@ -47,7 +47,9 @@
     widened = values.astype(F32)
     squares = split_dot(widened * widened, gather)
     factor = lax.rsqrt(squares * (1.0 / head_dim) + EPSILON)
-    return (widened * split_dot(factor, spread) * gain_row).astype(BF16)
+    high = factor.astype(BF16)
+    pieces = jnp.concatenate([high, (factor - high.astype(F32)).astype(BF16)], axis=1)
+    return (widened * jnp.dot(pieces, spread, preferred_element_type=F32) * gain_row).astype(BF16)
 
 
 def head_window(head, head_dim, width):

time: 94.2 us -> 93.6 us (level)
  transfers between devices with their start and end apart: 13 -> 13, of which waited for: 8 -> 8; matrix products, arithmetic and copies ran while one was open for 0% -> 0% of each run, Pallas kernels for 34% -> 33%
where the time goes in v5:
time: 93.6 us; the launch traced here: 93.1 us
  Pallas kernels  31.3 us (33%)
  waiting for transfers between devices  29 us (31%)
  starting transfers between devices  28.7 us (31%)
  local copies, waits for them, and re-layouts  2.84 us (3%)
  other arithmetic  1 us (1%)
    all_to_all x3, starting transfers between devices, exchange(): lax.all_to_all(split, 'frame', split_axis=0, concat_axis=0, tiled=True)  16.8 us
    ppermute x4, waiting for transfers between devices, per_device(): remotes[video, which] = [lax.ppermute(own, 'pos', step) for step in steps]  16.5 us
    pallas_call x2, Pallas kernels, temporal(): pl.pallas_call(functools.partial(temporal_kernel, head_dim, tokens, outer...  14.7 us
    ppermute x3, waiting for transfers between devices, way_back(): held.append(lax.ppermute(grouped[t], 'frame', pairs))  8.92 us
    pallas_call x2, Pallas kernels, score_weights(): pl.pallas_call(functools.partial(score_kernel, head_dim, video, len(remot...  7.16 us
    pallas_call x2, Pallas kernels, attend(): pl.pallas_call(functools.partial(attend_kernel, head_dim, video, len(remo...  6.78 us
    ppermute x4, starting transfers between devices, per_device(): remotes[video, which] = [lax.ppermute(own, 'pos', step) for step in steps]  5.25 us
    ppermute x3, starting transfers between devices, way_back(): held.append(lax.ppermute(blocks[s], 'frame', pairs))  4.48 us
  transfers between devices with their start and end apart: 13, of which 8 were waited for; matrix products, arithmetic and copies ran while one was open for 0% of the time, Pallas kernels for 33%

profile of v5, /device:TPU:0, one launch (start us, length us, event | category | flops | bytes accessed | tf_op | source)
XLA Modules:
  0.0 93.1 jit_solution(11973090132461851525)
XLA Ops:
  0.0 1.7 %copy-done = bf16[2,1,192,3,1152]{4,2,3,1,0:T(8,128)(2,1)S(1)} copy-done((bf16[2,1,192,3,1152]{4,2,3,1,0:T(8,128)(2,1)S(1)}, bf16[2,1,192,3,1152]{4,2,3,1,0:T(8,128)(2,1)}, u32[]{:S(2)}) %copy-start) | copy-done | bytes 2654232
  1.8 0.3 pick_0_1.1
  2.0 3.0 %collective-permute-start = (bf16[192,1152]{1,0:T(8,128)(2,1)S(1)}, bf16[192,1152]{1,0:T(8,128)(2,1)S(1)}, u32[]{:S(2)}, u32[]{:S(2)}) collective-permute-start(bf16[192,1152]{1,0:T(8,128)(2,1)S(1)} %pick_0_1.1), channel_id=1, source_target_pairs={{0,1},{1,0},{2,3},{3,2},{4,5},{5,4},{6,7},{7,6},{8,9},{9,8},{10,11... | collective-permute-start | bytes 1327112 | tf_op jit(solution)/shard_map/ppermute | solution.py:358
  5.0 0.3 pick_0_2.1
  5.4 1.0 %pick_1_1.1 = bf16[192,1152]{1,0:T(8,128)(2,1)} custom-call(bf16[2,3,192,1152]{3,2,1,0:T(8,128)(2,1)S(1)} %bitcast.18), custom_call_target="tpu_custom_call" | custom-call | flops 1000 | bytes 1048576 | tf_op jit(solution)/shard_map/pick_1_1/pallas_call | solution.py:309
  6.4 2.1 %collective-permute-start.8 = (bf16[192,1152]{1,0:T(8,128)(2,1)}, bf16[192,1152]{1,0:T(8,128)(2,1)S(1)}, u32[]{:S(2)}, u32[]{:S(2)}) collective-permute-start(bf16[192,1152]{1,0:T(8,128)(2,1)} %pick_1_1.1), channel_id=1, source_target_pairs={{0,1},{1,0},{2,3},{3,2},{4,5},{5,4},{6,7},{7,6},{8,9},{9,8},{10,11... | collective-permute-start | bytes 1327112 | tf_op jit(solution)/shard_map/ppermute | solution.py:358
  8.5 1.0 %pick_1_2.1 = bf16[192,1152]{1,0:T(8,128)(2,1)} custom-call(bf16[2,3,192,1152]{3,2,1,0:T(8,128)(2,1)S(1)} %bitcast.19), custom_call_target="tpu_custom_call" | custom-call | flops 1000 | bytes 1048576 | tf_op jit(solution)/shard_map/pick_1_2/pallas_call | solution.py:309
  9.6 6.4 %collective-permute-done.refs_1_ = bf16[192,1152]{1,0:T(8,128)(2,1)S(1)} collective-permute-done((bf16[192,1152]{1,0:T(8,128)(2,1)S(1)}, bf16[192,1152]{1,0:T(8,128)(2,1)S(1)}, u32[]{:S(2)}, u32[]{:S(2)}) %collective-permute-start) | collective-permute-done | bytes 442400 | tf_op jit(solution)/shard_map/ppermute | solution.py:358
  16.1 3.6 %scores_0.1.refs_0_ = bf16[16,192,384]{2,1,0:T(8,128)(2,1)S(1)} custom-call(bf16[2,3,192,1152]{3,2,1,0:T(8,128)(2,1)S(1)} %bitcast.20, bf16[192,1152]{1,0:T(8,128)(2,1)S(1)} %collective-permute-done.refs_1_, f32[1,72]{1,0:T(1,128)S(1)} %bitcast.28, f32[1,72]{1,0:T(1,128)S(1)} %bitcast.30), custom_call_target="tpu_custom_call" | custom-call | flops 500000000 | bytes 1048576 | tf_op jit(solution)/shard_map/scores_0/pallas_call | solution.py:101
  19.7 5.8 %collective-permute-done.1.refs_2_ = bf16[192,1152]{1,0:T(8,128)(2,1)S(1)} collective-permute-done((bf16[192,1152]{1,0:T(8,128)(2,1)S(1)}, bf16[192,1152]{1,0:T(8,128)(2,1)S(1)}, u32[]{:S(2)}, u32[]{:S(2)}) %collective-permute-start.1) | collective-permute-done | bytes 442400 | tf_op jit(solution)/shard_map/ppermute | solution.py:358
  25.5 2.9 %attend_0.1 = bf16[48,4,1152]{2,1,0:T(4,128)(2,1)} custom-call(bf16[16,192,384]{2,1,0:T(8,128)(2,1)S(1)} %scores_0.1.refs_0_, bf16[2,3,192,1152]{3,2,1,0:T(8,128)(2,1)S(1)} %bitcast.21, bf16[192,1152]{1,0:T(8,128)(2,1)S(1)} %collective-permute-done.1.refs_2_, bf16[2,192,1152]{2,1,0:T(8,128)(2,1)S(1)} %bitcast.26, bf16[1152,1152]{1,0:T(8,128)(2,1)S(1)} %copy-done.2, ...), custom_call_target="tpu_custom_call" | custom-call | flops 500000000 | bytes 1048576 | tf_op jit(solution)/shard_map/attend_0/pallas_call | solution.py:141
  28.5 6.5 %all-to-all-start = ((bf16[16,3,4,1152]{3,2,1,0:T(4,128)(2,1)}), bf16[16,3,4,1152]{3,2,1,0:T(4,128)(2,1)S(1)}, u32[]{:S(2)}, u32[]{:S(2)}) async-start(bf16[16,3,4,1152]{3,2,1,0:T(4,128)(2,1)} %bitcast.7), calls=%async_computation | async-start | bytes 884736 | tf_op jit(solution)/shard_map/all_to_all | solution.py:324
  35.0 0.8 copy-done.13
  35.8 3.6 %scores_1.1.refs_0_ = bf16[16,192,384]{2,1,0:T(8,128)(2,1)S(1)} custom-call(bf16[2,3,192,1152]{3,2,1,0:T(8,128)(2,1)S(1)} %bitcast.22, bf16[192,1152]{1,0:T(8,128)(2,1)S(1)} %collective-permute-done.8.refs_1_, f32[1,72]{1,0:T(1,128)S(1)} %bitcast.29, f32[1,72]{1,0:T(1,128)S(1)} %bitcast.31), custom_call_target="tpu_custom_call" | custom-call | flops 500000000 | bytes 1048576 | tf_op jit(solution)/shard_map/scores_1/pallas_call | solution.py:101
  39.5 4.3 %collective-permute-done.9.refs_2_ = bf16[192,1152]{1,0:T(8,128)(2,1)} collective-permute-done((bf16[192,1152]{1,0:T(8,128)(2,1)}, bf16[192,1152]{1,0:T(8,128)(2,1)}, u32[]{:S(2)}, u32[]{:S(2)}) %collective-permute-start.9) | collective-permute-done | bytes 442400 | tf_op jit(solution)/shard_map/ppermute | solution.py:358
  43.8 3.8 %attend_1.1 = bf16[48,4,1152]{2,1,0:T(4,128)(2,1)} custom-call(bf16[16,192,384]{2,1,0:T(8,128)(2,1)S(1)} %scores_1.1.refs_0_, bf16[2,3,192,1152]{3,2,1,0:T(8,128)(2,1)S(1)} %bitcast.23, bf16[192,1152]{1,0:T(8,128)(2,1)} %collective-permute-done.9.refs_2_, bf16[2,192,1152]{2,1,0:T(8,128)(2,1)S(1)} %bitcast.27, bf16[1152,1152]{1,0:T(8,128)(2,1)S(1)} %copy-done.3, ...), custom_call_target="tpu_custom_call" | custom-call | flops 20000000000 | bytes 1048576 | tf_op jit(solution)/shard_map/attend_1/pallas_call | solution.py:141
  47.6 0.4 all-to-all-done
  48.0 5.8 %all-to-all-start.1 = ((bf16[16,3,4,1152]{3,2,1,0:T(4,128)(2,1)}), bf16[16,3,4,1152]{3,2,1,0:T(4,128)(2,1)S(1)}, u32[]{:S(2)}, u32[]{:S(2)}) async-start(bf16[16,3,4,1152]{3,2,1,0:T(4,128)(2,1)} %bitcast.11), calls=%async_computation.1 | async-start | bytes 884736 | tf_op jit(solution)/shard_map/all_to_all | solution.py:324
  53.8 7.0 %temporal_0.1 = (bf16[12,4,1152]{2,1,0:T(4,128)(2,1)S(1)}, bf16[12,4,1152]{2,1,0:T(4,128)(2,1)S(1)}, bf16[12,4,1152]{2,1,0:T(4,128)(2,1)S(1)}, bf16[12,4,1152]{2,1,0:T(4,128)(2,1)S(1)}) custom-call(s32[1]{0:T(128)} %bitcast.refs_0_.me_ref, bf16[48,4,1152]{2,1,0:T(4,128)(2,1)S(1)} %bitcast.24, bf16[1152,3456]{1,0:T(8,128)(2,1)} %refs_2_.3, ...), custom_call_target="tpu_custom_call" | custom-call | flops 500000000 | bytes 1048576 | tf_op jit(solution)/shard_map/temporal_0/pallas_call | solution.py:213
  60.8 2.0 %collective-permute-start.2 = (bf16[12,4,1152]{2,1,0:T(4,128)(2,1)S(1)}, bf16[12,4,1152]{2,1,0:T(4,128)(2,1)S(1)}, u32[]{:S(2)}, u32[]{:S(2)}) collective-permute-start(bf16[12,4,1152]{2,1,0:T(4,128)(2,1)S(1)} %get-tuple-element.16), channel_id=1, source_target_pairs={{0,8},{2,10},{4,12},{6,14},{8,0},{10,2},{12,4},{14,6},{16,24},{18,... | collective-permute-start | bytes 331784 | tf_op jit(solution)/shard_map/ppermute | solution.py:286
  62.8 2.4 %collective-permute-start.3 = (bf16[12,4,1152]{2,1,0:T(4,128)(2,1)S(1)}, bf16[12,4,1152]{2,1,0:T(4,128)(2,1)S(1)}, u32[]{:S(2)}, u32[]{:S(2)}) collective-permute-start(bf16[12,4,1152]{2,1,0:T(4,128)(2,1)S(1)} %get-tuple-element.17), channel_id=1, source_target_pairs={{0,16},{2,18},{4,20},{6,22},{8,24},{10,26},{12,28},{14,30},{16,0},... | collective-permute-start | bytes 331784 | tf_op jit(solution)/shard_map/ppermute | solution.py:286
  65.1 0.2 collective-permute-start.4
  65.3 1.5 %all-to-all-done.1 = bf16[16,3,4,1152]{3,2,1,0:T(4,128)(2,1)S(1)} async-done(((bf16[16,3,4,1152]{3,2,1,0:T(4,128)(2,1)}), bf16[16,3,4,1152]{3,2,1,0:T(4,128)(2,1)S(1)}, u32[]{:S(2)}, u32[]{:S(2)}) %all-to-all-start.1) | async-done | bytes 442400 | tf_op jit(solution)/shard_map/all_to_all | solution.py:324
  66.8 7.7 %temporal_1.1 = bf16[48,4,1152]{2,1,0:T(4,128)(2,1)} custom-call(s32[1]{0:T(128)} %bitcast.refs_0_.me_ref, bf16[48,4,1152]{2,1,0:T(4,128)(2,1)S(1)} %bitcast.25, bf16[1152,3456]{1,0:T(8,128)(2,1)} %refs_2_.3, f32[1,72]{1,0:T(1,128)S(1)} %bitcast.33, f32[1,72]{1,0:T(1,128)S(1)} %bitcast.35), custom_call_target="tpu_custom_call" | custom-call | flops 500000000 | bytes 1048576 | tf_op jit(solution)/shard_map/temporal_1/pallas_call | solution.py:213
  74.6 4.4 %all-to-all-start.2 = ((bf16[16,3,4,1152]{3,2,1,0:T(4,128)(2,1)}), bf16[16,3,4,1152]{3,2,1,0:T(4,128)(2,1)S(1)}, u32[]{:S(2)}, u32[]{:S(2)}) async-start(bf16[16,3,4,1152]{3,2,1,0:T(4,128)(2,1)} %bitcast.13), calls=%async_computation.2 | async-start | bytes 884736 | tf_op jit(solution)/shard_map/all_to_all | solution.py:324
  79.1 0.5 collective-permute-start.5
  79.6 1.7 %collective-permute-start.6 = (bf16[12,4,1152]{2,1,0:T(4,128)(2,1)S(1)}, bf16[12,4,1152]{2,1,0:T(4,128)(2,1)S(1)}, u32[]{:S(2)}, u32[]{:S(2)}) collective-permute-start(bf16[12,4,1152]{2,1,0:T(4,128)(2,1)S(1)} %get-tuple-element.21), channel_id=1, source_target_pairs={{0,4},{2,6},{4,0},{6,2},{8,12},{10,14},{12,8},{14,10},{16,20},{18,... | collective-permute-start | bytes 331784 | tf_op jit(solution)/shard_map/ppermute | solution.py:295
  81.3 7.1 %collective-permute-done.6.refs_2_ = bf16[12,4,1152]{2,1,0:T(4,128)(2,1)S(1)} collective-permute-done((bf16[12,4,1152]{2,1,0:T(4,128)(2,1)S(1)}, bf16[12,4,1152]{2,1,0:T(4,128)(2,1)S(1)}, u32[]{:S(2)}, u32[]{:S(2)}) %collective-permute-start.6) | collective-permute-done | bytes 110624 | tf_op jit(solution)/shard_map/ppermute | solution.py:295
  88.4 1.8 %collective-permute-done.7.refs_3_ = bf16[12,4,1152]{2,1,0:T(4,128)(2,1)S(1)} collective-permute-done((bf16[12,4,1152]{2,1,0:T(4,128)(2,1)S(1)}, bf16[12,4,1152]{2,1,0:T(4,128)(2,1)S(1)}, u32[]{:S(2)}, u32[]{:S(2)}) %collective-permute-start.7) | collective-permute-done | bytes 110624 | tf_op jit(solution)/shard_map/ppermute | solution.py:295
  90.2 0.1 stack_reshape.3
  90.3 1.7 %all-to-all-done.2 = bf16[16,3,4,1152]{3,2,1,0:T(4,128)(2,1)S(1)} async-done(((bf16[16,3,4,1152]{3,2,1,0:T(4,128)(2,1)}), bf16[16,3,4,1152]{3,2,1,0:T(4,128)(2,1)S(1)}, u32[]{:S(2)}, u32[]{:S(2)}) %all-to-all-start.2) | async-done | bytes 442400 | tf_op jit(solution)/shard_map/all_to_all | solution.py:324
  92.1 1.0 %maximum_bitcast_fusion = bf16[2,1,192,1152]{3,2,1,0:T(8,128)(2,1)} fusion(bf16[1,192,1152]{2,1,0:T(8,128)(2,1)S(1)} %stack_reshape_reshape.3, bf16[1,192,1152]{2,1,0:T(8,128)(2,1)S(1)} %stack_reshape.3), kind=kLoop, calls=%fused_computation | loop fusion | flops 442368 | bytes 1769472 | tf_op jit(solution)/shard_map/reshape | solution.py:383
  (41 shorter events, 0.5 us)
Async XLA Ops:
  0.0 1.7 %copy-start = (bf16[2,1,192,3,1152]{4,2,3,1,0:T(8,128)(2,1)S(1)}, bf16[2,1,192,3,1152]{4,2,3,1,0:T(8,128)(2,1)}, u32[]{:S(2)}) copy-start(bf16[2,1,192,3,1152]{4,2,3,1,0:T(8,128)(2,1)} %param.11) | copy-start | bytes 7962628
  2.0 14.0 %collective-permute-start = (bf16[192,1152]{1,0:T(8,128)(2,1)S(1)}, bf16[192,1152]{1,0:T(8,128)(2,1)S(1)}, u32[]{:S(2)}, u32[]{:S(2)}) collective-permute-start(bf16[192,1152]{1,0:T(8,128)(2,1)S(1)} %pick_0_1.1), channel_id=1, source_target_pairs={{0,1},{1,0},{2,3},{3,2},{4,5},{5,4},{6,7},{7,6},{8,9},{9,8},{10,11... | collective-permute-start | bytes 1327112 | tf_op jit(solution)/shard_map/ppermute | solution.py:358
  5.3 10.7 %copy-start.1 = (bf16[2,1,192,3,1152]{4,2,3,1,0:T(8,128)(2,1)S(1)}, bf16[2,1,192,3,1152]{4,2,3,1,0:T(8,128)(2,1)}, u32[]{:S(2)}) copy-start(bf16[2,1,192,3,1152]{4,2,3,1,0:T(8,128)(2,1)} %param.11) | copy-start | bytes 7962628
  5.3 10.7 %copy-start.11 = (f32[72]{0:T(128)S(1)}, f32[72]{0:T(128)}, u32[]{:S(2)}) copy-start(f32[72]{0:T(128)} %param.15) | copy-start | bytes 868
  5.3 10.7 %copy-start.12 = (f32[72]{0:T(128)S(1)}, f32[72]{0:T(128)}, u32[]{:S(2)}) copy-start(f32[72]{0:T(128)} %param.16) | copy-start | bytes 868
  5.3 20.2 %collective-permute-start.1 = (bf16[192,1152]{1,0:T(8,128)(2,1)S(1)}, bf16[192,1152]{1,0:T(8,128)(2,1)S(1)}, u32[]{:S(2)}, u32[]{:S(2)}) collective-permute-start(bf16[192,1152]{1,0:T(8,128)(2,1)S(1)} %pick_0_2.1), channel_id=1, source_target_pairs={{0,1},{1,0},{2,3},{3,2},{4,5},{5,4},{6,7},{7,6},{8,9},{9,8},{10,11... | collective-permute-start | bytes 1327112 | tf_op jit(solution)/shard_map/ppermute | solution.py:358
  6.4 28.6 %collective-permute-start.8 = (bf16[192,1152]{1,0:T(8,128)(2,1)}, bf16[192,1152]{1,0:T(8,128)(2,1)S(1)}, u32[]{:S(2)}, u32[]{:S(2)}) collective-permute-start(bf16[192,1152]{1,0:T(8,128)(2,1)} %pick_1_1.1), channel_id=1, source_target_pairs={{0,1},{1,0},{2,3},{3,2},{4,5},{5,4},{6,7},{7,6},{8,9},{9,8},{10,11... | collective-permute-start | bytes 1327112 | tf_op jit(solution)/shard_map/ppermute | solution.py:358
  9.5 34.2 %collective-permute-start.9 = (bf16[192,1152]{1,0:T(8,128)(2,1)}, bf16[192,1152]{1,0:T(8,128)(2,1)}, u32[]{:S(2)}, u32[]{:S(2)}) collective-permute-start(bf16[192,1152]{1,0:T(8,128)(2,1)} %pick_1_2.1), channel_id=1, source_target_pairs={{0,1},{1,0},{2,3},{3,2},{4,5},{5,4},{6,7},{7,6},{8,9},{9,8},{10,11... | collective-permute-start | bytes 1327112 | tf_op jit(solution)/shard_map/ppermute | solution.py:358
  16.0 9.5 %copy-start.2 = (bf16[1152,1152]{1,0:T(8,128)(2,1)S(1)}, bf16[1152,1152]{1,0:T(8,128)(2,1)}, u32[]{:S(2)}) copy-start(bf16[1152,1152]{1,0:T(8,128)(2,1)} %refs_4_.3) | copy-start | bytes 7962628
  16.0 9.5 %copy-start.4 = (bf16[2,1,192,1152]{3,2,1,0:T(8,128)(2,1)S(1)}, bf16[2,1,192,1152]{3,2,1,0:T(8,128)(2,1)}, u32[]{:S(2)}) copy-start(bf16[2,1,192,1152]{3,2,1,0:T(8,128)(2,1)} %param.12) | copy-start | bytes 2654212
  16.0 9.5 %copy-start.6 = (f32[2,1152]{1,0:T(2,128)S(1)}, f32[2,1152]{1,0:T(2,128)}, u32[]{:S(2)}) copy-start(f32[2,1152]{1,0:T(2,128)} %refs_5_.3) | copy-start | bytes 27652
  16.1 9.4 %copy-start.7 = (f32[2,1152]{1,0:T(2,128)S(1)}, f32[2,1152]{1,0:T(2,128)}, u32[]{:S(2)}) copy-start(f32[2,1152]{1,0:T(2,128)} %refs_6_.3) | copy-start | bytes 27652
  16.1 9.4 %copy-start.9 = (f32[2,1152]{1,0:T(2,128)S(1)}, f32[2,1152]{1,0:T(2,128)}, u32[]{:S(2)}) copy-start(f32[2,1152]{1,0:T(2,128)} %refs_7_.3) | copy-start | bytes 27652
  28.5 19.5 %all-to-all-start = ((bf16[16,3,4,1152]{3,2,1,0:T(4,128)(2,1)}), bf16[16,3,4,1152]{3,2,1,0:T(4,128)(2,1)S(1)}, u32[]{:S(2)}, u32[]{:S(2)}) async-start(bf16[16,3,4,1152]{3,2,1,0:T(4,128)(2,1)} %bitcast.7), calls=%async_computation | async-start | bytes 884736 | tf_op jit(solution)/shard_map/all_to_all | solution.py:324
  35.0 8.8 %copy-start.3 = (bf16[1152,1152]{1,0:T(8,128)(2,1)S(1)}, bf16[1152,1152]{1,0:T(8,128)(2,1)}, u32[]{:S(2)}) copy-start(bf16[1152,1152]{1,0:T(8,128)(2,1)} %refs_4_.3) | copy-start | bytes 7962628
  35.0 8.8 %copy-start.5 = (bf16[2,1,192,1152]{3,2,1,0:T(8,128)(2,1)S(1)}, bf16[2,1,192,1152]{3,2,1,0:T(8,128)(2,1)}, u32[]{:S(2)}) copy-start(bf16[2,1,192,1152]{3,2,1,0:T(8,128)(2,1)} %param.12) | copy-start | bytes 2654212
  35.0 8.7 %copy-start.8 = (f32[2,1152]{1,0:T(2,128)S(1)}, f32[2,1152]{1,0:T(2,128)}, u32[]{:S(2)}) copy-start(f32[2,1152]{1,0:T(2,128)} %refs_6_.3) | copy-start | bytes 27652
  35.0 8.7 %copy-start.10 = (f32[2,1152]{1,0:T(2,128)S(1)}, f32[2,1152]{1,0:T(2,128)}, u32[]{:S(2)}) copy-start(f32[2,1152]{1,0:T(2,128)} %refs_7_.3) | copy-start | bytes 27652
  35.0 0.8 copy-start.13
  39.4 14.4 %copy-start.14 = (f32[72]{0:T(128)S(1)}, f32[72]{0:T(128)}, u32[]{:S(2)}) copy-start(f32[72]{0:T(128)} %param.20) | copy-start | bytes 868
  39.4 14.4 %copy-start.15 = (f32[72]{0:T(128)S(1)}, f32[72]{0:T(128)}, u32[]{:S(2)}) copy-start(f32[72]{0:T(128)} %param.21) | copy-start | bytes 868
  48.0 18.9 %all-to-all-start.1 = ((bf16[16,3,4,1152]{3,2,1,0:T(4,128)(2,1)}), bf16[16,3,4,1152]{3,2,1,0:T(4,128)(2,1)S(1)}, u32[]{:S(2)}, u32[]{:S(2)}) async-start(bf16[16,3,4,1152]{3,2,1,0:T(4,128)(2,1)} %bitcast.11), calls=%async_computation.1 | async-start | bytes 884736 | tf_op jit(solution)/shard_map/all_to_all | solution.py:324
  60.8 18.2 %collective-permute-start.2 = (bf16[12,4,1152]{2,1,0:T(4,128)(2,1)S(1)}, bf16[12,4,1152]{2,1,0:T(4,128)(2,1)S(1)}, u32[]{:S(2)}, u32[]{:S(2)}) collective-permute-start(bf16[12,4,1152]{2,1,0:T(4,128)(2,1)S(1)} %get-tuple-element.16), channel_id=1, source_target_pairs={{0,8},{2,10},{4,12},{6,14},{8,0},{10,2},{12,4},{14,6},{16,24},{18,... | collective-permute-start | bytes 331784 | tf_op jit(solution)/shard_map/ppermute | solution.py:286
  62.8 16.3 %collective-permute-start.3 = (bf16[12,4,1152]{2,1,0:T(4,128)(2,1)S(1)}, bf16[12,4,1152]{2,1,0:T(4,128)(2,1)S(1)}, u32[]{:S(2)}, u32[]{:S(2)}) collective-permute-start(bf16[12,4,1152]{2,1,0:T(4,128)(2,1)S(1)} %get-tuple-element.17), channel_id=1, source_target_pairs={{0,16},{2,18},{4,20},{6,22},{8,24},{10,26},{12,28},{14,30},{16,0},... | collective-permute-start | bytes 331784 | tf_op jit(solution)/shard_map/ppermute | solution.py:286
  65.1 13.9 %collective-permute-start.4 = (bf16[12,4,1152]{2,1,0:T(4,128)(2,1)S(1)}, bf16[12,4,1152]{2,1,0:T(4,128)(2,1)S(1)}, u32[]{:S(2)}, u32[]{:S(2)}) collective-permute-start(bf16[12,4,1152]{2,1,0:T(4,128)(2,1)S(1)} %get-tuple-element.18), channel_id=1, source_target_pairs={{0,24},{2,26},{4,28},{6,30},{8,16},{10,18},{12,20},{14,22},{16,8},... | collective-permute-start | bytes 331784 | tf_op jit(solution)/shard_map/ppermute | solution.py:286
  74.6 17.4 %all-to-all-start.2 = ((bf16[16,3,4,1152]{3,2,1,0:T(4,128)(2,1)}), bf16[16,3,4,1152]{3,2,1,0:T(4,128)(2,1)S(1)}, u32[]{:S(2)}, u32[]{:S(2)}) async-start(bf16[16,3,4,1152]{3,2,1,0:T(4,128)(2,1)} %bitcast.13), calls=%async_computation.2 | async-start | bytes 884736 | tf_op jit(solution)/shard_map/all_to_all | solution.py:324
  79.1 2.2 %collective-permute-start.5 = (bf16[12,4,1152]{2,1,0:T(4,128)(2,1)S(1)}, bf16[12,4,1152]{2,1,0:T(4,128)(2,1)S(1)}, u32[]{:S(2)}, u32[]{:S(2)}) collective-permute-start(bf16[12,4,1152]{2,1,0:T(4,128)(2,1)S(1)} %get-tuple-element.20), channel_id=1, source_target_pairs={{0,2},{2,0},{4,6},{6,4},{8,10},{10,8},{12,14},{14,12},{16,18},{18,... | collective-permute-start | bytes 331784 | tf_op jit(solution)/shard_map/ppermute | solution.py:295
  79.6 8.8 %collective-permute-start.6 = (bf16[12,4,1152]{2,1,0:T(4,128)(2,1)S(1)}, bf16[12,4,1152]{2,1,0:T(4,128)(2,1)S(1)}, u32[]{:S(2)}, u32[]{:S(2)}) collective-permute-start(bf16[12,4,1152]{2,1,0:T(4,128)(2,1)S(1)} %get-tuple-element.21), channel_id=1, source_target_pairs={{0,4},{2,6},{4,0},{6,2},{8,12},{10,14},{12,8},{14,10},{16,20},{18,... | collective-permute-start | bytes 331784 | tf_op jit(solution)/shard_map/ppermute | solution.py:295
  81.3 8.9 %collective-permute-start.7 = (bf16[12,4,1152]{2,1,0:T(4,128)(2,1)S(1)}, bf16[12,4,1152]{2,1,0:T(4,128)(2,1)S(1)}, u32[]{:S(2)}, u32[]{:S(2)}) collective-permute-start(bf16[12,4,1152]{2,1,0:T(4,128)(2,1)S(1)} %get-tuple-element.22), channel_id=1, source_target_pairs={{0,6},{2,4},{4,2},{6,0},{8,14},{10,12},{12,10},{14,8},{16,22},{18,... | collective-permute-start | bytes 331784 | tf_op jit(solution)/shard_map/ppermute | solution.py:295

commit v6 on v5

--- a/solution.py
+++ b/solution.py
@@ -53,9 +53,8 @@
 
 
 def head_window(head, head_dim, width):
-    tiles = width // LANES
-    start = LANES * min(head * head_dim // LANES, max(tiles - 2, 0))
-    span = min(2 * LANES, width)
+    start = head * head_dim // LANES * LANES
+    span = min(-(-(head + 1) * head_dim // LANES) * LANES, width) - start
     lane = lax.broadcasted_iota(jnp.int32, (1, span), 1) + start
     mask = (lane >= head * head_dim) & (lane < (head + 1) * head_dim)
     return start, span, mask
@@ -166,11 +165,15 @@
         for i, c in enumerate(columns)
         for j in range(SPLITS)
     ]
-    for copy in copies:
-        copy.start()
+    for i, copy in enumerate(copies):
+        copy.start(priority=0 if i < SPLITS else 1)
     rows = pieces * sub
     scale = math.log2(math.e) / math.sqrt(head_dim)
     gather, spread = segment_masks(width, head_dim)
+    first = lax.broadcasted_iota(jnp.int32, (rows, rows), 0)
+    second = lax.broadcasted_iota(jnp.int32, (rows, rows), 1)
+    same = lax.rem(first, tokens) == lax.rem(second, tokens)
+    bias[...] = jnp.where(same, 0.0, -1e30)
     for i in range(pieces):
         arranged[i * sub : (i + 1) * sub, :] = in_ref[i].astype(F32)
     incoming = arranged[...].astype(BF16)
@@ -181,10 +184,6 @@
         if gain is not None:
             projected = head_norm(projected, gain, gather, spread, head_dim)
         place[...] = projected
-    first = lax.broadcasted_iota(jnp.int32, (rows, rows), 0)
-    second = lax.broadcasted_iota(jnp.int32, (rows, rows), 1)
-    same = lax.rem(first, tokens) == lax.rem(second, tokens)
-    bias[...] = jnp.where(same, 0.0, -1e30)
     for head in range(width // head_dim):
         start, span, mask = head_window(head, head_dim, width)
         window = slice(start, start + span)

time: 93.6 us -> 93.5 us (level)
  no operation moved by 1% of the time
where the time goes in v6:
time: 93.5 us; the launch traced here: 93 us
  Pallas kernels  31.2 us (33%)
  waiting for transfers between devices  29 us (31%)
  starting transfers between devices  28.7 us (31%)
  local copies, waits for them, and re-layouts  2.84 us (3%)
  other arithmetic  1 us (1%)
    all_to_all x3, starting transfers between devices, exchange(): lax.all_to_all(split, 'frame', split_axis=0, concat_axis=0, tiled=True)  16.8 us
    ppermute x4, waiting for transfers between devices, per_device(): remotes[video, which] = [lax.ppermute(own, 'pos', step) for step in steps]  16.5 us
    pallas_call x2, Pallas kernels, temporal(): pl.pallas_call(functools.partial(temporal_kernel, head_dim, tokens, outer...  14.7 us
    ppermute x3, waiting for transfers between devices, way_back(): held.append(lax.ppermute(grouped[t], 'frame', pairs))  8.92 us
    pallas_call x2, Pallas kernels, score_weights(): pl.pallas_call(functools.partial(score_kernel, head_dim, video, len(remot...  7.19 us
    pallas_call x2, Pallas kernels, attend(): pl.pallas_call(functools.partial(attend_kernel, head_dim, video, len(remo...  6.68 us
    ppermute x4, starting transfers between devices, per_device(): remotes[video, which] = [lax.ppermute(own, 'pos', step) for step in steps]  5.25 us
    ppermute x3, starting transfers between devices, way_back(): held.append(lax.ppermute(blocks[s], 'frame', pairs))  4.48 us
  transfers between devices with their start and end apart: 13, of which 8 were waited for; matrix products, arithmetic and copies ran while one was open for 0% of the time, Pallas kernels for 33%

profile of v6, /device:TPU:0, one launch (start us, length us, event | category | flops | bytes accessed | tf_op | source)
XLA Modules:
  0.0 93.0 jit_solution(1828370800860059897)
XLA Ops:
  0.0 1.7 %copy-done = bf16[2,1,192,3,1152]{4,2,3,1,0:T(8,128)(2,1)S(1)} copy-done((bf16[2,1,192,3,1152]{4,2,3,1,0:T(8,128)(2,1)S(1)}, bf16[2,1,192,3,1152]{4,2,3,1,0:T(8,128)(2,1)}, u32[]{:S(2)}) %copy-start) | copy-done | bytes 2654232
  1.8 0.3 pick_0_1.1
  2.0 3.0 %collective-permute-start = (bf16[192,1152]{1,0:T(8,128)(2,1)S(1)}, bf16[192,1152]{1,0:T(8,128)(2,1)S(1)}, u32[]{:S(2)}, u32[]{:S(2)}) collective-permute-start(bf16[192,1152]{1,0:T(8,128)(2,1)S(1)} %pick_0_1.1), channel_id=1, source_target_pairs={{0,1},{1,0},{2,3},{3,2},{4,5},{5,4},{6,7},{7,6},{8,9},{9,8},{10,11... | collective-permute-start | bytes 1327112 | tf_op jit(solution)/shard_map/ppermute | solution.py:357
  5.0 0.3 pick_0_2.1
  5.4 1.0 %pick_1_1.1 = bf16[192,1152]{1,0:T(8,128)(2,1)} custom-call(bf16[2,3,192,1152]{3,2,1,0:T(8,128)(2,1)S(1)} %bitcast.18), custom_call_target="tpu_custom_call" | custom-call | flops 1000 | bytes 1048576 | tf_op jit(solution)/shard_map/pick_1_1/pallas_call | solution.py:308
  6.4 2.1 %collective-permute-start.8 = (bf16[192,1152]{1,0:T(8,128)(2,1)}, bf16[192,1152]{1,0:T(8,128)(2,1)S(1)}, u32[]{:S(2)}, u32[]{:S(2)}) collective-permute-start(bf16[192,1152]{1,0:T(8,128)(2,1)} %pick_1_1.1), channel_id=1, source_target_pairs={{0,1},{1,0},{2,3},{3,2},{4,5},{5,4},{6,7},{7,6},{8,9},{9,8},{10,11... | collective-permute-start | bytes 1327112 | tf_op jit(solution)/shard_map/ppermute | solution.py:357
  8.5 1.0 %pick_1_2.1 = bf16[192,1152]{1,0:T(8,128)(2,1)} custom-call(bf16[2,3,192,1152]{3,2,1,0:T(8,128)(2,1)S(1)} %bitcast.19), custom_call_target="tpu_custom_call" | custom-call | flops 1000 | bytes 1048576 | tf_op jit(solution)/shard_map/pick_1_2/pallas_call | solution.py:308
  9.6 6.4 %collective-permute-done.refs_1_ = bf16[192,1152]{1,0:T(8,128)(2,1)S(1)} collective-permute-done((bf16[192,1152]{1,0:T(8,128)(2,1)S(1)}, bf16[192,1152]{1,0:T(8,128)(2,1)S(1)}, u32[]{:S(2)}, u32[]{:S(2)}) %collective-permute-start) | collective-permute-done | bytes 442400 | tf_op jit(solution)/shard_map/ppermute | solution.py:357
  16.1 3.6 %scores_0.1.refs_0_ = bf16[16,192,384]{2,1,0:T(8,128)(2,1)S(1)} custom-call(bf16[2,3,192,1152]{3,2,1,0:T(8,128)(2,1)S(1)} %bitcast.20, bf16[192,1152]{1,0:T(8,128)(2,1)S(1)} %collective-permute-done.refs_1_, f32[1,72]{1,0:T(1,128)S(1)} %bitcast.28, f32[1,72]{1,0:T(1,128)S(1)} %bitcast.30), custom_call_target="tpu_custom_call" | custom-call | flops 500000000 | bytes 1048576 | tf_op jit(solution)/shard_map/scores_0/pallas_call | solution.py:100
  19.7 5.8 %collective-permute-done.1.refs_2_ = bf16[192,1152]{1,0:T(8,128)(2,1)S(1)} collective-permute-done((bf16[192,1152]{1,0:T(8,128)(2,1)S(1)}, bf16[192,1152]{1,0:T(8,128)(2,1)S(1)}, u32[]{:S(2)}, u32[]{:S(2)}) %collective-permute-start.1) | collective-permute-done | bytes 442400 | tf_op jit(solution)/shard_map/ppermute | solution.py:357
  25.5 2.9 %attend_0.1 = bf16[48,4,1152]{2,1,0:T(4,128)(2,1)} custom-call(bf16[16,192,384]{2,1,0:T(8,128)(2,1)S(1)} %scores_0.1.refs_0_, bf16[2,3,192,1152]{3,2,1,0:T(8,128)(2,1)S(1)} %bitcast.21, bf16[192,1152]{1,0:T(8,128)(2,1)S(1)} %collective-permute-done.1.refs_2_, bf16[2,192,1152]{2,1,0:T(8,128)(2,1)S(1)} %bitcast.26, bf16[1152,1152]{1,0:T(8,128)(2,1)S(1)} %copy-done.2, ...), custom_call_target="tpu_custom_call" | custom-call | flops 500000000 | bytes 1048576 | tf_op jit(solution)/shard_map/attend_0/pallas_call | solution.py:140
  28.4 6.5 %all-to-all-start = ((bf16[16,3,4,1152]{3,2,1,0:T(4,128)(2,1)}), bf16[16,3,4,1152]{3,2,1,0:T(4,128)(2,1)S(1)}, u32[]{:S(2)}, u32[]{:S(2)}) async-start(bf16[16,3,4,1152]{3,2,1,0:T(4,128)(2,1)} %bitcast.7), calls=%async_computation | async-start | bytes 884736 | tf_op jit(solution)/shard_map/all_to_all | solution.py:323
  35.0 0.8 copy-done.13
  35.8 3.6 %scores_1.1.refs_0_ = bf16[16,192,384]{2,1,0:T(8,128)(2,1)S(1)} custom-call(bf16[2,3,192,1152]{3,2,1,0:T(8,128)(2,1)S(1)} %bitcast.22, bf16[192,1152]{1,0:T(8,128)(2,1)S(1)} %collective-permute-done.8.refs_1_, f32[1,72]{1,0:T(1,128)S(1)} %bitcast.29, f32[1,72]{1,0:T(1,128)S(1)} %bitcast.31), custom_call_target="tpu_custom_call" | custom-call | flops 500000000 | bytes 1048576 | tf_op jit(solution)/shard_map/scores_1/pallas_call | solution.py:100
  39.4 4.3 %collective-permute-done.9.refs_2_ = bf16[192,1152]{1,0:T(8,128)(2,1)} collective-permute-done((bf16[192,1152]{1,0:T(8,128)(2,1)}, bf16[192,1152]{1,0:T(8,128)(2,1)}, u32[]{:S(2)}, u32[]{:S(2)}) %collective-permute-start.9) | collective-permute-done | bytes 442400 | tf_op jit(solution)/shard_map/ppermute | solution.py:357
  43.8 3.8 %attend_1.1 = bf16[48,4,1152]{2,1,0:T(4,128)(2,1)} custom-call(bf16[16,192,384]{2,1,0:T(8,128)(2,1)S(1)} %scores_1.1.refs_0_, bf16[2,3,192,1152]{3,2,1,0:T(8,128)(2,1)S(1)} %bitcast.23, bf16[192,1152]{1,0:T(8,128)(2,1)} %collective-permute-done.9.refs_2_, bf16[2,192,1152]{2,1,0:T(8,128)(2,1)S(1)} %bitcast.27, bf16[1152,1152]{1,0:T(8,128)(2,1)S(1)} %copy-done.3, ...), custom_call_target="tpu_custom_call" | custom-call | flops 20000000000 | bytes 1048576 | tf_op jit(solution)/shard_map/attend_1/pallas_call | solution.py:140
  47.5 0.4 all-to-all-done
  47.9 5.8 %all-to-all-start.1 = ((bf16[16,3,4,1152]{3,2,1,0:T(4,128)(2,1)}), bf16[16,3,4,1152]{3,2,1,0:T(4,128)(2,1)S(1)}, u32[]{:S(2)}, u32[]{:S(2)}) async-start(bf16[16,3,4,1152]{3,2,1,0:T(4,128)(2,1)} %bitcast.11), calls=%async_computation.1 | async-start | bytes 884736 | tf_op jit(solution)/shard_map/all_to_all | solution.py:323
  53.8 6.9 %temporal_0.1 = (bf16[12,4,1152]{2,1,0:T(4,128)(2,1)S(1)}, bf16[12,4,1152]{2,1,0:T(4,128)(2,1)S(1)}, bf16[12,4,1152]{2,1,0:T(4,128)(2,1)S(1)}, bf16[12,4,1152]{2,1,0:T(4,128)(2,1)S(1)}) custom-call(s32[1]{0:T(128)} %bitcast.refs_0_.me_ref, bf16[48,4,1152]{2,1,0:T(4,128)(2,1)S(1)} %bitcast.24, bf16[1152,3456]{1,0:T(8,128)(2,1)} %refs_2_.3, ...), custom_call_target="tpu_custom_call" | custom-call | flops 500000000 | bytes 1048576 | tf_op jit(solution)/shard_map/temporal_0/pallas_call | solution.py:212
  60.7 2.0 %collective-permute-start.2 = (bf16[12,4,1152]{2,1,0:T(4,128)(2,1)S(1)}, bf16[12,4,1152]{2,1,0:T(4,128)(2,1)S(1)}, u32[]{:S(2)}, u32[]{:S(2)}) collective-permute-start(bf16[12,4,1152]{2,1,0:T(4,128)(2,1)S(1)} %get-tuple-element.16), channel_id=1, source_target_pairs={{0,8},{2,10},{4,12},{6,14},{8,0},{10,2},{12,4},{14,6},{16,24},{18,... | collective-permute-start | bytes 331784 | tf_op jit(solution)/shard_map/ppermute | solution.py:285
  62.7 2.4 %collective-permute-start.3 = (bf16[12,4,1152]{2,1,0:T(4,128)(2,1)S(1)}, bf16[12,4,1152]{2,1,0:T(4,128)(2,1)S(1)}, u32[]{:S(2)}, u32[]{:S(2)}) collective-permute-start(bf16[12,4,1152]{2,1,0:T(4,128)(2,1)S(1)} %get-tuple-element.17), channel_id=1, source_target_pairs={{0,16},{2,18},{4,20},{6,22},{8,24},{10,26},{12,28},{14,30},{16,0},... | collective-permute-start | bytes 331784 | tf_op jit(solution)/shard_map/ppermute | solution.py:285
  65.1 0.2 collective-permute-start.4
  65.2 1.6 %all-to-all-done.1 = bf16[16,3,4,1152]{3,2,1,0:T(4,128)(2,1)S(1)} async-done(((bf16[16,3,4,1152]{3,2,1,0:T(4,128)(2,1)}), bf16[16,3,4,1152]{3,2,1,0:T(4,128)(2,1)S(1)}, u32[]{:S(2)}, u32[]{:S(2)}) %all-to-all-start.1) | async-done | bytes 442400 | tf_op jit(solution)/shard_map/all_to_all | solution.py:323
  66.8 7.7 %temporal_1.1 = bf16[48,4,1152]{2,1,0:T(4,128)(2,1)} custom-call(s32[1]{0:T(128)} %bitcast.refs_0_.me_ref, bf16[48,4,1152]{2,1,0:T(4,128)(2,1)S(1)} %bitcast.25, bf16[1152,3456]{1,0:T(8,128)(2,1)} %refs_2_.3, f32[1,72]{1,0:T(1,128)S(1)} %bitcast.33, f32[1,72]{1,0:T(1,128)S(1)} %bitcast.35), custom_call_target="tpu_custom_call" | custom-call | flops 500000000 | bytes 1048576 | tf_op jit(solution)/shard_map/temporal_1/pallas_call | solution.py:212
  74.5 4.4 %all-to-all-start.2 = ((bf16[16,3,4,1152]{3,2,1,0:T(4,128)(2,1)}), bf16[16,3,4,1152]{3,2,1,0:T(4,128)(2,1)S(1)}, u32[]{:S(2)}, u32[]{:S(2)}) async-start(bf16[16,3,4,1152]{3,2,1,0:T(4,128)(2,1)} %bitcast.13), calls=%async_computation.2 | async-start | bytes 884736 | tf_op jit(solution)/shard_map/all_to_all | solution.py:323
  79.0 0.5 collective-permute-start.5
  79.5 1.7 %collective-permute-start.6 = (bf16[12,4,1152]{2,1,0:T(4,128)(2,1)S(1)}, bf16[12,4,1152]{2,1,0:T(4,128)(2,1)S(1)}, u32[]{:S(2)}, u32[]{:S(2)}) collective-permute-start(bf16[12,4,1152]{2,1,0:T(4,128)(2,1)S(1)} %get-tuple-element.21), channel_id=1, source_target_pairs={{0,4},{2,6},{4,0},{6,2},{8,12},{10,14},{12,8},{14,10},{16,20},{18,... | collective-permute-start | bytes 331784 | tf_op jit(solution)/shard_map/ppermute | solution.py:294
  81.2 7.1 %collective-permute-done.6.refs_2_ = bf16[12,4,1152]{2,1,0:T(4,128)(2,1)S(1)} collective-permute-done((bf16[12,4,1152]{2,1,0:T(4,128)(2,1)S(1)}, bf16[12,4,1152]{2,1,0:T(4,128)(2,1)S(1)}, u32[]{:S(2)}, u32[]{:S(2)}) %collective-permute-start.6) | collective-permute-done | bytes 110624 | tf_op jit(solution)/shard_map/ppermute | solution.py:294
  88.3 1.8 %collective-permute-done.7.refs_3_ = bf16[12,4,1152]{2,1,0:T(4,128)(2,1)S(1)} collective-permute-done((bf16[12,4,1152]{2,1,0:T(4,128)(2,1)S(1)}, bf16[12,4,1152]{2,1,0:T(4,128)(2,1)S(1)}, u32[]{:S(2)}, u32[]{:S(2)}) %collective-permute-start.7) | collective-permute-done | bytes 110624 | tf_op jit(solution)/shard_map/ppermute | solution.py:294
  90.2 0.1 stack_reshape.3
  90.3 1.7 %all-to-all-done.2 = bf16[16,3,4,1152]{3,2,1,0:T(4,128)(2,1)S(1)} async-done(((bf16[16,3,4,1152]{3,2,1,0:T(4,128)(2,1)}), bf16[16,3,4,1152]{3,2,1,0:T(4,128)(2,1)S(1)}, u32[]{:S(2)}, u32[]{:S(2)}) %all-to-all-start.2) | async-done | bytes 442400 | tf_op jit(solution)/shard_map/all_to_all | solution.py:323
  92.0 1.0 %maximum_bitcast_fusion = bf16[2,1,192,1152]{3,2,1,0:T(8,128)(2,1)} fusion(bf16[1,192,1152]{2,1,0:T(8,128)(2,1)S(1)} %stack_reshape_reshape.3, bf16[1,192,1152]{2,1,0:T(8,128)(2,1)S(1)} %stack_reshape.3), kind=kLoop, calls=%fused_computation | loop fusion | flops 442368 | bytes 1769472 | tf_op jit(solution)/shard_map/reshape | solution.py:382
  (41 shorter events, 0.5 us)
Async XLA Ops:
  0.0 1.7 %copy-start = (bf16[2,1,192,3,1152]{4,2,3,1,0:T(8,128)(2,1)S(1)}, bf16[2,1,192,3,1152]{4,2,3,1,0:T(8,128)(2,1)}, u32[]{:S(2)}) copy-start(bf16[2,1,192,3,1152]{4,2,3,1,0:T(8,128)(2,1)} %param.11) | copy-start | bytes 7962628
  2.0 14.0 %collective-permute-start = (bf16[192,1152]{1,0:T(8,128)(2,1)S(1)}, bf16[192,1152]{1,0:T(8,128)(2,1)S(1)}, u32[]{:S(2)}, u32[]{:S(2)}) collective-permute-start(bf16[192,1152]{1,0:T(8,128)(2,1)S(1)} %pick_0_1.1), channel_id=1, source_target_pairs={{0,1},{1,0},{2,3},{3,2},{4,5},{5,4},{6,7},{7,6},{8,9},{9,8},{10,11... | collective-permute-start | bytes 1327112 | tf_op jit(solution)/shard_map/ppermute | solution.py:357
  5.3 10.7 %copy-start.1 = (bf16[2,1,192,3,1152]{4,2,3,1,0:T(8,128)(2,1)S(1)}, bf16[2,1,192,3,1152]{4,2,3,1,0:T(8,128)(2,1)}, u32[]{:S(2)}) copy-start(bf16[2,1,192,3,1152]{4,2,3,1,0:T(8,128)(2,1)} %param.11) | copy-start | bytes 7962628
  5.3 10.7 %copy-start.11 = (f32[72]{0:T(128)S(1)}, f32[72]{0:T(128)}, u32[]{:S(2)}) copy-start(f32[72]{0:T(128)} %param.15) | copy-start | bytes 868
  5.3 10.7 %copy-start.12 = (f32[72]{0:T(128)S(1)}, f32[72]{0:T(128)}, u32[]{:S(2)}) copy-start(f32[72]{0:T(128)} %param.16) | copy-start | bytes 868
  5.3 20.2 %collective-permute-start.1 = (bf16[192,1152]{1,0:T(8,128)(2,1)S(1)}, bf16[192,1152]{1,0:T(8,128)(2,1)S(1)}, u32[]{:S(2)}, u32[]{:S(2)}) collective-permute-start(bf16[192,1152]{1,0:T(8,128)(2,1)S(1)} %pick_0_2.1), channel_id=1, source_target_pairs={{0,1},{1,0},{2,3},{3,2},{4,5},{5,4},{6,7},{7,6},{8,9},{9,8},{10,11... | collective-permute-start | bytes 1327112 | tf_op jit(solution)/shard_map/ppermute | solution.py:357
  6.4 28.5 %collective-permute-start.8 = (bf16[192,1152]{1,0:T(8,128)(2,1)}, bf16[192,1152]{1,0:T(8,128)(2,1)S(1)}, u32[]{:S(2)}, u32[]{:S(2)}) collective-permute-start(bf16[192,1152]{1,0:T(8,128)(2,1)} %pick_1_1.1), channel_id=1, source_target_pairs={{0,1},{1,0},{2,3},{3,2},{4,5},{5,4},{6,7},{7,6},{8,9},{9,8},{10,11... | collective-permute-start | bytes 1327112 | tf_op jit(solution)/shard_map/ppermute | solution.py:357
  9.5 34.2 %collective-permute-start.9 = (bf16[192,1152]{1,0:T(8,128)(2,1)}, bf16[192,1152]{1,0:T(8,128)(2,1)}, u32[]{:S(2)}, u32[]{:S(2)}) collective-permute-start(bf16[192,1152]{1,0:T(8,128)(2,1)} %pick_1_2.1), channel_id=1, source_target_pairs={{0,1},{1,0},{2,3},{3,2},{4,5},{5,4},{6,7},{7,6},{8,9},{9,8},{10,11... | collective-permute-start | bytes 1327112 | tf_op jit(solution)/shard_map/ppermute | solution.py:357
  16.0 9.5 %copy-start.2 = (bf16[1152,1152]{1,0:T(8,128)(2,1)S(1)}, bf16[1152,1152]{1,0:T(8,128)(2,1)}, u32[]{:S(2)}) copy-start(bf16[1152,1152]{1,0:T(8,128)(2,1)} %refs_4_.3) | copy-start | bytes 7962628
  16.0 9.5 %copy-start.4 = (bf16[2,1,192,1152]{3,2,1,0:T(8,128)(2,1)S(1)}, bf16[2,1,192,1152]{3,2,1,0:T(8,128)(2,1)}, u32[]{:S(2)}) copy-start(bf16[2,1,192,1152]{3,2,1,0:T(8,128)(2,1)} %param.12) | copy-start | bytes 2654212
  16.0 9.5 %copy-start.6 = (f32[2,1152]{1,0:T(2,128)S(1)}, f32[2,1152]{1,0:T(2,128)}, u32[]{:S(2)}) copy-start(f32[2,1152]{1,0:T(2,128)} %refs_5_.3) | copy-start | bytes 27652
  16.1 9.4 %copy-start.7 = (f32[2,1152]{1,0:T(2,128)S(1)}, f32[2,1152]{1,0:T(2,128)}, u32[]{:S(2)}) copy-start(f32[2,1152]{1,0:T(2,128)} %refs_6_.3) | copy-start | bytes 27652
  16.1 9.4 %copy-start.9 = (f32[2,1152]{1,0:T(2,128)S(1)}, f32[2,1152]{1,0:T(2,128)}, u32[]{:S(2)}) copy-start(f32[2,1152]{1,0:T(2,128)} %refs_7_.3) | copy-start | bytes 27652
  28.4 19.5 %all-to-all-start = ((bf16[16,3,4,1152]{3,2,1,0:T(4,128)(2,1)}), bf16[16,3,4,1152]{3,2,1,0:T(4,128)(2,1)S(1)}, u32[]{:S(2)}, u32[]{:S(2)}) async-start(bf16[16,3,4,1152]{3,2,1,0:T(4,128)(2,1)} %bitcast.7), calls=%async_computation | async-start | bytes 884736 | tf_op jit(solution)/shard_map/all_to_all | solution.py:323
  34.9 8.8 %copy-start.3 = (bf16[1152,1152]{1,0:T(8,128)(2,1)S(1)}, bf16[1152,1152]{1,0:T(8,128)(2,1)}, u32[]{:S(2)}) copy-start(bf16[1152,1152]{1,0:T(8,128)(2,1)} %refs_4_.3) | copy-start | bytes 7962628
  34.9 8.8 %copy-start.5 = (bf16[2,1,192,1152]{3,2,1,0:T(8,128)(2,1)S(1)}, bf16[2,1,192,1152]{3,2,1,0:T(8,128)(2,1)}, u32[]{:S(2)}) copy-start(bf16[2,1,192,1152]{3,2,1,0:T(8,128)(2,1)} %param.12) | copy-start | bytes 2654212
  34.9 8.8 %copy-start.8 = (f32[2,1152]{1,0:T(2,128)S(1)}, f32[2,1152]{1,0:T(2,128)}, u32[]{:S(2)}) copy-start(f32[2,1152]{1,0:T(2,128)} %refs_6_.3) | copy-start | bytes 27652
  35.0 8.8 %copy-start.10 = (f32[2,1152]{1,0:T(2,128)S(1)}, f32[2,1152]{1,0:T(2,128)}, u32[]{:S(2)}) copy-start(f32[2,1152]{1,0:T(2,128)} %refs_7_.3) | copy-start | bytes 27652
  35.0 0.8 copy-start.13
  39.4 14.4 %copy-start.14 = (f32[72]{0:T(128)S(1)}, f32[72]{0:T(128)}, u32[]{:S(2)}) copy-start(f32[72]{0:T(128)} %param.20) | copy-start | bytes 868
  39.4 14.4 %copy-start.15 = (f32[72]{0:T(128)S(1)}, f32[72]{0:T(128)}, u32[]{:S(2)}) copy-start(f32[72]{0:T(128)} %param.21) | copy-start | bytes 868
  47.9 18.9 %all-to-all-start.1 = ((bf16[16,3,4,1152]{3,2,1,0:T(4,128)(2,1)}), bf16[16,3,4,1152]{3,2,1,0:T(4,128)(2,1)S(1)}, u32[]{:S(2)}, u32[]{:S(2)}) async-start(bf16[16,3,4,1152]{3,2,1,0:T(4,128)(2,1)} %bitcast.11), calls=%async_computation.1 | async-start | bytes 884736 | tf_op jit(solution)/shard_map/all_to_all | solution.py:323
  60.7 18.2 %collective-permute-start.2 = (bf16[12,4,1152]{2,1,0:T(4,128)(2,1)S(1)}, bf16[12,4,1152]{2,1,0:T(4,128)(2,1)S(1)}, u32[]{:S(2)}, u32[]{:S(2)}) collective-permute-start(bf16[12,4,1152]{2,1,0:T(4,128)(2,1)S(1)} %get-tuple-element.16), channel_id=1, source_target_pairs={{0,8},{2,10},{4,12},{6,14},{8,0},{10,2},{12,4},{14,6},{16,24},{18,... | collective-permute-start | bytes 331784 | tf_op jit(solution)/shard_map/ppermute | solution.py:285
  62.7 16.3 %collective-permute-start.3 = (bf16[12,4,1152]{2,1,0:T(4,128)(2,1)S(1)}, bf16[12,4,1152]{2,1,0:T(4,128)(2,1)S(1)}, u32[]{:S(2)}, u32[]{:S(2)}) collective-permute-start(bf16[12,4,1152]{2,1,0:T(4,128)(2,1)S(1)} %get-tuple-element.17), channel_id=1, source_target_pairs={{0,16},{2,18},{4,20},{6,22},{8,24},{10,26},{12,28},{14,30},{16,0},... | collective-permute-start | bytes 331784 | tf_op jit(solution)/shard_map/ppermute | solution.py:285
  65.1 13.9 %collective-permute-start.4 = (bf16[12,4,1152]{2,1,0:T(4,128)(2,1)S(1)}, bf16[12,4,1152]{2,1,0:T(4,128)(2,1)S(1)}, u32[]{:S(2)}, u32[]{:S(2)}) collective-permute-start(bf16[12,4,1152]{2,1,0:T(4,128)(2,1)S(1)} %get-tuple-element.18), channel_id=1, source_target_pairs={{0,24},{2,26},{4,28},{6,30},{8,16},{10,18},{12,20},{14,22},{16,8},... | collective-permute-start | bytes 331784 | tf_op jit(solution)/shard_map/ppermute | solution.py:285
  74.5 17.4 %all-to-all-start.2 = ((bf16[16,3,4,1152]{3,2,1,0:T(4,128)(2,1)}), bf16[16,3,4,1152]{3,2,1,0:T(4,128)(2,1)S(1)}, u32[]{:S(2)}, u32[]{:S(2)}) async-start(bf16[16,3,4,1152]{3,2,1,0:T(4,128)(2,1)} %bitcast.13), calls=%async_computation.2 | async-start | bytes 884736 | tf_op jit(solution)/shard_map/all_to_all | solution.py:323
  79.0 2.2 %collective-permute-start.5 = (bf16[12,4,1152]{2,1,0:T(4,128)(2,1)S(1)}, bf16[12,4,1152]{2,1,0:T(4,128)(2,1)S(1)}, u32[]{:S(2)}, u32[]{:S(2)}) collective-permute-start(bf16[12,4,1152]{2,1,0:T(4,128)(2,1)S(1)} %get-tuple-element.20), channel_id=1, source_target_pairs={{0,2},{2,0},{4,6},{6,4},{8,10},{10,8},{12,14},{14,12},{16,18},{18,... | collective-permute-start | bytes 331784 | tf_op jit(solution)/shard_map/ppermute | solution.py:294
  79.5 8.8 %collective-permute-start.6 = (bf16[12,4,1152]{2,1,0:T(4,128)(2,1)S(1)}, bf16[12,4,1152]{2,1,0:T(4,128)(2,1)S(1)}, u32[]{:S(2)}, u32[]{:S(2)}) collective-permute-start(bf16[12,4,1152]{2,1,0:T(4,128)(2,1)S(1)} %get-tuple-element.21), channel_id=1, source_target_pairs={{0,4},{2,6},{4,0},{6,2},{8,12},{10,14},{12,8},{14,10},{16,20},{18,... | collective-permute-start | bytes 331784 | tf_op jit(solution)/shard_map/ppermute | solution.py:294
  81.2 8.9 %collective-permute-start.7 = (bf16[12,4,1152]{2,1,0:T(4,128)(2,1)S(1)}, bf16[12,4,1152]{2,1,0:T(4,128)(2,1)S(1)}, u32[]{:S(2)}, u32[]{:S(2)}) collective-permute-start(bf16[12,4,1152]{2,1,0:T(4,128)(2,1)S(1)} %get-tuple-element.22), channel_id=1, source_target_pairs={{0,6},{2,4},{4,2},{6,0},{8,14},{10,12},{12,10},{14,8},{16,22},{18,... | collective-permute-start | bytes 331784 | tf_op jit(solution)/shard_map/ppermute | solution.py:294
